TPU v7x, 32 devices: a whole 2x2x4 slice. The times are simulated.
32 devices in a mesh: rep: 8 (over z, core), shard: 4 (over y, x).
Axes of the slice: x: 2, y: 2, z: 4, core: 2. Of those that a mesh axis runs over, the one named last changes fastest.
Arguments:
- tokens: bfloat16 [6144, 2304], P(('rep', 'shard')), may hold values from -7 to 7
- seg_ids: int32 [6144], P(('rep', 'shard')), may hold values from 0 to 13, as said below
- parents: int32 [8, 13], P('rep'), may hold values from 0 to 12, as said below
- attn_gain: bfloat16 [2304], replicated, may hold values from 0.25 to 1.75
- w_query: bfloat16 [2304, 2048], P('shard'), may hold values from -1 to 1
- w_key: bfloat16 [2304, 1024], P('shard'), may hold values from -1 to 1
- w_value: bfloat16 [2304, 1024], P('shard'), may hold values from -0.125 to 0.125
- w_out: bfloat16 [2048, 2304], P('shard'), may hold values from -0.125 to 0.125
- post_attn_gain: bfloat16 [2304], replicated, may hold values from 0.25 to 1.75
- ffn_gain: bfloat16 [2304], replicated, may hold values from 0.25 to 1.75
- w_gate: bfloat16 [2304, 9216], P(None, 'shard'), may hold values from -0.125 to 0.125
- w_up: bfloat16 [2304, 9216], P(None, 'shard'), may hold values from -0.125 to 0.125
- w_down: bfloat16 [9216, 2304], P('shard'), may hold values from -0.0625 to 0.0625
- post_ffn_gain: bfloat16 [2304], replicated, may hold values from 0.25 to 1.75
- cotangent: bfloat16 [6144, 2304], P(('rep', 'shard')), may hold values from -6 to 6
Outputs:
- output: bfloat16 [6144, 2304], P(('rep', 'shard'))
- grad_tokens: bfloat16 [6144, 2304], P(('rep', 'shard'))
- attn_gain_grad: float32 [2304], replicated
- query_grad: float32 [2304, 2048], P('shard')
- key_grad: float32 [2304, 1024], P('shard')
- value_grad: float32 [2304, 1024], P('shard')
- out_grad: float32 [2048, 2304], P('shard')
- post_attn_gain_grad: float32 [2304], replicated
- ffn_gain_grad: float32 [2304], replicated
- gate_grad: float32 [2304, 9216], P(None, 'shard')
- up_grad: float32 [2304, 9216], P(None, 'shard')
- down_grad: float32 [9216, 2304], P('shard')
- post_ffn_gain_grad: float32 [2304], replicated
Inputs may be any that keep to these rules, and one draw needn't show every extreme that they name: `seg_ids`: within each block of 768 tokens (one index of rep) the segments form one tree of 13: a root, four children of the root and two children of each of these. A segment's tokens are contiguous, a multiple of 12 in number, and come after its parent's; the root begins the block. Exactly the last 48 tokens of each block are padding and carry 13. `parents`: row r gives, for each segment of block r, its parent segment; the root's parent is the root itself.
All inputs are finite; a program needn't handle non-finite values.
Results may differ from a plain program's by a relative error of at most 0.024.
Values may be sent and summed in bfloat16 or wider, within the bound.
A program may use at most 640 MiB of HBM per device.

v0:
```python
import jax
import jax.numpy as jnp
from jax import lax
from jax.sharding import PartitionSpec as P

QUERY_HEADS = 8
KV = 4
HEAD_SIZE = 256
SEGS = 13


softcap = 50.0
norm_eps = 1e-06


def normalize(values, gain_vec):
    inv_rms = lax.rsqrt(jnp.mean(values * values, axis=-1, keepdims=True) + norm_eps)
    return (values * inv_rms * gain_vec, inv_rms)


def norm_back(values, inv_rms, gain_vec, grad_in):
    weighted = grad_in * gain_vec
    row_mean = jnp.mean(weighted * values, axis=-1, keepdims=True)
    grad_back = inv_rms * weighted - values * (inv_rms * inv_rms * inv_rms) * row_mean
    return (grad_back, jnp.sum(grad_in * values * inv_rms, axis=0))


def geglu(gate_pre, up_pre):
    return jax.nn.gelu(gate_pre, approximate=True) * up_pre


def body(
    tokens,
    seg_ids,
    parents,
    attn_gain,
    w_query,
    w_key,
    w_value,
    w_out,
    post_attn_gain,
    ffn_gain,
    w_gate,
    w_up,
    w_down,
    post_ffn_gain,
    cotangent,
):
    tok_rows = tokens.shape[0]
    head_dim = HEAD_SIZE
    kv_heads = KV
    repeat = QUERY_HEADS // KV
    q_width = QUERY_HEADS * HEAD_SIZE
    k_width = KV * HEAD_SIZE
    head_scale = head_dim ** (-0.5)
    gain_one = attn_gain.astype(jnp.float32)
    gain_two = post_attn_gain.astype(jnp.float32)
    gain_three = ffn_gain.astype(jnp.float32)
    gain_four = post_ffn_gain.astype(jnp.float32)
    qkv_local = jnp.concatenate((w_query, w_key, w_value), axis=1)
    qkv_full, out_full = (
        lax.all_gather(qkv_local, "shard", axis=0, tiled=True),
        lax.all_gather(w_out, "shard", axis=0, tiled=True),
    )
    residual = tokens.astype(jnp.float32)
    normed, rms_one = normalize(residual, gain_one)
    normed_b = normed.astype(jnp.bfloat16)
    qkv = jnp.dot(normed_b, qkv_full, preferred_element_type=jnp.float32).astype(jnp.bfloat16)
    queries = qkv[:, :q_width]
    keys_local = qkv[:, q_width : q_width + k_width]
    values_local = qkv[:, q_width + k_width :]
    key_code = seg_ids.astype(jnp.bfloat16)
    keys_all, values_all, codes_all = (
        lax.all_gather(keys_local, "shard", axis=0, tiled=True),
        lax.all_gather(values_local, "shard", axis=0, tiled=True),
        lax.all_gather(key_code, "shard", axis=0, tiled=True),
    )
    group_rows = keys_all.shape[0]
    parent_row = parents[0]
    labels = jnp.arange(SEGS)

    def lookup(ident):
        return jnp.sum(jnp.where(ident[:, None] == labels[None, :], parent_row[None, :], 0), axis=1)

    real_rows = seg_ids < SEGS
    parent_one = lookup(seg_ids)
    parent_two = lookup(parent_one)
    offset = lax.axis_index("shard") * tok_rows
    query_pos = offset + jnp.arange(tok_rows)
    key_pos = jnp.arange(group_rows)
    code_keys = codes_all.astype(jnp.int32)
    related = (
        (code_keys[None, :] == seg_ids[:, None])
        | (code_keys[None, :] == parent_one[:, None])
        | (code_keys[None, :] == parent_two[:, None])
    )
    visible = (key_pos[None, :] <= query_pos[:, None]) & real_rows[:, None] & (
        code_keys[None, :] < SEGS
    ) & related | (key_pos[None, :] == query_pos[:, None])
    grouped_queries = queries.reshape(tok_rows, kv_heads, repeat, head_dim)
    key_head_rows = keys_all.reshape(group_rows, kv_heads, head_dim)
    value_head_rows = values_all.reshape(group_rows, kv_heads, head_dim)

    def scores():
        score_matrix = jnp.einsum(
            "ziwh,fih->iwzf", grouped_queries, key_head_rows, preferred_element_type=jnp.float32
        )
        tanh_part = jnp.tanh(score_matrix * (head_scale / softcap))
        return (jnp.where(visible[None, None], softcap * tanh_part, -1e30), tanh_part)

    masked, tanh_part = scores()
    row_max = jnp.max(masked, axis=-1, keepdims=True)
    expo_terms = jnp.exp(masked - row_max)
    row_total = jnp.sum(expo_terms, axis=-1, keepdims=True)
    attention_probabilities = expo_terms / row_total
    log_total = row_max + jnp.log(row_total)
    mixed_out = jnp.einsum(
        "xbcv,vxu->cxbu",
        attention_probabilities.astype(jnp.bfloat16),
        value_head_rows,
        preferred_element_type=jnp.float32,
    )
    mixed_out = mixed_out.reshape(tok_rows, q_width).astype(jnp.bfloat16)
    attn_out = jnp.dot(mixed_out, out_full, preferred_element_type=jnp.float32)
    post_one, rms_two = normalize(attn_out, gain_two)
    middle = residual + post_one
    normed_two, rms_three = normalize(middle, gain_three)
    normed_two_b = normed_two.astype(jnp.bfloat16)
    gate_full, up_full, down_full = (
        lax.all_gather(w_gate, "shard", axis=1, tiled=True),
        lax.all_gather(w_up, "shard", axis=1, tiled=True),
        lax.all_gather(w_down, "shard", axis=0, tiled=True),
    )
    gate_pre = jnp.dot(normed_two_b, gate_full, preferred_element_type=jnp.float32)
    up_pre = jnp.dot(normed_two_b, up_full, preferred_element_type=jnp.float32)
    hidden, geglu_back = jax.vjp(geglu, gate_pre, up_pre)
    hidden_b = hidden.astype(jnp.bfloat16)
    ffn_out = jnp.dot(hidden_b, down_full, preferred_element_type=jnp.float32)
    post_two, rms_four = normalize(ffn_out, gain_four)
    output = (middle + post_two).astype(jnp.bfloat16)
    grad_out = cotangent.astype(jnp.float32)
    grad_ffn, grad_gain_four = norm_back(ffn_out, rms_four, gain_four, grad_out)
    grad_ffn_b = grad_ffn.astype(jnp.bfloat16)
    grad_hidden = jnp.einsum("td,fd->tf", grad_ffn_b, down_full, preferred_element_type=jnp.float32)
    columns_part = hidden_b
    down_part = lax.psum_scatter(
        jnp.einsum(
            "tf,td->fd", columns_part, grad_ffn_b, preferred_element_type=jnp.float32
        ).astype(jnp.bfloat16),
        "shard",
        scatter_dimension=0,
        tiled=True,
    )
    grad_gate, grad_up = geglu_back(grad_hidden)
    grad_gate_b = grad_gate.astype(jnp.bfloat16)
    grad_up_b = grad_up.astype(jnp.bfloat16)
    from_gate = jnp.einsum("tf,df->td", grad_gate_b, gate_full, preferred_element_type=jnp.float32)
    grad_normed_two = from_gate + jnp.einsum(
        "tf,df->td", grad_up_b, up_full, preferred_element_type=jnp.float32
    )
    gate_term = jnp.einsum(
        "td,tf->df", normed_two_b, grad_gate_b, preferred_element_type=jnp.float32
    )
    up_term = jnp.einsum("td,tf->df", normed_two_b, grad_up_b, preferred_element_type=jnp.float32)
    gate_part, up_part = (
        lax.psum_scatter(
            gate_term.astype(jnp.bfloat16), "shard", scatter_dimension=1, tiled=True
        ).astype(jnp.float32),
        lax.psum_scatter(
            up_term.astype(jnp.bfloat16), "shard", scatter_dimension=1, tiled=True
        ).astype(jnp.float32),
    )
    grad_middle_part, grad_gain_three = norm_back(middle, rms_three, gain_three, grad_normed_two)
    grad_middle = grad_out + grad_middle_part
    grad_attn, grad_gain_two = norm_back(attn_out, rms_two, gain_two, grad_middle)
    grad_attn_b = grad_attn.astype(jnp.bfloat16)
    grad_mixed = jnp.einsum(
        "td,jd->tj", grad_attn_b, out_full, preferred_element_type=jnp.float32
    ).astype(jnp.bfloat16)
    columns_part = mixed_out
    out_part = lax.psum_scatter(
        jnp.einsum(
            "tj,td->jd", columns_part, grad_attn_b, preferred_element_type=jnp.float32
        ).astype(jnp.bfloat16),
        "shard",
        scatter_dimension=0,
        tiled=True,
    )
    masked, tanh_part = scores()
    attention_probabilities = jnp.exp(masked - log_total)
    head_gradients = grad_mixed.reshape(tok_rows, kv_heads, repeat, head_dim)
    grad_probs = jnp.einsum(
        "ziwh,fih->iwzf", head_gradients, value_head_rows, preferred_element_type=jnp.float32
    )
    row_inner = jnp.sum(attention_probabilities * grad_probs, axis=-1, keepdims=True)
    score_gradient = (
        attention_probabilities
        * (grad_probs - row_inner)
        * (1.0 - tanh_part * tanh_part)
        * head_scale
    ).astype(jnp.bfloat16)
    grad_queries = jnp.einsum(
        "xbcv,vxu->cxbu", score_gradient, key_head_rows, preferred_element_type=jnp.float32
    )
    grad_queries = grad_queries.reshape(tok_rows, q_width).astype(jnp.bfloat16)
    key_terms = jnp.einsum(
        "bkpo,pbkv->obv", score_gradient, grouped_queries, preferred_element_type=jnp.float32
    ).reshape(group_rows, k_width)
    value_terms = jnp.einsum(
        "bkpo,pbkv->obv",
        attention_probabilities.astype(jnp.bfloat16),
        head_gradients,
        preferred_element_type=jnp.float32,
    ).reshape(group_rows, k_width)
    grad_keys, grad_values = (
        lax.psum_scatter(
            key_terms.astype(jnp.bfloat16), "shard", scatter_dimension=0, tiled=True
        ).astype(jnp.float32),
        lax.psum_scatter(
            value_terms.astype(jnp.bfloat16), "shard", scatter_dimension=0, tiled=True
        ).astype(jnp.float32),
    )
    grad_qkv = jnp.concatenate(
        (grad_queries, grad_keys.astype(jnp.bfloat16), grad_values.astype(jnp.bfloat16)), axis=1
    )
    grad_normed = jnp.einsum("tj,dj->td", grad_qkv, qkv_full, preferred_element_type=jnp.float32)
    columns_part = normed_b
    qkv_part = lax.psum_scatter(
        jnp.einsum("td,tj->dj", columns_part, grad_qkv, preferred_element_type=jnp.float32).astype(
            jnp.bfloat16
        ),
        "shard",
        scatter_dimension=0,
        tiled=True,
    )
    grad_resid_part, grad_gain_one = norm_back(residual, rms_one, gain_one, grad_normed)
    grad_tokens = (grad_middle + grad_resid_part).astype(jnp.bfloat16)
    qkv_sum, out_sum, gate_sum, up_sum, down_sum = (
        lax.psum(qkv_part, "rep").astype(jnp.float32),
        lax.psum(out_part, "rep").astype(jnp.float32),
        lax.psum(gate_part.astype(jnp.bfloat16), "rep").astype(jnp.float32),
        lax.psum(up_part.astype(jnp.bfloat16), "rep").astype(jnp.float32),
        lax.psum(down_part, "rep").astype(jnp.float32),
    )
    gain_sum_one, gain_sum_two, gain_sum_three, gain_sum_four = lax.psum(
        (grad_gain_one, grad_gain_two, grad_gain_three, grad_gain_four), ("rep", "shard")
    )
    return (
        output,
        grad_tokens,
        gain_sum_one,
        qkv_sum[:, :q_width],
        qkv_sum[:, q_width : q_width + k_width],
        qkv_sum[:, q_width + k_width :],
        out_sum,
        gain_sum_two,
        gain_sum_three,
        gate_sum,
        up_sum,
        down_sum,
        gain_sum_four,
    )


def solution(mesh):
    return jax.shard_map(
        body,
        mesh=mesh,
        in_specs=(
            P(("rep", "shard"), None),
            P(("rep", "shard")),
            P("rep", None),
            P(),
            P("shard", None),
            P("shard", None),
            P("shard", None),
            P("shard", None),
            P(),
            P(),
            P(None, "shard"),
            P(None, "shard"),
            P("shard", None),
            P(),
            P(("rep", "shard"), None),
        ),
        out_specs=(
            P(("rep", "shard"), None),
            P(("rep", "shard"), None),
            P(),
            P("shard", None),
            P("shard", None),
            P("shard", None),
            P("shard", None),
            P(),
            P(),
            P(None, "shard"),
            P(None, "shard"),
            P("shard", None),
            P(),
        ),
        check_vma=False,
    )
```

profile of v0, /device:TPU:0, one launch (start us, length us, event | category | flops | bytes accessed | tf_op | source)
XLA Modules:
  0.0 3851.8 jit_solution(6177591642241089158)
XLA Ops:
  7.2 4.1 pad_maximum_fusion
  13.3 176.8 %all-gather.8.cloned.1.call-done = bf16[2304,4096]{1,0:T(8,128)(2,1)} async-done(((bf16[576,4096]{1,0:T(8,128)(2,1)}), bf16[2304,4096]{1,0:T(8,128)(2,1)}) %all-gather.8.cloned.1.call-update) | async-done | bytes 18874384 | tf_op jit(solution)/shard_map/all_gather | solution.py:62
  190.1 10.3 convolution_convert_fusion.5
  200.4 0.9 fusion.88
  206.3 9.3 all-reduce
  218.1 14.5 all-gather.10.cloned.1.call-done
  232.6 2.9 reshape.285
  235.5 30.5 all-gather.12.cloned.1.call-done
  266.0 3.9 reshape.286
  269.9 3.1 fusion.38
  273.0 1.8 fusion.11
  274.8 2.1 fusion.47
  278.4 85.7 %all-gather.14.cloned.1.call-done = bf16[2048,2304]{1,0:T(8,128)(2,1)} async-done(((bf16[512,2304]{1,0:T(8,128)(2,1)}), bf16[2048,2304]{1,0:T(8,128)(2,1)}) %all-gather.14.cloned.1.call-update) | async-done | bytes 9437200 | tf_op jit(solution)/shard_map/all_gather | solution.py:63
  364.1 5.8 multiply_reduce_fusion.6
  373.0 364.6 %all-gather.16.cloned.1.call-done = bf16[2304,9216]{1,0:T(8,128)(2,1)} async-done(((bf16[2304,2304]{1,0:T(8,128)(2,1)}), bf16[2304,9216]{1,0:T(8,128)(2,1)}) %all-gather.16.cloned.1.call-update) | async-done | bytes 42467344 | tf_op jit(solution)/shard_map/all_gather | solution.py:130
  737.6 27.2 fusion.89
  764.8 346.4 %all-gather.18.cloned.1.call-done = bf16[2304,9216]{1,0:T(8,128)(2,1)} async-done(((bf16[2304,2304]{1,0:T(8,128)(2,1)}), bf16[2304,9216]{1,0:T(8,128)(2,1)}) %all-gather.18.cloned.1.call-update) | async-done | bytes 42467344 | tf_op jit(solution)/shard_map/all_gather | solution.py:131
  1111.2 29.0 multiply_convert_fusion.1
  1140.2 344.8 %all-gather.20.cloned.1.call-done = bf16[9216,2304]{1,0:T(8,128)(2,1)} async-done(((bf16[2304,2304]{1,0:T(8,128)(2,1)}), bf16[9216,2304]{1,0:T(8,128)(2,1)}) %all-gather.20.cloned.1.call-update) | async-done | bytes 42467344 | tf_op jit(solution)/shard_map/all_gather | solution.py:132
  1484.9 20.1 multiply_reduce_fusion.4
  1505.1 2.6 fusion.23
  1507.7 3.0 fusion.20
  1510.7 25.3 multiply_convert_fusion
  1536.1 21.7 fusion.90
  1557.8 22.4 multiply_reduce_fusion
  1580.3 3.2 multiply_reduce_fusion.1
  1584.8 7.9 convolution_convert_fusion.6
  1592.7 3.4 reshape.288
  1596.1 4.2 fusion.44
  1600.2 16.9 bitcast_convert_fusion.1
  1617.1 2.6 copy.59
  1619.9 5.6 bitcast_convert_fusion
  1625.4 2.9 copy.61
  1628.4 5.4 convolution_convert_fusion.4
  1633.9 1.4 copy-done.20
  1635.3 15.1 fusion.50
  1650.4 2.0 copy.57
  1652.5 1.5 convert_element_type.165
  1653.9 2.1 constant_dynamic-update-slice_fusion.2
  1656.0 1.8 constant_dynamic-update-slice_fusion.1
  1657.8 27.1 reduce-scatter.10.cloned.1.call-done
  1684.9 1.8 constant_dynamic-update-slice_fusion
  1686.7 11.0 convolution_convert_fusion.3
  1697.8 1.1 copy-done.6
  1698.9 20.7 convolution_convert_fusion.1
  1719.7 20.7 convolution_convert_fusion.2
  1740.5 1.1 copy-done.15
  1741.6 20.4 convolution_convert_fusion
  1762.2 21.3 reduce-scatter.14.cloned.1.call-done
  1783.5 174.6 %reduce-scatter.12.cloned.1.call-done = bf16[576,4096]{1,0:T(8,128)(2,1)} async-done(((bf16[2304,4096]{1,0:T(8,128)(2,1)}), bf16[576,4096]{1,0:T(8,128)(2,1)}) %reduce-scatter.12.cloned.1.call-update) | async-done | bytes 4718608 | tf_op jit(solution)/shard_map/reduce_scatter | solution.py:228
  1958.1 363.9 %reduce-scatter.18.cloned.1.call-done = bf16[2304,2304]{1,0:T(8,128)(2,1)} async-done(((bf16[2304,9216]{1,0:T(8,128)(2,1)}), bf16[2304,2304]{1,0:T(8,128)(2,1)}) %reduce-scatter.18.cloned.1.call-update) | async-done | bytes 10616848 | tf_op jit(solution)/shard_map/reduce_scatter | solution.py:169
  2321.9 363.7 %reduce-scatter.16.cloned.1.call-done = bf16[2304,2304]{1,0:T(8,128)(2,1)} async-done(((bf16[2304,9216]{1,0:T(8,128)(2,1)}), bf16[2304,2304]{1,0:T(8,128)(2,1)}) %reduce-scatter.16.cloned.1.call-update) | async-done | bytes 10616848 | tf_op jit(solution)/shard_map/reduce_scatter | solution.py:166
  2685.6 363.9 %reduce-scatter.20.cloned.1.call-done = bf16[2304,2304]{1,0:T(8,128)(2,1)} async-done(((bf16[9216,2304]{1,0:T(8,128)(2,1)}), bf16[2304,2304]{1,0:T(8,128)(2,1)}) %reduce-scatter.20.cloned.1.call-update) | async-done | bytes 10616848 | tf_op jit(solution)/shard_map/reduce_scatter | solution.py:146
  3049.5 14.6 fusion.33
  3064.1 42.3 %all-reduce.1 = (f32[2304]{0:T(1024)}, f32[2304]{0:T(1024)}, f32[2304]{0:T(1024)}, f32[2304]{0:T(1024)}) all-reduce(f32[2304]{0:T(1024)S(1)} %get-tuple-element.19, f32[2304]{0:T(1024)S(1)} %copy-done.31, f32[2304]{0:T(1024)S(1)} %copy-done.38, f32[2304]{0:T(1024)S(1)} %copy-done.30), channel_id=1, replica_groups=mesh['rep'=8,'shard'=4] {'rep','shard'}, use_global_device_ids=true, to_apply=%region_16.17 | all-reduce | flops 9216 | bytes 73728 | tf_op jit(solution)/shard_map/psum | solution.py:245
  3106.4 2.9 fusion.30
  3109.4 697.1 %all-reduce.5.cloned.1.call-done = (bf16[576,4096]{1,0:T(8,128)(2,1)}, bf16[512,2304]{1,0:T(8,128)(2,1)}, bf16[2304,2304]{1,0:T(8,128)(2,1)}, bf16[2304,2304]{1,0:T(8,128)(2,1)}, bf16[2304,2304]{1,0:T(8,128)(2,1)}) async-done(((bf16[576,4096]{1,0:T(8,128)(2,1)}, bf16[512,2304]{1,0:T(8,128)(2,1)}, bf16[2304,2304]{1,0:T(8,128)(2,1)}, bf16[2304,2304]{1,0:T(8,128)(2,1)}, bf16[2304,2304]{1,0:T(8,128)(2,1)}), ...) | async-done | bytes 38928400 | tf_op jit(solution)/shard_map/psum | solution.py:239
  3806.4 4.8 slice.27
  3811.3 2.9 fusion.87
  3814.2 1.2 copy-done.19
  3815.4 2.7 convert_element_type.177
  3818.2 10.5 convert_element_type.179
  3828.8 8.6 convert_element_type.181
  3837.5 7.6 convert_element_type.183
  (186 shorter events, 15.3 us)
Async XLA Ops:
  7.2 182.9 %all-gather.8.cloned.1.call-start = ((), (), s32[]{:S(2)}) async-start(), calls=%async_computation.7 | async-start | bytes 23592960 | tf_op jit(solution)/shard_map/all_gather | solution.py:62
  11.3 221.3 %all-gather.10.cloned.1.call-start = ((), (), s32[]{:S(2)}) async-start(), calls=%async_computation.8 | async-start | bytes 1966080 | tf_op jit(solution)/shard_map/all_gather | solution.py:75
  12.5 187.9 %copy-start.24 = (f32[2304]{0:T(1024)}, f32[2304]{0:T(1024)S(1)}, u32[]{:S(2)}) copy-start(f32[2304]{0:T(1024)S(1)} %convert_element_type.141) | copy-start | bytes 27652
  13.3 187.1 %copy-start.36 = (f32[192]{0:T(256)}, f32[192]{0:T(256)S(1)}, u32[]{:S(2)}) copy-start(f32[192]{0:T(256)S(1)} %get-tuple-element.42) | copy-start | bytes 2308
  201.4 64.6 %all-gather.12.cloned.1.call-start = ((), (), s32[]{:S(2)}) async-start(), calls=%async_computation.9 | async-start | bytes 1966080 | tf_op jit(solution)/shard_map/all_gather | solution.py:74
  202.1 162.0 %all-gather.14.cloned.1.call-start = ((), (), s32[]{:S(2)}) async-start(), calls=%async_computation.10 | async-start | bytes 11796480 | tf_op jit(solution)/shard_map/all_gather | solution.py:63
  202.7 534.9 %all-gather.16.cloned.1.call-start = ((), (), s32[]{:S(2)}) async-start(), calls=%async_computation.11 | async-start | bytes 53084160 | tf_op jit(solution)/shard_map/all_gather | solution.py:130
  203.3 907.9 %all-gather.18.cloned.1.call-start = ((), (), s32[]{:S(2)}) async-start(), calls=%async_computation.12 | async-start | bytes 53084160 | tf_op jit(solution)/shard_map/all_gather | solution.py:131
  203.9 11.7 copy-start.44
  203.9 11.7 copy-start.45
  203.9 12.3 copy-start.46
  203.9 12.9 copy-start.51
  203.9 1281.0 %all-gather.20.cloned.1.call-start = ((), (), s32[]{:S(2)}) async-start(), calls=%async_computation.13 | async-start | bytes 53084160 | tf_op jit(solution)/shard_map/all_gather | solution.py:132
  204.7 1451.3 %reduce-scatter.8.cloned.1.call-start = ((), (), s32[]{:S(2)}) async-start(), calls=%async_computation.14 | async-start | bytes 1966080 | tf_op jit(solution)/shard_map/reduce_scatter | solution.py:216
  217.4 57.4 %copy-start.22 = (pred[192,768]{1,0:T(8,128)(4,1)}, pred[192,768]{1,0:T(8,128)(4,1)S(1)}, u32[]{:S(2)}) copy-start(pred[192,768]{1,0:T(8,128)(4,1)S(1)} %fusion.60) | copy-start | bytes 442372
  218.1 54.9 %copy-start.21 = (bf16[192,4,2,256]{3,2,1,0:T(2,128)(2,1)}, bf16[192,4,2,256]{3,2,1,0:T(2,128)(2,1)S(1)}, u32[]{:S(2)}) copy-start(bf16[192,4,2,256]{3,2,1,0:T(2,128)(2,1)S(1)} %reshape.287) | copy-start | bytes 2359300
  235.5 39.4 %copy-start.9 = (bf16[768,4,256]{2,1,0:T(4,128)(2,1)}, bf16[768,4,256]{2,1,0:T(4,128)(2,1)S(1)}, u32[]{:S(2)}) copy-start(bf16[768,4,256]{2,1,0:T(4,128)(2,1)S(1)} %reshape.285) | copy-start | bytes 4718596
  273.0 3.9 copy-start.11
  273.0 3.9 copy-start.32
  278.4 91.5 %copy-start.12 = (bf16[192,2048]{1,0:T(8,128)(2,1)}, bf16[192,2048]{1,0:T(8,128)(2,1)S(1)}, u32[]{:S(2)}) copy-start(bf16[192,2048]{1,0:T(8,128)(2,1)S(1)} %convert_element_type.149) | copy-start | bytes 2359300
  278.4 93.8 %copy-start.33 = (f32[4,2,192]{2,1,0:T(2,128)S(1)}, f32[4,2,192]{2,1,0:T(2,128)}, u32[]{:S(2)}) copy-start(f32[4,2,192]{2,1,0:T(2,128)} %copy-done.32) | copy-start | bytes 18436
  278.4 93.8 %copy-start.35 = (f32[4,2,192]{2,1,0:T(2,128)S(1)}, f32[4,2,192]{2,1,0:T(2,128)}, u32[]{:S(2)}) copy-start(f32[4,2,192]{2,1,0:T(2,128)} %copy-done.34) | copy-start | bytes 18436
  278.4 94.4 %copy-start.26 = (f32[2304]{0:T(1024)S(1)}, f32[2304]{0:T(1024)}, u32[]{:S(2)}) copy-start(f32[2304]{0:T(1024)} %convert_element_type.151) | copy-start | bytes 27652
  372.2 392.6 %copy-start.39 = (f32[192]{0:T(256)}, f32[192]{0:T(256)S(1)}, u32[]{:S(2)}) copy-start(f32[192]{0:T(256)S(1)} %get-tuple-element.46) | copy-start | bytes 2308
  373.0 738.2 %copy-start.5 = (bf16[192,2304]{1,0:T(8,128)(2,1)}, bf16[192,2304]{1,0:T(8,128)(2,1)S(1)}, u32[]{:S(2)}) copy-start(bf16[192,2304]{1,0:T(8,128)(2,1)S(1)} %multiply_convert_fusion.2) | copy-start | bytes 2654212
  1484.9 20.2 copy-start.7
  1484.9 20.2 copy-start.29
  1510.7 25.3 copy-start.14
  1536.1 21.7 copy-start.27
  1536.1 21.7 copy-start.40
  1557.7 22.5 copy-start.2
  1557.7 22.5 copy-start.8
  1557.8 22.5 copy-start.28
  1557.8 22.5 copy-start.41
  1557.8 22.5 copy-start.48
  1580.2 3.2 copy-start.50
  1584.8 11.3 copy-start.10
  1592.7 7.6 copy-start.23
  1592.7 7.6 copy-start.42
  1619.8 65.1 %reduce-scatter.10.cloned.1.call-start = ((), (), s32[]{:S(2)}) async-start(), calls=%async_computation.15 | async-start | bytes 1966080 | tf_op jit(solution)/shard_map/reduce_scatter | solution.py:219
  1628.3 155.1 %reduce-scatter.14.cloned.1.call-start = ((), (), s32[]{:S(2)}) async-start(), calls=%async_computation.17 | async-start | bytes 11796480 | tf_op jit(solution)/shard_map/reduce_scatter | solution.py:181
  1633.9 324.2 %reduce-scatter.12.cloned.1.call-start = ((), (), s32[]{:S(2)}) async-start(), calls=%async_computation.16 | async-start | bytes 23592960 | tf_op jit(solution)/shard_map/reduce_scatter | solution.py:228
  1650.4 36.2 copy-start.4
  1650.4 36.2 copy-start.25
  1650.4 36.2 copy-start.37
  1697.7 624.2 %reduce-scatter.18.cloned.1.call-start = ((), (), s32[]{:S(2)}) async-start(), calls=%async_computation.19 | async-start | bytes 53084160 | tf_op jit(solution)/shard_map/reduce_scatter | solution.py:169
  1719.6 966.0 %reduce-scatter.16.cloned.1.call-start = ((), (), s32[]{:S(2)}) async-start(), calls=%async_computation.18 | async-start | bytes 53084160 | tf_op jit(solution)/shard_map/reduce_scatter | solution.py:166
  1740.4 1309.0 %reduce-scatter.20.cloned.1.call-start = ((), (), s32[]{:S(2)}) async-start(), calls=%async_computation.20 | async-start | bytes 53084160 | tf_op jit(solution)/shard_map/reduce_scatter | solution.py:146
  1762.0 2044.4 %all-reduce.5.cloned.1.call-start = ((), (), s32[]{:S(2)}) async-start(), calls=%async_computation.21 | async-start | bytes 77856768 | tf_op jit(solution)/shard_map/psum | solution.py:239
  3049.5 14.6 copy-start.30
  3049.5 14.6 copy-start.31
  3049.5 14.6 copy-start.38
  3049.5 56.9 %copy-start.47 = (f32[192]{0:T(256)S(1)}, f32[192]{0:T(256)}, u32[]{:S(2)}) copy-start(f32[192]{0:T(256)} %get-tuple-element.41) | copy-start | bytes 2308
  3806.4 4.8 copy-start
  3806.4 11.8 slice-start.6
  3806.4 11.8 slice-start.7
  3811.3 4.2 copy-start.19
  3811.3 6.9 slice-start.8
  3815.4 13.3 slice-start.3
  3818.2 10.6 slice-start.4
  3818.2 10.6 slice-start.5
  3818.2 19.2 slice-start
  3818.2 19.2 slice-start.1
  3828.8 8.7 slice-start.2
  (13 other events, 20.4 us)
Sparse Core Ops, SparseCore 0:
  11.4 178.6 all-gather.7
  201.5 31.0 all-gather.9
  235.0 30.9 all-gather.11
  267.7 96.3 all-gather.13
  365.8 371.7 all-gather.15
  739.4 371.7 all-gather.17
  1113.1 371.8 all-gather.19
  1619.9 30.9 reduce-scatter.7
  1653.9 30.9 reduce-scatter.9
  1688.4 95.0 reduce-scatter.13
  1787.2 170.8 reduce-scatter.11
  1961.3 360.5 reduce-scatter.17
  2325.0 360.5 reduce-scatter.15
  2688.9 360.5 reduce-scatter.19
  3052.5 753.9 all-reduce.4
where the time goes:
time: 3860 us; the launch traced here: 3850 us
  waiting for transfers between devices  3380 us (88%)
  matrix products  309 us (8%)
  other arithmetic  52.7 us (1%)
  blocking collectives  51.6 us (1%)
  local copies, waits for them, and re-layouts  44.1 us (1%)
    psum x1, waiting for transfers between devices, body(): lax.psum(qkv_part, 'rep').astype(jnp.float32)  697 us
    all_gather x1, waiting for transfers between devices, body(): lax.all_gather(w_gate, 'shard', axis=1, tiled=True)  365 us
    reduce_scatter x1, waiting for transfers between devices, body(): lax.psum_scatter(jnp.einsum('tf,td->fd', columns_part, grad_ffn_b, prefer...  364 us
    reduce_scatter x1, waiting for transfers between devices, body(): lax.psum_scatter(up_term.astype(jnp.bfloat16), 'shard', scatter_dimension...  364 us
    reduce_scatter x1, waiting for transfers between devices, body(): lax.psum_scatter(gate_term.astype(jnp.bfloat16), 'shard', scatter_dimensi...  364 us
    all_gather x1, waiting for transfers between devices, body(): lax.all_gather(w_up, 'shard', axis=1, tiled=True)  346 us
    all_gather x1, waiting for transfers between devices, body(): lax.all_gather(w_down, 'shard', axis=0, tiled=True)  345 us
    all_gather x1, waiting for transfers between devices, body(): lax.all_gather(qkv_local, 'shard', axis=0, tiled=True)  177 us
  transfers between devices with their start and end apart: 15, of which 14 were waited for; matrix products, arithmetic and copies ran while one was open for 6% of the time, Pallas kernels for 0%

commit v1 on v0

v1 whole, which is shorter than its diff:
```python
import jax
import jax.numpy as jnp
from jax import lax
from jax.sharding import PartitionSpec as P

QUERY_HEADS = 8
KV = 4
HEAD_SIZE = 256
SEGS = 13


softcap = 50.0
norm_eps = 1e-06


def normalize(values, gain_vec):
    inv_rms = lax.rsqrt(jnp.mean(values * values, axis=-1, keepdims=True) + norm_eps)
    return (values * inv_rms * gain_vec, inv_rms)


def norm_back(values, inv_rms, gain_vec, grad_in):
    weighted = grad_in * gain_vec
    row_mean = jnp.mean(weighted * values, axis=-1, keepdims=True)
    grad_back = inv_rms * weighted - values * (inv_rms * inv_rms * inv_rms) * row_mean
    return (grad_back, jnp.sum(grad_in * values * inv_rms, axis=0))


def geglu(gate_pre, up_pre):
    return jax.nn.gelu(gate_pre, approximate=True) * up_pre


def gather_rows(block):
    return lax.all_gather(block, "shard", axis=0, tiled=True)


def scatter_rows(partial):
    return lax.psum_scatter(partial, "shard", scatter_dimension=0, tiled=True)


def rep_sum(grads):
    return [lax.psum(grad, "rep").astype(jnp.float32) for grad in grads]


def body(
    tokens,
    seg_ids,
    parents,
    attn_gain,
    w_query,
    w_key,
    w_value,
    w_out,
    post_attn_gain,
    ffn_gain,
    w_gate,
    w_up,
    w_down,
    post_ffn_gain,
    cotangent,
):
    f32, bf16 = jnp.float32, jnp.bfloat16
    tok_rows, width = tokens.shape
    n = lax.axis_size("shard")
    me = lax.axis_index("shard")
    group_rows = tok_rows * n
    part_rows = w_query.shape[0]
    head_scale = HEAD_SIZE ** (-0.5)
    q_heads = QUERY_HEADS // n
    kv_heads = max(1, KV // n)
    share = n * kv_heads // KV
    repeat = q_heads // kv_heads
    q_cols = q_heads * HEAD_SIZE
    k_cols = kv_heads * HEAD_SIZE
    gain_one = attn_gain.astype(f32)
    gain_two = post_attn_gain.astype(f32)
    gain_three = ffn_gain.astype(f32)
    gain_four = post_ffn_gain.astype(f32)

    def by_device(weight):
        heads = weight.reshape(part_rows, KV, -1)
        if share > 1:
            heads = jnp.repeat(heads, share, axis=1)
        return heads.reshape(part_rows, n, -1)

    qkv_parts = jnp.concatenate(
        (w_query.reshape(part_rows, n, q_cols), by_device(w_key), by_device(w_value)), axis=2
    ).transpose(1, 0, 2)
    qkv_heads = lax.all_to_all(qkv_parts, "shard", 0, 0, tiled=True).reshape(width, -1)

    residual = tokens.astype(f32)
    normed, rms_one = normalize(residual, gain_one)
    normed_all = gather_rows(normed.astype(bf16))
    codes = gather_rows(seg_ids.astype(bf16)).astype(jnp.int32)
    qkv = jnp.dot(normed_all, qkv_heads, preferred_element_type=f32).astype(bf16)
    queries = qkv[:, :q_cols].reshape(group_rows, kv_heads, repeat, HEAD_SIZE)
    keys = qkv[:, q_cols : q_cols + k_cols].reshape(group_rows, kv_heads, HEAD_SIZE)
    values = qkv[:, q_cols + k_cols :].reshape(group_rows, kv_heads, HEAD_SIZE)

    parent_row = parents[0]
    labels = jnp.arange(SEGS)

    def lookup(ident):
        return jnp.sum(jnp.where(ident[:, None] == labels[None, :], parent_row[None, :], 0), axis=1)

    parent_one = lookup(codes)
    parent_two = lookup(parent_one)
    positions = jnp.arange(group_rows)
    real = codes < SEGS
    related = (
        (codes[None, :] == codes[:, None])
        | (codes[None, :] == parent_one[:, None])
        | (codes[None, :] == parent_two[:, None])
    )
    visible = (positions[None, :] <= positions[:, None]) & real[:, None] & real[
        None, :
    ] & related | (positions[None, :] == positions[:, None])

    score_matrix = jnp.einsum("tkrh,skh->krts", queries, keys, preferred_element_type=f32)
    tanh_part = jnp.tanh(score_matrix * (head_scale / softcap))
    masked = jnp.where(visible[None, None], softcap * tanh_part, -1e30)
    row_max = jnp.max(masked, axis=-1, keepdims=True)
    expo_terms = jnp.exp(masked - row_max)
    row_total = jnp.sum(expo_terms, axis=-1, keepdims=True)
    probs = expo_terms / row_total
    probs_b = probs.astype(bf16)
    mixed = jnp.einsum("krts,skh->tkrh", probs_b, values, preferred_element_type=f32)
    mixed = mixed.reshape(group_rows, q_cols).astype(bf16)
    attn_out = scatter_rows(
        jnp.dot(mixed, w_out, preferred_element_type=f32).astype(bf16)
    ).astype(f32)
    post_one, rms_two = normalize(attn_out, gain_two)
    middle = residual + post_one
    normed_two, rms_three = normalize(middle, gain_three)
    normed_two_all = gather_rows(normed_two.astype(bf16))
    gate_pre = jnp.dot(normed_two_all, w_gate, preferred_element_type=f32)
    up_pre = jnp.dot(normed_two_all, w_up, preferred_element_type=f32)
    hidden, geglu_back = jax.vjp(geglu, gate_pre, up_pre)
    hidden_b = hidden.astype(bf16)
    ffn_out = scatter_rows(
        jnp.dot(hidden_b, w_down, preferred_element_type=f32).astype(bf16)
    ).astype(f32)
    post_two, rms_four = normalize(ffn_out, gain_four)
    output = (middle + post_two).astype(bf16)

    grad_out = cotangent.astype(f32)
    grad_ffn, grad_gain_four = norm_back(ffn_out, rms_four, gain_four, grad_out)
    grad_ffn_all = gather_rows(grad_ffn.astype(bf16))
    down_part = jnp.einsum("tf,td->fd", hidden_b, grad_ffn_all, preferred_element_type=f32)
    grad_hidden = jnp.einsum("td,fd->tf", grad_ffn_all, w_down, preferred_element_type=f32)
    grad_gate, grad_up = geglu_back(grad_hidden)
    grad_gate_b = grad_gate.astype(bf16)
    grad_up_b = grad_up.astype(bf16)
    grad_normed_two = jnp.einsum("tf,df->td", grad_gate_b, w_gate, preferred_element_type=f32)
    grad_normed_two += jnp.einsum("tf,df->td", grad_up_b, w_up, preferred_element_type=f32)
    grad_normed_two = scatter_rows(grad_normed_two.astype(bf16)).astype(f32)
    gate_part = jnp.einsum("td,tf->df", normed_two_all, grad_gate_b, preferred_element_type=f32)
    up_part = jnp.einsum("td,tf->df", normed_two_all, grad_up_b, preferred_element_type=f32)
    grad_middle_part, grad_gain_three = norm_back(middle, rms_three, gain_three, grad_normed_two)
    grad_middle = grad_out + grad_middle_part
    grad_attn, grad_gain_two = norm_back(attn_out, rms_two, gain_two, grad_middle)
    grad_attn_all = gather_rows(grad_attn.astype(bf16))
    out_part = jnp.einsum("tj,td->jd", mixed, grad_attn_all, preferred_element_type=f32)
    grad_mixed = jnp.einsum("td,jd->tj", grad_attn_all, w_out, preferred_element_type=f32)
    grad_mixed = grad_mixed.astype(bf16).reshape(group_rows, kv_heads, repeat, HEAD_SIZE)
    grad_probs = jnp.einsum("tkrh,skh->krts", grad_mixed, values, preferred_element_type=f32)
    row_inner = jnp.sum(probs * grad_probs, axis=-1, keepdims=True)
    grad_dots = (
        probs * (grad_probs - row_inner) * (1.0 - tanh_part * tanh_part) * head_scale
    ).astype(bf16)
    grad_queries = jnp.einsum("krts,skh->tkrh", grad_dots, keys, preferred_element_type=f32)
    grad_keys = jnp.einsum("krts,tkrh->skh", grad_dots, queries, preferred_element_type=f32)
    grad_values = jnp.einsum("krts,tkrh->skh", probs_b, grad_mixed, preferred_element_type=f32)
    grad_parts = jnp.concatenate(
        (
            grad_queries.reshape(group_rows, q_cols),
            grad_keys.reshape(group_rows, k_cols),
            grad_values.reshape(group_rows, k_cols),
        ),
        axis=1,
    ).astype(bf16)
    grad_parts = lax.all_gather(grad_parts, "shard", axis=0)

    def whole_heads(parts):
        if share > 1:
            parts = parts.reshape(KV, share, group_rows, HEAD_SIZE).astype(f32).sum(axis=1).astype(bf16)
        return parts.transpose(1, 0, 2).reshape(group_rows, -1)

    grad_qkv = jnp.concatenate(
        (
            grad_parts[:, :, :q_cols].transpose(1, 0, 2).reshape(group_rows, -1),
            whole_heads(grad_parts[:, :, q_cols : q_cols + k_cols]),
            whole_heads(grad_parts[:, :, q_cols + k_cols :]),
        ),
        axis=1,
    )
    qkv_local = jnp.concatenate((w_query, w_key, w_value), axis=1)
    grad_normed = jnp.einsum("tj,dj->td", grad_qkv, qkv_local, preferred_element_type=f32)
    grad_normed = lax.all_to_all(
        grad_normed.astype(bf16).reshape(n, tok_rows, part_rows), "shard", 0, 0, tiled=True
    )
    grad_normed = grad_normed.transpose(1, 0, 2).reshape(tok_rows, width).astype(f32)
    normed_cols = lax.dynamic_slice_in_dim(normed_all, me * part_rows, part_rows, axis=1)
    qkv_part = jnp.einsum("td,tj->dj", normed_cols, grad_qkv, preferred_element_type=f32)
    grad_resid_part, grad_gain_one = norm_back(residual, rms_one, gain_one, grad_normed)
    grad_tokens = (grad_middle + grad_resid_part).astype(bf16)
    qkv_sum, out_sum, gate_sum, up_sum, down_sum = rep_sum(
        [part.astype(bf16) for part in (qkv_part, out_part, gate_part, up_part, down_part)]
    )
    gain_sum_one, gain_sum_two, gain_sum_three, gain_sum_four = lax.psum(
        (grad_gain_one, grad_gain_two, grad_gain_three, grad_gain_four), ("rep", "shard")
    )
    q_width = w_query.shape[1]
    k_width = w_key.shape[1]
    return (
        output,
        grad_tokens,
        gain_sum_one,
        qkv_sum[:, :q_width],
        qkv_sum[:, q_width : q_width + k_width],
        qkv_sum[:, q_width + k_width :],
        out_sum,
        gain_sum_two,
        gain_sum_three,
        gate_sum,
        up_sum,
        down_sum,
        gain_sum_four,
    )


def solution(mesh):
    return jax.shard_map(
        body,
        mesh=mesh,
        in_specs=(
            P(("rep", "shard"), None),
            P(("rep", "shard")),
            P("rep", None),
            P(),
            P("shard", None),
            P("shard", None),
            P("shard", None),
            P("shard", None),
            P(),
            P(),
            P(None, "shard"),
            P(None, "shard"),
            P("shard", None),
            P(),
            P(("rep", "shard"), None),
        ),
        out_specs=(
            P(("rep", "shard"), None),
            P(("rep", "shard"), None),
            P(),
            P("shard", None),
            P("shard", None),
            P("shard", None),
            P("shard", None),
            P(),
            P(),
            P(None, "shard"),
            P(None, "shard"),
            P("shard", None),
            P(),
        ),
        check_vma=False,
    )
```

time: 3860 us -> 1470 us (0.38)
  waiting for transfers between devices: 3380 us -> 986 us
  matrix products: 309 us -> 183 us
  blocking collectives: 51.6 us -> 133 us
    all_gather x7 -> x5, waiting for transfers between devices: 1360 us -> 172 us  [the longest x4 141 us: gather_rows(): return lax.all_gather(block, 'shard', axis=0, tiled=True)]
    reduce_scatter x7 -> x3, waiting for transfers between devices: 1310 us -> 141 us  [scatter_rows(): return lax.psum_scatter(partial, 'shard', scatter_dimension=0, tiled=True)]
    dot_general x21, matrix products: 309 us -> 183 us  [the longest x1 21.8 us: body(): jnp.einsum('td,fd->tf', grad_ffn_all, w_down, preferred_element_type=f32)]
    unnamed x1, blocking collectives: 9.29 us -> 74.6 us
  transfers between devices with their start and end apart: 15 -> 10, of which waited for: 14 -> 8; matrix products, arithmetic and copies ran while one was open for 6% -> 6% of each run, Pallas kernels for 0% -> 0%
where the time goes in v1:
time: 1470 us; the launch traced here: 1460 us
  waiting for transfers between devices  986 us (67%)
  matrix products  183 us (12%)
  blocking collectives  133 us (9%)
  other arithmetic  72.8 us (5%)
  local copies, waits for them, and re-layouts  63.6 us (4%)
  between operations  15.1 us (1%)
    psum x1, waiting for transfers between devices, rep_sum(): return [lax.psum(grad, 'rep').astype(jnp.float32) for grad in grads]  673 us
    all_gather x4, waiting for transfers between devices, gather_rows(): return lax.all_gather(block, 'shard', axis=0, tiled=True)  141 us
    reduce_scatter x3, waiting for transfers between devices, scatter_rows(): return lax.psum_scatter(partial, 'shard', scatter_dimension=0, tiled=True)  141 us
    unnamed x1, blocking collectives  74.6 us
    psum x1, blocking collectives, body(): lax.psum((grad_gain_one, grad_gain_two, grad_gain_three, grad_gain_four),...  42.1 us
    all_gather x1, waiting for transfers between devices, body(): grad_parts = lax.all_gather(grad_parts, 'shard', axis=0)  31.1 us
    convert_element_type x4, other arithmetic, rep_sum(): return [lax.psum(grad, 'rep').astype(jnp.float32) for grad in grads]  29.5 us
  transfers between devices with their start and end apart: 10, of which 8 were waited for; matrix products, arithmetic and copies ran while one was open for 6% of the time, Pallas kernels for 0%

profile of v1, /device:TPU:0, one launch (start us, length us, event | category | flops | bytes accessed | tf_op | source)
XLA Modules:
  0.0 1461.1 jit_solution(17044944784730753573)
XLA Ops:
  7.2 1.6 fusion.55
  10.1 2.4 fusion.57
  12.5 3.5 reshape.381
  16.0 3.5 reshape.382
  19.5 6.2 reshape.380
  25.7 5.1 maximum_bitcast_fusion
  30.8 3.8 copy.94
  34.6 5.3 all-to-all-start
  41.4 74.6 %all-reduce = bf16[768]{0:T(1024)(128)(2,1)S(1)} all-reduce(bf16[768]{0:T(1024)(128)(2,1)S(1)} %dynamic-update-slice), channel_id=1, replica_groups=mesh['rep'=8,'shard'=4] {'shard'}, use_global_device_ids=true, to_apply=%add | all-reduce | flops 768 | bytes 3072
  117.8 7.4 convolution_convert_fusion.7
  127.3 2.3 copy.124
  129.6 2.6 fusion.19
  133.6 3.2 fusion.68
  137.7 3.8 convolution_convert_fusion.5
  142.2 46.8 %reduce-scatter.4.cloned.1.call-done = bf16[192,2304]{1,0:T(8,128)(2,1)} async-done(((bf16[768,2304]{1,0:T(8,128)(2,1)}), bf16[192,2304]{1,0:T(8,128)(2,1)}) %reduce-scatter.4.cloned.1.call-update) | async-done | bytes 884752 | tf_op jit(solution)/shard_map/reduce_scatter | solution.py:37
  190.4 1.7 multiply_reduce_fusion
  192.2 2.6 multiply_convert_fusion.2
  195.1 47.1 %all-gather.8.cloned.1.call-done = bf16[768,2304]{1,0:T(8,128)(2,1)} async-done(((bf16[192,2304]{1,0:T(8,128)(2,1)}), bf16[768,2304]{1,0:T(8,128)(2,1)}) %all-gather.8.cloned.1.call-update) | async-done | bytes 3538960 | tf_op jit(solution)/shard_map/all_gather | solution.py:33
  242.2 15.0 %fusion.92 = f32[768,2304]{1,0:T(8,128)} fusion(bf16[768,2304]{1,0:T(8,128)(2,1)} %all-gather.8.cloned.1.call-done, bf16[2304,2304]{1,0:T(8,128)(2,1)} %param.25), kind=kOutput, calls=%fused_computation.150 | convolution fusion | flops 8153726976 | bytes 21233664 | tf_op jit(solution)/shard_map/dot_general | solution.py:135
  257.2 15.8 %multiply_convert_fusion.1 = (bf16[768,2304]{1,0:T(8,128)(2,1)}, f32[768,2304]{1,0:T(8,128)}) fusion(f32[768,2304]{1,0:T(8,128)} %fusion.92, bf16[768,2304]{1,0:T(8,128)(2,1)S(1)} %copy-done.25, bf16[2304,2304]{1,0:T(8,128)(2,1)} %param.26), kind=kOutput, calls=%fused_computation.14 | convolution fusion | flops 8171421696 | bytes 31850496 | tf_op jit(solution)/shard_map/dot_general | solution.py:136
  273.1 11.3 convolution_convert_fusion.4
  285.0 46.7 %reduce-scatter.6.cloned.1.call-done = bf16[192,2304]{1,0:T(8,128)(2,1)} async-done(((bf16[768,2304]{1,0:T(8,128)(2,1)}), bf16[192,2304]{1,0:T(8,128)(2,1)}) %reduce-scatter.6.cloned.1.call-update) | async-done | bytes 884752 | tf_op jit(solution)/shard_map/reduce_scatter | solution.py:37
  333.2 2.6 fusion.54
  335.8 2.8 fusion.34
  339.1 46.9 %all-gather.10.cloned.1.call-done = bf16[768,2304]{1,0:T(8,128)(2,1)} async-done(((bf16[192,2304]{1,0:T(8,128)(2,1)}), bf16[768,2304]{1,0:T(8,128)(2,1)}) %all-gather.10.cloned.1.call-update) | async-done | bytes 3538960 | tf_op jit(solution)/shard_map/all_gather | solution.py:33
  386.0 21.8 %multiply_convert_fusion = (bf16[768,2304]{1,0:T(8,128)(2,1)}, bf16[768,2304]{1,0:T(8,128)(2,1)}) fusion(f32[768,2304]{1,0:T(8,128)} %fusion.92, f32[768,2304]{1,0:T(8,128)} %get-tuple-element.49, bf16[768,2304]{1,0:T(8,128)(2,1)} %all-gather.10.cloned.1.call-done, bf16[2304,2304]{1,0:T(8,128)(2,1)} %param.27), kind=kOutput, calls=%fused_computation.13 | convolution fusion | flops 8196194304 | bytes 35389440 | tf_op jit(solution)/shard_map/td,fd->tf/dot_general | solution.py:149
  407.8 14.9 %fusion.93 = f32[768,2304]{1,0:T(8,128)} fusion(bf16[768,2304]{1,0:T(8,128)(2,1)} %get-tuple-element.32, bf16[2304,2304]{1,0:T(8,128)(2,1)} %param.25), kind=kOutput, calls=%fused_computation.151 | convolution fusion | flops 8153726976 | bytes 21233664 | tf_op jit(solution)/shard_map/tf,df->td/dot_general | solution.py:153
  422.7 15.5 %add_convert_fusion = bf16[768,2304]{1,0:T(8,128)(2,1)} fusion(f32[768,2304]{1,0:T(8,128)} %fusion.93, bf16[768,2304]{1,0:T(8,128)(2,1)} %get-tuple-element.31, bf16[2304,2304]{1,0:T(8,128)(2,1)} %param.26), kind=kOutput, calls=%fused_computation.12 | convolution fusion | flops 8157265920 | bytes 24772608 | tf_op jit(solution)/shard_map/tf,df->td/dot_general | solution.py:154
  438.4 47.2 %reduce-scatter.8.cloned.1.call-done = bf16[192,2304]{1,0:T(8,128)(2,1)} async-done(((bf16[768,2304]{1,0:T(8,128)(2,1)}), bf16[192,2304]{1,0:T(8,128)(2,1)}) %reduce-scatter.8.cloned.1.call-update) | async-done | bytes 884752 | tf_op jit(solution)/shard_map/reduce_scatter | solution.py:37
  485.5 2.3 fusion.38
  487.9 4.7 fusion.46
  495.2 47.3 %all-gather.12.cloned.1.call-done = bf16[768,2304]{1,0:T(8,128)(2,1)} async-done(((bf16[192,2304]{1,0:T(8,128)(2,1)}), bf16[768,2304]{1,0:T(8,128)(2,1)}) %all-gather.12.cloned.1.call-update) | async-done | bytes 3538960 | tf_op jit(solution)/shard_map/all_gather | solution.py:33
  542.5 4.2 convolution_convert_fusion.9
  546.8 5.3 fusion.78
  552.1 2.1 fusion.15
  554.2 2.5 fusion.20
  556.7 1.7 convolution_convert_fusion.8
  558.4 1.6 fusion.81
  565.4 13.8 convolution_convert_fusion
  579.2 10.7 convolution_convert_fusion.1
  589.9 11.0 convolution_convert_fusion.2
  600.9 3.4 convolution_convert_fusion.6
  604.4 31.1 %all-gather.14.cloned.1.call-done = bf16[4,768,1024]{2,1,0:T(8,128)(2,1)} async-done(((bf16[1,768,1024]{2,1,0:T(8,128)(2,1)}), bf16[4,768,1024]{2,1,0:T(8,128)(2,1)}) %all-gather.14.cloned.1.call-update) | async-done | bytes 6291472 | tf_op jit(solution)/shard_map/all_gather | solution.py:181
  635.4 3.2 fusion.90
  638.7 3.0 copy.122
  641.6 3.8 slice.39
  645.4 4.6 copy.121
  650.0 1.6 copy.123
  651.6 10.1 convolution_convert_fusion.3
  661.7 1.6 copy-done.11
  663.3 8.3 fusion.65
  673.1 16.5 %all_to_all.10 = bf16[4,192,576]{2,1,0:T(8,128)(2,1)S(1)} all-to-all(bf16[4,192,576]{2,1,0:T(8,128)(2,1)S(1)} %bitcast.167), channel_id=1, replica_groups=mesh['rep'=8,'shard'=4] {'shard'}, dimensions={0} | all-to-all | bytes 1769472 | tf_op jit(solution)/shard_map/all_to_all | solution.py:198
  689.7 2.5 copy.111
  692.3 3.4 reshape.394
  695.6 2.0 fusion.64
  697.6 42.1 %all-reduce.1 = (f32[2304]{0:T(1024)}, f32[2304]{0:T(1024)}, f32[2304]{0:T(1024)}, f32[2304]{0:T(1024)}) all-reduce(f32[2304]{0:T(1024)S(1)} %get-tuple-element.17, f32[2304]{0:T(1024)S(1)} %get-tuple-element.15, f32[2304]{0:T(1024)S(1)} %get-tuple-element.13, ...), channel_id=1, replica_groups=mesh['rep'=8,'shard'=4] {'rep','shard'}, use_global_device_ids=true, to_apply=%region_17.18 | all-reduce | flops 9216 | bytes 73728 | tf_op jit(solution)/shard_map/psum | solution.py:209
  739.8 2.9 fusion.61
  742.7 673.1 %all-reduce.5.cloned.1.call-done = (bf16[576,4096]{1,0:T(8,128)(2,1)}, bf16[512,2304]{1,0:T(8,128)(2,1)}, bf16[2304,2304]{1,0:T(8,128)(2,1)}, bf16[2304,2304]{1,0:T(8,128)(2,1)}, bf16[2304,2304]{1,0:T(8,128)(2,1)}) async-done(((bf16[576,4096]{1,0:T(8,128)(2,1)}, bf16[512,2304]{1,0:T(8,128)(2,1)}, bf16[2304,2304]{1,0:T(8,128)(2,1)}, bf16[2304,2304]{1,0:T(8,128)(2,1)}, bf16[2304,2304]{1,0:T(8,128)(2,1)}), ...) | async-done | bytes 38928400 | tf_op jit(solution)/shard_map/psum | solution.py:41
  1415.8 4.8 slice.42
  1420.6 2.9 fusion.91
  1424.8 2.7 convert_element_type.181
  1427.6 10.5 convert_element_type.183
  1438.1 8.7 convert_element_type.185
  1446.8 7.6 convert_element_type.187
  (152 shorter events, 24.6 us)
Async XLA Ops:
  7.2 130.5 %copy-start = (bf16[512,2304]{1,0:T(8,128)(2,1)S(1)}, bf16[512,2304]{1,0:T(8,128)(2,1)}, u32[]{:S(2)}) copy-start(bf16[512,2304]{1,0:T(8,128)(2,1)} %param.22) | copy-start | bytes 7077892
  7.2 110.6 %all-gather.6.cloned.1.call-start = ((), (), s32[]{:S(2)}) async-start(), calls=%async_computation.5 | async-start | bytes 4423680 | tf_op jit(solution)/shard_map/all_gather | solution.py:33
  9.4 10.1 copy-start.18
  10.1 9.4 copy-start.15
  34.6 5.3 copy-start.28
  34.6 5.3 copy-start.31
  34.6 81.4 %copy-start.24 = (s32[1,13]{1,0:T(1,128)S(1)}, s32[1,13]{1,0:T(1,128)}, u32[]{:S(2)}) copy-start(s32[1,13]{1,0:T(1,128)} %param.17) | copy-start | bytes 160
  34.6 83.1 %all-to-all-start = ((bf16[4,576,1024]{2,1,0:T(8,128)(2,1)}), bf16[4,576,1024]{2,1,0:T(8,128)(2,1)}, u32[]{:S(2)}, u32[]{:S(2)}) async-start(bf16[4,576,1024]{2,1,0:T(8,128)(2,1)} %copy.94), calls=%async_computation | async-start | bytes 9437184 | tf_op jit(solution)/shard_map/all_to_all | solution.py:88
  39.9 149.1 %reduce-scatter.4.cloned.1.call-start = ((), (), s32[]{:S(2)}) async-start(), calls=%async_computation.6 | async-start | bytes 4423680 | tf_op jit(solution)/shard_map/reduce_scatter | solution.py:37
  117.8 15.9 %copy-start.8 = (pred[768,768]{0,1:T(8,128)(4,1)}, pred[768,768]{0,1:T(8,128)(4,1)S(1)}, u32[]{:S(2)}) copy-start(pred[768,768]{0,1:T(8,128)(4,1)S(1)} %fusion.28) | copy-start | bytes 1769476
  125.2 1.1 copy-start.13
  132.2 4.7 copy-start.4
  136.8 0.9 copy-start.29
  141.5 0.7 copy-start.20
  141.5 0.7 copy-start.21
  141.5 48.9 %copy-start.2 = (bf16[192,2304]{1,0:T(8,128)(2,1)S(1)}, bf16[192,2304]{1,0:T(8,128)(2,1)}, u32[]{:S(2)}) copy-start(bf16[192,2304]{1,0:T(8,128)(2,1)} %param.15) | copy-start | bytes 2654212
  141.6 100.7 %all-gather.8.cloned.1.call-start = ((), (), s32[]{:S(2)}) async-start(), calls=%async_computation.7 | async-start | bytes 4423680 | tf_op jit(solution)/shard_map/all_gather | solution.py:33
  194.8 136.9 %reduce-scatter.6.cloned.1.call-start = ((), (), s32[]{:S(2)}) async-start(), calls=%async_computation.8 | async-start | bytes 4423680 | tf_op jit(solution)/shard_map/reduce_scatter | solution.py:37
  242.2 15.0 %copy-start.25 = (bf16[768,2304]{1,0:T(8,128)(2,1)S(1)}, bf16[768,2304]{1,0:T(8,128)(2,1)}, u32[]{:S(2)}) copy-start(bf16[768,2304]{1,0:T(8,128)(2,1)} %all-gather.8.cloned.1.call-done) | copy-start | bytes 10616836
  242.2 30.8 %slice-start.11 = ((s8[10616832]{0:T(1024)(128)(4,1)}), s8[4194304]{0:T(1024)(128)(4,1)S(1)}, s32[]{:S(2)}) async-start(s8[10616832]{0:T(1024)(128)(4,1)} %bitcast.179), calls=%async_computation.25 | async-start | bytes 8388608
  242.2 30.8 %slice-start.12 = ((s8[10616832]{0:T(1024)(128)(4,1)}), s8[4194304]{0:T(1024)(128)(4,1)S(1)}, s32[]{:S(2)}) async-start(s8[10616832]{0:T(1024)(128)(4,1)} %bitcast.179), calls=%async_computation.26 | async-start | bytes 8388608
  257.2 15.8 %slice-start.13 = ((s8[10616832]{0:T(1024)(128)(4,1)}), s8[2228224]{0:T(1024)(128)(4,1)S(1)}, s32[]{:S(2)}) async-start(s8[10616832]{0:T(1024)(128)(4,1)} %bitcast.179), calls=%async_computation.27 | async-start | bytes 4456448
  284.3 0.7 copy-start.22
  284.4 101.7 %all-gather.10.cloned.1.call-start = ((), (), s32[]{:S(2)}) async-start(), calls=%async_computation.9 | async-start | bytes 4423680 | tf_op jit(solution)/shard_map/all_gather | solution.py:33
  338.6 146.9 %reduce-scatter.8.cloned.1.call-start = ((), (), s32[]{:S(2)}) async-start(), calls=%async_computation.10 | async-start | bytes 4423680 | tf_op jit(solution)/shard_map/reduce_scatter | solution.py:37
  438.2 104.4 %all-gather.12.cloned.1.call-start = ((), (), s32[]{:S(2)}) async-start(), calls=%async_computation.11 | async-start | bytes 4423680 | tf_op jit(solution)/shard_map/all_gather | solution.py:33
  487.9 5.9 copy-start.3
  492.5 1.2 copy-start.6
  495.2 140.3 %all-gather.14.cloned.1.call-start = ((), (), s32[]{:S(2)}) async-start(), calls=%async_computation.12 | async-start | bytes 7864320 | tf_op jit(solution)/shard_map/all_gather | solution.py:181
  542.5 4.2 copy-start.9
  542.5 9.5 slice-start
  546.7 5.3 slice-start.1
  546.7 5.3 copy-start.14
  556.7 1.7 copy-start.12
  565.1 850.7 %all-reduce.5.cloned.1.call-start = ((), (), s32[]{:S(2)}) async-start(), calls=%async_computation.13 | async-start | bytes 77856768 | tf_op jit(solution)/shard_map/psum | solution.py:41
  565.4 13.8 copy-start.26
  565.4 13.8 copy-start.33
  579.2 10.7 copy-start.32
  589.9 11.0 copy-start.27
  589.9 11.0 copy-start.30
  661.6 1.7 copy-start.11
  689.7 5.9 copy-start.16
  689.7 5.9 copy-start.19
  692.3 5.3 copy-start.17
  692.3 47.5 %copy-start.7 = (f32[192,2304]{1,0:T(8,128)S(1)}, f32[192,2304]{1,0:T(8,128)}, u32[]{:S(2)}) copy-start(f32[192,2304]{1,0:T(8,128)} %copy-done.6) | copy-start | bytes 5308420
  692.3 47.5 %copy-start.23 = (f32[192]{0:T(256)S(1)}, f32[192]{0:T(256)}, u32[]{:S(2)}) copy-start(f32[192]{0:T(256)} %get-tuple-element.38) | copy-start | bytes 2308
  1415.8 4.8 copy-start.5
  1415.8 11.7 slice-start.8
  1415.8 11.7 slice-start.9
  1420.6 4.2 copy-start.10
  1420.6 6.9 slice-start.10
  1424.8 13.3 slice-start.5
  1427.5 10.6 slice-start.6
  1427.5 10.6 slice-start.7
  1427.5 19.3 %slice-start.2 = ((s8[10616832]{0:T(1024)(128)(4,1)}), s8[4194304]{0:T(1024)(128)(4,1)S(1)}, s32[]{:S(2)}) async-start(s8[10616832]{0:T(1024)(128)(4,1)} %bitcast.161), calls=%async_computation.16 | async-start | bytes 8388608
  1427.5 19.2 %slice-start.3 = ((s8[10616832]{0:T(1024)(128)(4,1)}), s8[4194304]{0:T(1024)(128)(4,1)S(1)}, s32[]{:S(2)}) async-start(s8[10616832]{0:T(1024)(128)(4,1)} %bitcast.161), calls=%async_computation.17 | async-start | bytes 8388608
  1438.1 8.7 slice-start.4
  1446.8 7.6 copy-start.1
Sparse Core Ops, SparseCore 0:
  12.6 94.0 all-gather.5
  141.7 47.2 reduce-scatter.3
  194.9 47.2 all-gather.7
  284.5 47.2 reduce-scatter.5
  338.8 47.2 all-gather.9
  438.3 47.2 reduce-scatter.7
  495.3 47.2 all-gather.11
  565.2 70.1 all-gather.13
  661.8 753.9 all-reduce.4

commit v2 on v1

--- a/solution.py
+++ b/solution.py
@@ -1,7 +1,262 @@
+import functools
+
 import jax
 import jax.numpy as jnp
 from jax import lax
+from jax.experimental import pallas as pl
+from jax.experimental.pallas import tpu as pltpu
 from jax.sharding import PartitionSpec as P
+
+SLOTS = 8
+CHUNK = 64
+
+
+def remote(src, dst, send_sem, recv_sem, where):
+    return pltpu.make_async_remote_copy(
+        src_ref=src,
+        dst_ref=dst,
+        send_sem=send_sem,
+        recv_sem=recv_sem,
+        device_id=where,
+        device_id_type=pl.DeviceIdType.MESH,
+    )
+
+
+def add_low(left, right):
+    return (left.astype(jnp.float32) + right.astype(jnp.float32)).astype(jnp.bfloat16)
+
+
+def chain_kernel(counts, chunk, *refs):
+    jobs = len(counts)
+    ins, outs = refs[:jobs], refs[jobs : 2 * jobs]
+    (
+        mine, sib, acc, outer_in, inner_in, total,
+        load_sem, sib_send, sib_recv, up_send, outer_recv, inner_recv,
+        down_send, pair_send, pair_recv, store_sem,
+        sib_credit, up_credit, down_credit,
+    ) = refs[2 * jobs :]
+    slots = mine.shape[0]
+    steps = sum(counts)
+    place = lax.axis_index("rep")
+    chips = lax.axis_size("rep") // 2
+    chip, core = place // 2, place % 2
+    left = chip < chips // 2
+    is_end = (chip == 0) | (chip == chips - 1)
+    is_mid = (chip == chips // 2 - 1) | (chip == chips // 2)
+    twin = {"rep": place + 1 - 2 * core}
+    inner = {"rep": jnp.where(left, place + 2, place - 2)}
+    outer = {"rep": jnp.where(is_end, place, jnp.where(left, place - 2, place + 2))}
+
+    def tell(sem, where):
+        pl.semaphore_signal(sem, inc=1, device_id=where, device_id_type=pl.DeviceIdType.MESH)
+
+    barrier = pltpu.get_barrier_semaphore()
+    tell(barrier, twin)
+    tell(barrier, inner)
+
+    @pl.when(is_end)
+    def _():
+        pl.semaphore_wait(barrier, 2)
+
+    @pl.when(jnp.logical_not(is_end))
+    def _():
+        tell(barrier, outer)
+        pl.semaphore_wait(barrier, 3)
+
+    def with_rows(step, which, use):
+        low = 0
+        for job, count in enumerate(counts):
+            first = low
+
+            @pl.when((step >= low) & (step < low + count))
+            def _():
+                row = pl.multiple_of(((step - first) * 2 + which) * chunk, chunk)
+                use(job, pl.ds(row, chunk))
+
+            low += count
+
+    def pair_copy(job, rows, slot, step):
+        return remote(total.at[slot], outs[job].at[rows], pair_send.at[slot], pair_recv.at[step], twin)
+
+    def up_copy(slot, dst, sem):
+        return remote(acc.at[slot], dst.at[slot], up_send.at[slot], sem.at[slot], inner)
+
+    def down_copy(slot):
+        return remote(total.at[slot], inner_in.at[slot], down_send.at[slot], inner_recv.at[slot], outer)
+
+    def sib_copy(job, rows, slot):
+        return remote(ins[job].at[rows], sib.at[slot], sib_send.at[slot], sib_recv.at[slot], twin)
+
+    def load_copy(job, rows, slot):
+        return pltpu.make_async_copy(ins[job].at[rows], mine.at[slot], load_sem.at[slot])
+
+    def store_copy(job, rows, slot):
+        return pltpu.make_async_copy(total.at[slot], outs[job].at[rows], store_sem.at[slot])
+
+    some = pl.ds(0, chunk)
+
+    def take(step):
+        slot = step % slots
+
+        @pl.when(step >= slots)
+        def _():
+            pl.semaphore_wait(sib_credit, 1)
+
+        with_rows(step, 1 - core, lambda job, rows: sib_copy(job, rows, slot).start())
+        with_rows(step, core, lambda job, rows: load_copy(job, rows, slot).start())
+
+    def send_up(step):
+        slot = step % slots
+
+        @pl.when(step >= slots)
+        def _():
+            pl.semaphore_wait(up_credit, 1)
+
+        @pl.when(is_mid)
+        def _():
+            up_copy(slot, inner_in, inner_recv).start()
+
+        @pl.when(jnp.logical_not(is_mid))
+        def _():
+            up_copy(slot, outer_in, outer_recv).start()
+
+    def pair_up(step):
+        slot = step % slots
+        load_copy(0, some, slot).wait()
+        sib_copy(0, some, slot).wait()
+
+        @pl.when(step >= slots)
+        def _():
+            up_copy(slot, outer_in, outer_recv).wait_send()
+
+        acc[slot] = add_low(mine[slot], sib[slot])
+
+        @pl.when(step + slots < steps)
+        def _():
+            tell(sib_credit, twin)
+
+        @pl.when(is_end)
+        def _():
+            send_up(step)
+
+    def from_outer(step):
+        slot = step % slots
+        up_copy(slot, outer_in, outer_recv).wait_recv()
+        acc[slot] = add_low(acc[slot], outer_in[slot])
+
+        @pl.when(step + slots < steps)
+        def _():
+            tell(up_credit, outer)
+
+        send_up(step)
+
+    def sends_done(slot):
+        pair_copy(0, some, slot, 0).wait_send()
+        store_copy(0, some, slot).wait()
+
+        @pl.when(jnp.logical_not(is_end))
+        def _():
+            down_copy(slot).wait_send()
+
+    def from_inner(step):
+        slot = step % slots
+        down_copy(slot).wait_recv()
+
+        @pl.when(step >= slots)
+        def _():
+            sends_done(slot)
+
+        @pl.when(is_mid)
+        def _():
+            total[slot] = add_low(acc[slot], inner_in[slot])
+
+            @pl.when(step + slots < steps)
+            def _():
+                tell(up_credit, inner)
+
+        @pl.when(jnp.logical_not(is_mid))
+        def _():
+            total[slot] = inner_in[slot]
+
+            @pl.when(step + slots < steps)
+            def _():
+                tell(down_credit, inner)
+
+        @pl.when(jnp.logical_not(is_end))
+        def _():
+            @pl.when(step >= slots)
+            def _():
+                pl.semaphore_wait(down_credit, 1)
+
+            down_copy(slot).start()
+
+        with_rows(step, core, lambda job, rows: pair_copy(job, rows, slot, step).start())
+        with_rows(step, core, lambda job, rows: store_copy(job, rows, slot).start())
+
+    lag_outer = 3
+    lag_inner = jnp.where(is_end, 8, 6)
+
+    def tick(step, carry):
+        @pl.when(step < steps)
+        def _():
+            take(step)
+
+        @pl.when((step >= 1) & (step - 1 < steps))
+        def _():
+            pair_up(step - 1)
+
+        @pl.when(jnp.logical_not(is_end) & (step >= lag_outer) & (step - lag_outer < steps))
+        def _():
+            from_outer(step - lag_outer)
+
+        @pl.when((step >= lag_inner) & (step - lag_inner < steps))
+        def _():
+            from_inner(step - lag_inner)
+
+        return carry
+
+    lax.fori_loop(0, steps + 8, tick, 0)
+
+    def finish(step, carry):
+        slot = step % slots
+        sends_done(slot)
+        up_copy(slot, outer_in, outer_recv).wait_send()
+        return carry
+
+    lax.fori_loop(steps - slots, steps, finish, 0)
+
+    def arrived(step, carry):
+        pair_copy(0, some, 0, step).wait_recv()
+        return carry
+
+    lax.fori_loop(0, steps, arrived, 0)
+
+
+def chain_sum(parts, chunk=CHUNK, collective_id=1):
+    width = parts[0].shape[1]
+    counts = tuple(part.shape[0] // (2 * chunk) for part in parts)
+    steps = sum(counts)
+    slots = min(SLOTS, steps)
+    any_space = pl.BlockSpec(memory_space=pl.ANY)
+    block = pltpu.VMEM((slots, chunk, width), jnp.bfloat16)
+    sems = pltpu.SemaphoreType.DMA((slots,))
+    credit = pltpu.SemaphoreType.REGULAR
+    return pl.pallas_call(
+        functools.partial(chain_kernel, counts, chunk),
+        out_shape=[jax.ShapeDtypeStruct(part.shape, part.dtype) for part in parts],
+        in_specs=[any_space] * len(parts),
+        out_specs=[any_space] * len(parts),
+        scratch_shapes=[block] * 6
+        + [sems] * 8
+        + [pltpu.SemaphoreType.DMA((steps,)), sems, credit, credit, credit],
+        compiler_params=pltpu.CompilerParams(
+            collective_id=collective_id, has_side_effects=True, vmem_limit_bytes=48 * 1024 * 1024
+        ),
+        cost_estimate=pl.CostEstimate(
+            flops=0, bytes_accessed=8 * sum(part.size for part in parts), transcendentals=0
+        ),
+    )(*parts)
+
 
 QUERY_HEADS = 8
 KV = 4
@@ -37,8 +292,11 @@
     return lax.psum_scatter(partial, "shard", scatter_dimension=0, tiled=True)
 
 
-def rep_sum(grads):
-    return [lax.psum(grad, "rep").astype(jnp.float32) for grad in grads]
+def rep_sum(grads, width):
+    summed = chain_sum([grad.astype(jnp.bfloat16).reshape(-1, width) for grad in grads])
+    return [
+        total.reshape(grad.shape).astype(jnp.float32) for total, grad in zip(summed, grads)
+    ]
 
 
 def body(
@@ -203,28 +461,27 @@
     qkv_part = jnp.einsum("td,tj->dj", normed_cols, grad_qkv, preferred_element_type=f32)
     grad_resid_part, grad_gain_one = norm_back(residual, rms_one, gain_one, grad_normed)
     grad_tokens = (grad_middle + grad_resid_part).astype(bf16)
-    qkv_sum, out_sum, gate_sum, up_sum, down_sum = rep_sum(
-        [part.astype(bf16) for part in (qkv_part, out_part, gate_part, up_part, down_part)]
-    )
-    gain_sum_one, gain_sum_two, gain_sum_three, gain_sum_four = lax.psum(
-        (grad_gain_one, grad_gain_two, grad_gain_three, grad_gain_four), ("rep", "shard")
+    gain_parts = jnp.stack((grad_gain_one, grad_gain_two, grad_gain_three, grad_gain_four))
+    gain_sums = lax.all_gather(gain_parts, ("rep", "shard"), axis=0).sum(axis=0)
+    down_sum, gate_sum, up_sum, out_sum, qkv_sum = rep_sum(
+        (down_part, gate_part, up_part, out_part, qkv_part), width
     )
     q_width = w_query.shape[1]
     k_width = w_key.shape[1]
     return (
         output,
         grad_tokens,
-        gain_sum_one,
+        gain_sums[0],
         qkv_sum[:, :q_width],
         qkv_sum[:, q_width : q_width + k_width],
         qkv_sum[:, q_width + k_width :],
         out_sum,
-        gain_sum_two,
-        gain_sum_three,
+        gain_sums[1],
+        gain_sums[2],
         gate_sum,
         up_sum,
         down_sum,
-        gain_sum_four,
+        gain_sums[3],
     )
 
 

time: 1470 us -> 1240 us (0.84)
  waiting for transfers between devices: 986 us -> 328 us
  Pallas kernels: 0 us -> 457 us
  blocking collectives: 133 us -> 74.6 us
  local copies, waits for them, and re-layouts: 63.6 us -> 81.5 us
    psum x1 -> x0, waiting for transfers between devices: 673 us -> none  [rep_sum(): return [lax.psum(grad, 'rep').astype(jnp.float32) for grad in grads]]
    pallas_call x0 -> x1, Pallas kernels: none -> 457 us  [chain_sum(): pl.pallas_call(functools.partial(chain_kernel, counts, chunk), out_shape=...]
    psum x1 -> x0, blocking collectives: 42.1 us -> none  [body(): lax.psum((grad_gain_one, grad_gain_two, grad_gain_three, grad_gain_four),...]
    all_to_all x1 -> x0, blocking collectives: 16.5 us -> none  [body(): lax.all_to_all(grad_normed.astype(bf16).reshape(n, tok_rows, part_rows),...]
  transfers between devices with their start and end apart: 10 -> 11, of which waited for: 8 -> 7; matrix products, arithmetic and copies ran while one was open for 6% -> 12% of each run, Pallas kernels for 0% -> 37%
where the time goes in v2:
time: 1240 us
  Pallas kernels  457 us (37%)
  waiting for transfers between devices  328 us (26%)
  matrix products  189 us (15%)
  local copies, waits for them, and re-layouts  81.5 us (7%)
  other arithmetic  79.5 us (6%)
  blocking collectives  74.6 us (6%)
  between operations  15.6 us (1%)
    pallas_call x1, Pallas kernels, chain_sum(): pl.pallas_call(functools.partial(chain_kernel, counts, chunk), out_shape=...  457 us
    all_gather x4, waiting for transfers between devices, gather_rows(): return lax.all_gather(block, 'shard', axis=0, tiled=True)  142 us
    reduce_scatter x3, waiting for transfers between devices, scatter_rows(): return lax.psum_scatter(partial, 'shard', scatter_dimension=0, tiled=True)  140 us
    unnamed x1, blocking collectives  74.6 us
    all_gather x1, waiting for transfers between devices, body(): grad_parts = lax.all_gather(grad_parts, 'shard', axis=0)  45.7 us
    convert_element_type x4, other arithmetic, rep_sum(): total.reshape(grad.shape).astype(jnp.float32)  36 us
  transfers between devices with their start and end apart: 11, of which 7 were waited for; matrix products, arithmetic and copies ran while one was open for 12% of the time, Pallas kernels for 37%

profile of v2, /device:TPU:0, one launch (start us, length us, event | category | flops | bytes accessed | tf_op | source)
XLA Modules:
  0.0 1235.6 jit_solution(10219972165936584435)
XLA Ops:
  7.2 1.6 fusion.55
  10.1 2.4 fusion.57
  12.5 3.5 reshape.387
  16.0 3.5 reshape.388
  19.5 6.2 reshape.386
  25.7 5.1 maximum_bitcast_fusion
  30.8 3.8 copy.94
  34.6 5.3 all-to-all-start
  41.4 74.6 %all-reduce = bf16[768]{0:T(1024)(128)(2,1)S(1)} all-reduce(bf16[768]{0:T(1024)(128)(2,1)S(1)} %dynamic-update-slice), channel_id=1, replica_groups=mesh['rep'=8,'shard'=4] {'shard'}, use_global_device_ids=true, to_apply=%add | all-reduce | flops 768 | bytes 3072
  116.2 1.5 fusion.28
  117.8 7.4 convolution_convert_fusion.7
  127.3 2.3 copy.124
  129.6 2.6 fusion.19
  133.6 3.2 fusion.68
  137.7 3.8 convolution_convert_fusion.5
  142.3 46.8 %reduce-scatter.4.cloned.1.call-done = bf16[192,2304]{1,0:T(8,128)(2,1)} async-done(((bf16[768,2304]{1,0:T(8,128)(2,1)}), bf16[192,2304]{1,0:T(8,128)(2,1)}) %reduce-scatter.4.cloned.1.call-update) | async-done | bytes 884752 | tf_op jit(solution)/shard_map/reduce_scatter | solution.py:292
  190.5 1.7 multiply_reduce_fusion
  192.2 2.6 multiply_convert_fusion.2
  195.1 47.2 %all-gather.11.cloned.1.call-done = bf16[768,2304]{1,0:T(8,128)(2,1)} async-done(((bf16[192,2304]{1,0:T(8,128)(2,1)}), bf16[768,2304]{1,0:T(8,128)(2,1)}) %all-gather.11.cloned.1.call-update) | async-done | bytes 3538960 | tf_op jit(solution)/shard_map/all_gather | solution.py:288
  242.3 15.0 %fusion.92 = f32[768,2304]{1,0:T(8,128)} fusion(bf16[768,2304]{1,0:T(8,128)(2,1)} %all-gather.11.cloned.1.call-done, bf16[2304,2304]{1,0:T(8,128)(2,1)} %param.25), kind=kOutput, calls=%fused_computation.155 | convolution fusion | flops 8153726976 | bytes 21233664 | tf_op jit(solution)/shard_map/dot_general | solution.py:393
  257.3 15.8 %multiply_convert_fusion.1 = (bf16[768,2304]{1,0:T(8,128)(2,1)}, f32[768,2304]{1,0:T(8,128)}) fusion(f32[768,2304]{1,0:T(8,128)} %fusion.92, bf16[768,2304]{1,0:T(8,128)(2,1)S(1)} %copy-done.28, bf16[2304,2304]{1,0:T(8,128)(2,1)} %param.26), kind=kOutput, calls=%fused_computation.14 | convolution fusion | flops 8171421696 | bytes 31850496 | tf_op jit(solution)/shard_map/dot_general | solution.py:394
  273.1 11.3 convolution_convert_fusion.4
  285.1 46.7 %reduce-scatter.6.cloned.1.call-done = bf16[192,2304]{1,0:T(8,128)(2,1)} async-done(((bf16[768,2304]{1,0:T(8,128)(2,1)}), bf16[192,2304]{1,0:T(8,128)(2,1)}) %reduce-scatter.6.cloned.1.call-update) | async-done | bytes 884752 | tf_op jit(solution)/shard_map/reduce_scatter | solution.py:292
  333.2 2.0 fusion.54
  335.2 2.8 fusion.34
  338.3 47.1 %all-gather.13.cloned.1.call-done = bf16[768,2304]{1,0:T(8,128)(2,1)} async-done(((bf16[192,2304]{1,0:T(8,128)(2,1)}), bf16[768,2304]{1,0:T(8,128)(2,1)}) %all-gather.13.cloned.1.call-update) | async-done | bytes 3538960 | tf_op jit(solution)/shard_map/all_gather | solution.py:288
  385.5 21.9 %multiply_convert_fusion = (bf16[768,2304]{1,0:T(8,128)(2,1)}, bf16[768,2304]{1,0:T(8,128)(2,1)}) fusion(f32[768,2304]{1,0:T(8,128)} %fusion.92, f32[768,2304]{1,0:T(8,128)} %get-tuple-element.54, bf16[768,2304]{1,0:T(8,128)(2,1)} %all-gather.13.cloned.1.call-done, bf16[2304,2304]{1,0:T(8,128)(2,1)} %param.27), kind=kOutput, calls=%fused_computation.13 | convolution fusion | flops 8196194304 | bytes 35389440 | tf_op jit(solution)/shard_map/td,fd->tf/dot_general | solution.py:407
  407.3 14.9 %fusion.93 = f32[768,2304]{1,0:T(8,128)} fusion(bf16[768,2304]{1,0:T(8,128)(2,1)} %get-tuple-element.37, bf16[2304,2304]{1,0:T(8,128)(2,1)} %param.25), kind=kOutput, calls=%fused_computation.156 | convolution fusion | flops 8153726976 | bytes 21233664 | tf_op jit(solution)/shard_map/tf,df->td/dot_general | solution.py:411
  422.2 15.5 %add_convert_fusion = bf16[768,2304]{1,0:T(8,128)(2,1)} fusion(f32[768,2304]{1,0:T(8,128)} %fusion.93, bf16[768,2304]{1,0:T(8,128)(2,1)} %get-tuple-element.36, bf16[2304,2304]{1,0:T(8,128)(2,1)} %param.26), kind=kOutput, calls=%fused_computation.12 | convolution fusion | flops 8157265920 | bytes 24772608 | tf_op jit(solution)/shard_map/tf,df->td/dot_general | solution.py:412
  438.2 46.9 %reduce-scatter.8.cloned.1.call-done = bf16[192,2304]{1,0:T(8,128)(2,1)} async-done(((bf16[768,2304]{1,0:T(8,128)(2,1)}), bf16[192,2304]{1,0:T(8,128)(2,1)}) %reduce-scatter.8.cloned.1.call-update) | async-done | bytes 884752 | tf_op jit(solution)/shard_map/reduce_scatter | solution.py:292
  485.1 2.3 fusion.38
  487.4 4.7 fusion.46
  494.8 47.4 %all-gather.15.cloned.1.call-done = bf16[768,2304]{1,0:T(8,128)(2,1)} async-done(((bf16[192,2304]{1,0:T(8,128)(2,1)}), bf16[768,2304]{1,0:T(8,128)(2,1)}) %all-gather.15.cloned.1.call-update) | async-done | bytes 3538960 | tf_op jit(solution)/shard_map/all_gather | solution.py:288
  542.1 4.2 convolution_convert_fusion.9
  546.4 5.3 fusion.78
  551.7 2.2 fusion.15
  553.8 2.6 fusion.20
  556.5 1.7 convolution_convert_fusion.8
  558.2 1.6 fusion.81
  564.9 13.8 %convolution_convert_fusion.2.refs_0_ = bf16[2304,2304]{1,0:T(8,128)(2,1)} fusion(bf16[768,2304]{1,0:T(8,128)(2,1)} %get-tuple-element.53, bf16[768,2304]{1,0:T(8,128)(2,1)} %all-gather.13.cloned.1.call-done), kind=kOutput, calls=%fused_computation.2 | convolution fusion | flops 8159035392 | bytes 17694720 | tf_op jit(solution)/shard_map/tf,td->fd/dot_general | solution.py:406
  578.7 10.7 convolution_convert_fusion.refs_2_
  589.5 45.7 %all-gather.17.cloned.1.call-done = bf16[4,768,1024]{2,1,0:T(8,128)(2,1)} async-done(((bf16[1,768,1024]{2,1,0:T(8,128)(2,1)}), bf16[4,768,1024]{2,1,0:T(8,128)(2,1)}) %all-gather.17.cloned.1.call-update) | async-done | bytes 6291472 | tf_op jit(solution)/shard_map/all_gather | solution.py:439
  635.2 3.2 fusion.91
  638.5 2.6 copy.122
  641.1 3.8 slice.55
  644.8 4.6 copy.121
  649.4 1.7 copy.123
  651.2 8.0 fusion.65
  660.6 4.2 all-to-all-start.1
  664.9 13.6 %convolution_convert_fusion.1.refs_1_ = bf16[2304,2304]{1,0:T(8,128)(2,1)} fusion(bf16[768,2304]{1,0:T(8,128)(2,1)} %all-gather.11.cloned.1.call-done, bf16[768,2304]{1,0:T(8,128)(2,1)} %get-tuple-element.37), kind=kOutput, calls=%fused_computation.1 | convolution fusion | flops 8159035392 | bytes 17694720 | tf_op jit(solution)/shard_map/td,tf->df/dot_general | solution.py:414
  679.9 2.5 copy.111
  682.4 2.4 reshape.401
  686.2 4.4 convolution_convert_fusion.6.refs_3_
  690.6 12.2 convolution_convert_fusion.3
  702.8 9.4 reshape.398.refs_4_
  712.2 456.8 %shard_map.246 = (bf16[2304,2304]{1,0:T(8,128)(2,1)}, bf16[2304,2304]{1,0:T(8,128)(2,1)}, bf16[2304,2304]{1,0:T(8,128)(2,1)}, bf16[512,2304]{1,0:T(8,128)(2,1)S(1)}, bf16[1024,2304]{1,0:T(8,128)(2,1)}) custom-call(bf16[2304,2304]{1,0:T(8,128)(2,1)} %convolution_convert_fusion.2.refs_0_, bf16[2304,2304]{1,0:T(8,128)(2,1)} %convolution_convert_fusion.1.refs_1_, ...), custom_call_target="tpu_custom_call" | custom-call | bytes 155713536 | tf_op jit(solution)/shard_map/pallas_call | solution.py:244
  1170.4 10.0 reshape.402
  1180.4 5.2 slice.59
  1185.7 2.7 convert_element_type.188
  1188.4 15.6 %convert_element_type.189 = f32[2304,2304]{1,0:T(8,128)} convert(bf16[2304,2304]{1,0:T(8,128)(2,1)} %get-tuple-element.20) | non-fusion elementwise | flops 5308416 | bytes 31850496 | tf_op jit(solution)/shard_map/convert_element_type | solution.py:298
  1204.1 10.2 convert_element_type.190
  1214.2 7.6 convert_element_type.191
  1221.9 3.1 fusion.90
  1226.5 1.5 reduce_sum.169
  (162 shorter events, 27.6 us)
Async XLA Ops:
  7.2 130.6 %copy-start = (bf16[512,2304]{1,0:T(8,128)(2,1)S(1)}, bf16[512,2304]{1,0:T(8,128)(2,1)}, u32[]{:S(2)}) copy-start(bf16[512,2304]{1,0:T(8,128)(2,1)} %param.22) | copy-start | bytes 7077892
  7.2 110.6 %all-gather.9.cloned.1.call-start = ((), (), s32[]{:S(2)}) async-start(), calls=%async_computation.5 | async-start | bytes 4423680 | tf_op jit(solution)/shard_map/all_gather | solution.py:288
  9.4 10.1 copy-start.21
  10.1 9.4 copy-start.19
  34.6 5.3 copy-start.30
  34.6 5.3 copy-start.32
  34.6 81.4 %copy-start.27 = (s32[1,13]{1,0:T(1,128)S(1)}, s32[1,13]{1,0:T(1,128)}, u32[]{:S(2)}) copy-start(s32[1,13]{1,0:T(1,128)} %param.17) | copy-start | bytes 160
  34.6 83.1 %all-to-all-start = ((bf16[4,576,1024]{2,1,0:T(8,128)(2,1)}), bf16[4,576,1024]{2,1,0:T(8,128)(2,1)}, u32[]{:S(2)}, u32[]{:S(2)}) async-start(bf16[4,576,1024]{2,1,0:T(8,128)(2,1)} %copy.94), calls=%async_computation | async-start | bytes 9437184 | tf_op jit(solution)/shard_map/all_to_all | solution.py:346
  39.9 149.2 %reduce-scatter.4.cloned.1.call-start = ((), (), s32[]{:S(2)}) async-start(), calls=%async_computation.6 | async-start | bytes 4423680 | tf_op jit(solution)/shard_map/reduce_scatter | solution.py:292
  117.7 15.8 %copy-start.11 = (pred[768,768]{0,1:T(8,128)(4,1)}, pred[768,768]{0,1:T(8,128)(4,1)S(1)}, u32[]{:S(2)}) copy-start(pred[768,768]{0,1:T(8,128)(4,1)S(1)} %fusion.28) | copy-start | bytes 1769476
  125.2 1.1 copy-start.17
  132.1 4.7 copy-start.6
  136.8 0.9 copy-start.31
  141.6 0.7 copy-start.23
  141.6 0.7 copy-start.24
  141.6 48.9 %copy-start.4 = (bf16[192,2304]{1,0:T(8,128)(2,1)S(1)}, bf16[192,2304]{1,0:T(8,128)(2,1)}, u32[]{:S(2)}) copy-start(bf16[192,2304]{1,0:T(8,128)(2,1)} %param.15) | copy-start | bytes 2654212
  141.6 100.7 %all-gather.11.cloned.1.call-start = ((), (), s32[]{:S(2)}) async-start(), calls=%async_computation.7 | async-start | bytes 4423680 | tf_op jit(solution)/shard_map/all_gather | solution.py:288
  194.9 136.9 %reduce-scatter.6.cloned.1.call-start = ((), (), s32[]{:S(2)}) async-start(), calls=%async_computation.8 | async-start | bytes 4423680 | tf_op jit(solution)/shard_map/reduce_scatter | solution.py:292
  242.3 15.0 %copy-start.28 = (bf16[768,2304]{1,0:T(8,128)(2,1)S(1)}, bf16[768,2304]{1,0:T(8,128)(2,1)}, u32[]{:S(2)}) copy-start(bf16[768,2304]{1,0:T(8,128)(2,1)} %all-gather.11.cloned.1.call-done) | copy-start | bytes 10616836
  242.3 30.8 %slice-start.11 = ((s8[10616832]{0:T(1024)(128)(4,1)}), s8[4194304]{0:T(1024)(128)(4,1)S(1)}, s32[]{:S(2)}) async-start(s8[10616832]{0:T(1024)(128)(4,1)} %bitcast.180), calls=%async_computation.25 | async-start | bytes 8388608
  242.3 30.8 %slice-start.12 = ((s8[10616832]{0:T(1024)(128)(4,1)}), s8[4194304]{0:T(1024)(128)(4,1)S(1)}, s32[]{:S(2)}) async-start(s8[10616832]{0:T(1024)(128)(4,1)} %bitcast.180), calls=%async_computation.26 | async-start | bytes 8388608
  257.3 15.8 %slice-start.13 = ((s8[10616832]{0:T(1024)(128)(4,1)}), s8[2228224]{0:T(1024)(128)(4,1)S(1)}, s32[]{:S(2)}) async-start(s8[10616832]{0:T(1024)(128)(4,1)} %bitcast.180), calls=%async_computation.27 | async-start | bytes 4456448
  284.4 0.7 copy-start.25
  284.4 101.1 %all-gather.13.cloned.1.call-start = ((), (), s32[]{:S(2)}) async-start(), calls=%async_computation.9 | async-start | bytes 4423680 | tf_op jit(solution)/shard_map/all_gather | solution.py:288
  338.1 147.0 %reduce-scatter.8.cloned.1.call-start = ((), (), s32[]{:S(2)}) async-start(), calls=%async_computation.10 | async-start | bytes 4423680 | tf_op jit(solution)/shard_map/reduce_scatter | solution.py:292
  437.7 104.4 %all-gather.15.cloned.1.call-start = ((), (), s32[]{:S(2)}) async-start(), calls=%async_computation.11 | async-start | bytes 4423680 | tf_op jit(solution)/shard_map/all_gather | solution.py:288
  487.4 5.9 copy-start.5
  492.1 1.2 copy-start.7
  494.7 140.5 %all-gather.17.cloned.1.call-start = ((), (), s32[]{:S(2)}) async-start(), calls=%async_computation.12 | async-start | bytes 7864320 | tf_op jit(solution)/shard_map/all_gather | solution.py:439
  542.1 4.2 copy-start.12
  542.1 9.5 slice-start.3
  546.3 5.3 slice-start.4
  546.3 5.3 copy-start.18
  556.5 1.7 copy-start.16
  564.9 13.8 %copy-start.29 = (bf16[768,2304]{1,0:T(8,128)(2,1)S(1)}, bf16[768,2304]{1,0:T(8,128)(2,1)}, u32[]{:S(2)}) copy-start(bf16[768,2304]{1,0:T(8,128)(2,1)} %all-gather.11.cloned.1.call-done) | copy-start | bytes 10616836
  564.9 13.8 %copy-start.33 = (bf16[768,2304]{1,0:T(8,128)(2,1)S(1)}, bf16[768,2304]{1,0:T(8,128)(2,1)}, u32[]{:S(2)}) copy-start(bf16[768,2304]{1,0:T(8,128)(2,1)} %get-tuple-element.36) | copy-start | bytes 10616836
  660.6 18.0 %all-to-all-start.1 = ((bf16[4,192,576]{2,1,0:T(8,128)(2,1)}), bf16[4,192,576]{2,1,0:T(8,128)(2,1)}, u32[]{:S(2)}, u32[]{:S(2)}) async-start(bf16[4,192,576]{2,1,0:T(8,128)(2,1)} %bitcast.38), calls=%async_computation.4 | async-start | bytes 1966080 | tf_op jit(solution)/shard_map/all_to_all | solution.py:456
  664.8 561.6 %all-gather.19.cloned.1.call-start = ((), (), s32[]{:S(2)}) async-start(), calls=%async_computation.13 | async-start | bytes 1216512 | tf_op jit(solution)/shard_map/all_gather | solution.py:465
  679.9 4.9 copy-start.20
  679.9 4.9 copy-start.22
  684.8 1.3 copy-start.9
  686.2 4.4 copy-start.13
  686.2 4.4 copy-start.14
  686.2 4.4 copy-start.15
  1169.0 1.4 copy-start.2
  1180.4 5.2 copy-start.3
  1185.7 18.4 %slice-start.8 = ((s8[10616832]{0:T(1024)(128)(4,1)}), s8[4194304]{0:T(1024)(128)(4,1)S(1)}, s32[]{:S(2)}) async-start(s8[10616832]{0:T(1024)(128)(4,1)} %bitcast.167), calls=%async_computation.22 | async-start | bytes 8388608
  1188.4 15.6 %slice-start.9 = ((s8[10616832]{0:T(1024)(128)(4,1)}), s8[4194304]{0:T(1024)(128)(4,1)S(1)}, s32[]{:S(2)}) async-start(s8[10616832]{0:T(1024)(128)(4,1)} %bitcast.167), calls=%async_computation.23 | async-start | bytes 8388608
  1188.4 15.6 %slice-start.10 = ((s8[10616832]{0:T(1024)(128)(4,1)}), s8[2228224]{0:T(1024)(128)(4,1)S(1)}, s32[]{:S(2)}) async-start(s8[10616832]{0:T(1024)(128)(4,1)} %bitcast.167), calls=%async_computation.24 | async-start | bytes 4456448
  1188.4 25.8 %slice-start.5 = ((s8[10616832]{0:T(1024)(128)(4,1)}), s8[4194304]{0:T(1024)(128)(4,1)S(1)}, s32[]{:S(2)}) async-start(s8[10616832]{0:T(1024)(128)(4,1)} %bitcast.165), calls=%async_computation.19 | async-start | bytes 8388608
  1188.4 25.8 %slice-start.6 = ((s8[10616832]{0:T(1024)(128)(4,1)}), s8[4194304]{0:T(1024)(128)(4,1)S(1)}, s32[]{:S(2)}) async-start(s8[10616832]{0:T(1024)(128)(4,1)} %bitcast.165), calls=%async_computation.20 | async-start | bytes 8388608
  1204.0 10.2 slice-start.7
  1204.0 17.8 %slice-start = ((s8[9437184]{0:T(1024)(128)(4,1)}), s8[4194304]{0:T(1024)(128)(4,1)S(1)}, s32[]{:S(2)}) async-start(s8[9437184]{0:T(1024)(128)(4,1)} %bitcast.161), calls=%async_computation.14 | async-start | bytes 8388608
  1204.1 17.8 %slice-start.1 = ((s8[9437184]{0:T(1024)(128)(4,1)}), s8[4194304]{0:T(1024)(128)(4,1)S(1)}, s32[]{:S(2)}) async-start(s8[9437184]{0:T(1024)(128)(4,1)} %bitcast.161), calls=%async_computation.15 | async-start | bytes 8388608
  1214.2 7.6 slice-start.2
  1221.8 3.2 copy-start.8
  1221.8 3.2 copy-start.10
  1221.8 3.2 copy-start.26
  1221.9 6.8 copy-start.1
Sparse Core Ops, SparseCore 0:
  12.6 94.0 all-gather.8
  141.7 47.2 reduce-scatter.3
  195.0 47.2 all-gather.10
  284.5 47.2 reduce-scatter.5
  338.2 47.2 all-gather.12
  437.8 47.2 reduce-scatter.7
  494.9 47.2 all-gather.14
  565.0 70.1 all-gather.16
  686.3 56.2 all-gather.18

commit v3 on v2

--- a/solution.py
+++ b/solution.py
@@ -258,6 +258,337 @@
     )(*parts)
 
 
+def plane_places():
+    me = lax.axis_index("shard")
+    x_other = me + 1 - 2 * (me % 2)
+    y_other = (me + 2) % 4
+    far = x_other + y_other - me
+    return me, x_other, y_other, far
+
+
+def greet(places):
+    barrier = pltpu.get_barrier_semaphore()
+    for place in places:
+        pl.semaphore_signal(
+            barrier, inc=1, device_id={"shard": place}, device_id_type=pl.DeviceIdType.MESH
+        )
+    pl.semaphore_wait(barrier, len(places))
+
+
+def gather_kernel(x_ref, out_ref, send_sem, recv_sem, local_sem):
+    me, x_other, y_other, far = plane_places()
+    rows = x_ref.shape[0]
+    half = rows // 2
+
+    def part(block, which):
+        return out_ref.at[pl.ds(pl.multiple_of(block * rows + which * half, 16), half)]
+
+    def own(which):
+        return x_ref.at[pl.ds(which * half, half)]
+
+    def send(src, dst, index, where):
+        return remote(src, dst, send_sem.at[index], recv_sem.at[index], {"shard": where})
+
+    greet((x_other, y_other))
+    local = pltpu.make_async_copy(
+        x_ref, out_ref.at[pl.ds(pl.multiple_of(me * rows, 16), rows)], local_sem
+    )
+    first = (
+        send(own(0), part(me, 0), 0, x_other),
+        send(own(1), part(me, 1), 1, y_other),
+        send(own(1), part(me, 1), 2, x_other),
+        send(own(0), part(me, 0), 3, y_other),
+    )
+    for copy in first:
+        copy.start()
+    local.start()
+    first[0].wait_recv()
+    on_y = send(part(x_other, 0), part(x_other, 0), 4, y_other)
+    on_y.start()
+    first[1].wait_recv()
+    on_x = send(part(y_other, 1), part(y_other, 1), 5, x_other)
+    on_x.start()
+    first[2].wait_recv()
+    first[3].wait_recv()
+    on_y.wait_recv()
+    on_x.wait_recv()
+    for copy in first + (on_y, on_x):
+        copy.wait_send()
+    local.wait()
+
+
+def gather4(block, collective_id):
+    rows, width = block.shape
+    sems = pltpu.SemaphoreType.DMA((6,))
+    any_space = pl.BlockSpec(memory_space=pl.ANY)
+    return pl.pallas_call(
+        gather_kernel,
+        out_shape=jax.ShapeDtypeStruct((4 * rows, width), block.dtype),
+        in_specs=[any_space],
+        out_specs=any_space,
+        scratch_shapes=[sems, sems, pltpu.SemaphoreType.DMA],
+        compiler_params=pltpu.CompilerParams(collective_id=collective_id, has_side_effects=True),
+        cost_estimate=pl.CostEstimate(
+            flops=0, bytes_accessed=40 * rows * width * 2, transcendentals=0
+        ),
+    )(block)
+
+
+def scatter_kernel(part_ref, out_ref, *scratch):
+    landed, mine, passed = scratch[:3]
+    send_sem, recv_sem, load_sem = scratch[3:]
+    me, x_other, y_other, far = plane_places()
+    rows = out_ref.shape[0]
+    half = rows // 2
+
+    def part(block, which):
+        return part_ref.at[pl.ds(pl.multiple_of(block * rows + which * half, 16), half)]
+
+    def send(src, index, where):
+        return remote(
+            src, landed.at[index], send_sem.at[index], recv_sem.at[index], {"shard": where}
+        )
+
+    def load(src, index):
+        return pltpu.make_async_copy(src, mine.at[index], load_sem.at[index])
+
+    loads = (
+        load(part(y_other, 0), 0),
+        load(part(x_other, 1), 1),
+        load(part(me, 0), 2),
+        load(part(me, 1), 3),
+    )
+    for copy in loads:
+        copy.start()
+    greet((x_other, y_other))
+    first = (
+        send(part(far, 0), 0, x_other),
+        send(part(far, 1), 1, y_other),
+        send(part(x_other, 0), 2, x_other),
+        send(part(y_other, 1), 3, y_other),
+    )
+    for copy in first:
+        copy.start()
+    for copy in loads:
+        copy.wait()
+    first[0].wait_recv()
+    passed[0] = add_low(landed[0], mine[0])
+    on_y = send(passed.at[0], 4, y_other)
+    on_y.start()
+    first[1].wait_recv()
+    passed[1] = add_low(landed[1], mine[1])
+    on_x = send(passed.at[1], 5, x_other)
+    on_x.start()
+    first[2].wait_recv()
+    mine[2] = add_low(landed[2], mine[2])
+    first[3].wait_recv()
+    mine[3] = add_low(landed[3], mine[3])
+    on_y.wait_recv()
+    out_ref[pl.ds(0, half)] = mine[2].astype(jnp.float32) + landed[4].astype(jnp.float32)
+    on_x.wait_recv()
+    out_ref[pl.ds(half, half)] = mine[3].astype(jnp.float32) + landed[5].astype(jnp.float32)
+    for copy in first + (on_y, on_x):
+        copy.wait_send()
+
+
+def scatter4(partial, collective_id):
+    rows, width = partial.shape[0] // 4, partial.shape[1]
+    half = rows // 2
+    return pl.pallas_call(
+        scatter_kernel,
+        out_shape=jax.ShapeDtypeStruct((rows, width), jnp.float32),
+        in_specs=[pl.BlockSpec(memory_space=pl.ANY)],
+        out_specs=pl.BlockSpec(memory_space=pltpu.VMEM),
+        scratch_shapes=[
+            pltpu.VMEM((6, half, width), partial.dtype),
+            pltpu.VMEM((4, half, width), partial.dtype),
+            pltpu.VMEM((2, half, width), partial.dtype),
+            pltpu.SemaphoreType.DMA((6,)),
+            pltpu.SemaphoreType.DMA((6,)),
+            pltpu.SemaphoreType.DMA((4,)),
+        ],
+        compiler_params=pltpu.CompilerParams(
+            collective_id=collective_id, has_side_effects=True, vmem_limit_bytes=32 * 1024 * 1024
+        ),
+        cost_estimate=pl.CostEstimate(
+            flops=0, bytes_accessed=40 * rows * width * 2, transcendentals=0
+        ),
+    )(partial)
+
+
+def exchange_kernel(x_ref, out_ref, send_sem, recv_sem, local_sem):
+    me = lax.axis_index("shard")
+    others = [(me + step) % 4 for step in (1, 2, 3)]
+    greet(others)
+    local = pltpu.make_async_copy(x_ref.at[me], out_ref.at[me], local_sem)
+    local.start()
+    copies = [
+        remote(x_ref.at[place], out_ref.at[me], send_sem.at[i], recv_sem.at[i], {"shard": place})
+        for i, place in enumerate(others)
+    ]
+    for copy in copies:
+        copy.start()
+    for copy in copies:
+        copy.wait()
+    local.wait()
+
+
+def exchange4(blocks, collective_id):
+    any_space = pl.BlockSpec(memory_space=pl.ANY)
+    sems = pltpu.SemaphoreType.DMA((3,))
+    return pl.pallas_call(
+        exchange_kernel,
+        out_shape=jax.ShapeDtypeStruct(blocks.shape, blocks.dtype),
+        in_specs=[any_space],
+        out_specs=any_space,
+        scratch_shapes=[sems, sems, pltpu.SemaphoreType.DMA],
+        compiler_params=pltpu.CompilerParams(collective_id=collective_id, has_side_effects=True),
+        cost_estimate=pl.CostEstimate(
+            flops=0, bytes_accessed=10 * blocks.size * 2, transcendentals=0
+        ),
+    )(blocks)
+
+
+def prologue_kernel(counts, x_ref, code_ref, query_ref, key_ref, value_ref, out_ref, codes_ref,
+                    heads_ref, send_sem, recv_sem, local_sem, code_send, code_recv,
+                    head_send, head_recv, twin_send, twin_recv, head_local):
+    me, x_other, y_other, far = plane_places()
+    place = lax.axis_index("rep")
+    core = place % 2
+    twin = {"rep": place + 1 - 2 * core}
+    others = (x_other, y_other, far)
+    rows = x_ref.shape[0]
+    half = rows // 2
+    depth = query_ref.shape[0]
+    part_depth = depth // 2
+    weights = (query_ref, key_ref, value_ref)
+    starts = (0, counts[0], counts[0] + counts[1])
+
+    barrier = pltpu.get_barrier_semaphore()
+    for other in others:
+        pl.semaphore_signal(
+            barrier, inc=1, device_id={"shard": other}, device_id_type=pl.DeviceIdType.MESH
+        )
+    pl.semaphore_signal(barrier, inc=1, device_id=twin, device_id_type=pl.DeviceIdType.MESH)
+    pl.semaphore_wait(barrier, 4)
+
+    def my_rows(owner):
+        return pl.ds(pl.multiple_of(owner * depth + core * part_depth, 16), part_depth)
+
+    def head_copy(index, kind, other):
+        columns = pl.ds(pl.multiple_of(other * counts[kind], 128), counts[kind])
+        return remote(
+            weights[kind].at[pl.ds(pl.multiple_of(core * part_depth, 16), part_depth), columns],
+            heads_ref.at[my_rows(me), pl.ds(starts[kind], counts[kind])],
+            head_send.at[index, kind],
+            head_recv.at[index, kind],
+            {"shard": other},
+        )
+
+    def part(block, which):
+        return out_ref.at[pl.ds(pl.multiple_of(block * rows + which * half, 16), half)]
+
+    def own(which):
+        return x_ref.at[pl.ds(which * half, half)]
+
+    def send(src, dst, index, where):
+        return remote(src, dst, send_sem.at[index], recv_sem.at[index], {"shard": where})
+
+    head_copies = [
+        [head_copy(index, kind, other) for kind in range(3)] for index, other in enumerate(others)
+    ]
+    for index in (2, 0, 1):
+        for copy in head_copies[index]:
+            copy.start()
+    code_copies = [
+        remote(
+            code_ref, codes_ref.at[me], code_send.at[index], code_recv.at[index], {"shard": other}
+        )
+        for index, other in enumerate(others)
+    ]
+    for copy in code_copies:
+        copy.start()
+    first = (
+        send(own(0), part(me, 0), 0, x_other),
+        send(own(1), part(me, 1), 1, y_other),
+        send(own(1), part(me, 1), 2, x_other),
+        send(own(0), part(me, 0), 3, y_other),
+    )
+    for copy in first:
+        copy.start()
+    locals_ = [
+        pltpu.make_async_copy(
+            x_ref, out_ref.at[pl.ds(pl.multiple_of(me * rows, 16), rows)], local_sem.at[0]
+        ),
+        pltpu.make_async_copy(code_ref, codes_ref.at[me], local_sem.at[1]),
+    ]
+    for kind in range(3):
+        columns = pl.ds(pl.multiple_of(me * counts[kind], 128), counts[kind])
+        locals_.append(
+            pltpu.make_async_copy(
+                weights[kind].at[:, columns],
+                heads_ref.at[
+                    pl.ds(pl.multiple_of(me * depth, 16), depth), pl.ds(starts[kind], counts[kind])
+                ],
+                head_local.at[kind],
+            )
+        )
+    for copy in locals_:
+        copy.start()
+    twins = []
+    for index in (0, 1, 2):
+        for copy in head_copies[index]:
+            copy.wait_recv()
+        block = heads_ref.at[my_rows(others[index])]
+        twins.append(remote(block, block, twin_send.at[index], twin_recv.at[index], twin))
+        twins[-1].start()
+    first[0].wait_recv()
+    on_y = send(part(x_other, 0), part(x_other, 0), 4, y_other)
+    on_y.start()
+    first[1].wait_recv()
+    on_x = send(part(y_other, 1), part(y_other, 1), 5, x_other)
+    on_x.start()
+    first[2].wait_recv()
+    first[3].wait_recv()
+    for copy in code_copies + twins:
+        copy.wait_recv()
+    on_y.wait_recv()
+    on_x.wait_recv()
+    for copy in list(first) + [on_y, on_x] + code_copies + twins:
+        copy.wait_send()
+    for group in head_copies:
+        for copy in group:
+            copy.wait_send()
+    for copy in locals_:
+        copy.wait()
+
+
+def prologue4(block, codes, w_query, w_key, w_value, collective_id):
+    rows, width = block.shape
+    counts = tuple(weight.shape[1] // 4 for weight in (w_query, w_key, w_value))
+    depth = w_query.shape[0]
+    any_space = pl.BlockSpec(memory_space=pl.ANY)
+    dma = pltpu.SemaphoreType.DMA
+    return pl.pallas_call(
+        functools.partial(prologue_kernel, counts),
+        out_shape=(
+            jax.ShapeDtypeStruct((4 * rows, width), block.dtype),
+            jax.ShapeDtypeStruct((4,) + codes.shape, codes.dtype),
+            jax.ShapeDtypeStruct((4 * depth, sum(counts)), w_query.dtype),
+        ),
+        in_specs=[any_space] * 5,
+        out_specs=[any_space] * 3,
+        scratch_shapes=[
+            dma((6,)), dma((6,)), dma((2,)), dma((3,)), dma((3,)),
+            dma((3, 3)), dma((3, 3)), dma((3,)), dma((3,)), dma((3,)),
+        ],
+        compiler_params=pltpu.CompilerParams(collective_id=collective_id, has_side_effects=True),
+        cost_estimate=pl.CostEstimate(
+            flops=0, bytes_accessed=80 * rows * width * 2, transcendentals=0
+        ),
+    )(block, codes, w_query, w_key, w_value)
+
+
 QUERY_HEADS = 8
 KV = 4
 HEAD_SIZE = 256
@@ -284,12 +615,50 @@
     return jax.nn.gelu(gate_pre, approximate=True) * up_pre
 
 
-def gather_rows(block):
+def gather_rows(block, collective_id):
+    if lax.axis_size("shard") == 4:
+        return gather4(block, collective_id)
     return lax.all_gather(block, "shard", axis=0, tiled=True)
 
 
-def scatter_rows(partial):
-    return lax.psum_scatter(partial, "shard", scatter_dimension=0, tiled=True)
+def scatter_rows(partial, collective_id):
+    if lax.axis_size("shard") == 4:
+        return scatter4(partial, collective_id)
+    summed = lax.psum_scatter(partial, "shard", scatter_dimension=0, tiled=True)
+    return summed.astype(jnp.float32)
+
+
+def exchange(blocks, collective_id):
+    if lax.axis_size("shard") == 4:
+        return exchange4(blocks, collective_id)
+    return lax.all_to_all(blocks, "shard", 0, 0, tiled=True)
+
+
+def first_gather(normed, seg_ids, w_query, w_key, w_value):
+    n = lax.axis_size("shard")
+    tok_rows, width = normed.shape
+    codes = seg_ids.astype(jnp.bfloat16)
+    if n == 4:
+        codes = jnp.pad(codes, (0, 2048 - tok_rows)).reshape(16, 128)
+        normed_all, codes, heads = prologue4(normed, codes, w_query, w_key, w_value, 2)
+        codes = codes.reshape(n, -1)[:, :tok_rows].reshape(-1)
+        return normed_all, codes.astype(jnp.int32), heads
+    part_rows = w_query.shape[0]
+    share = max(1, n // KV)
+
+    def by_device(weight):
+        heads = weight.reshape(part_rows, KV, -1)
+        if share > 1:
+            heads = jnp.repeat(heads, share, axis=1)
+        return heads.reshape(part_rows, n, -1)
+
+    parts = jnp.concatenate(
+        (w_query.reshape(part_rows, n, -1), by_device(w_key), by_device(w_value)), axis=2
+    ).transpose(1, 0, 2)
+    heads = lax.all_to_all(parts, "shard", 0, 0, tiled=True).reshape(width, -1)
+    normed_all = lax.all_gather(normed, "shard", axis=0, tiled=True)
+    codes = lax.all_gather(codes, "shard", axis=0, tiled=True)
+    return normed_all, codes.astype(jnp.int32), heads
 
 
 def rep_sum(grads, width):
@@ -334,21 +703,11 @@
     gain_three = ffn_gain.astype(f32)
     gain_four = post_ffn_gain.astype(f32)
 
-    def by_device(weight):
-        heads = weight.reshape(part_rows, KV, -1)
-        if share > 1:
-            heads = jnp.repeat(heads, share, axis=1)
-        return heads.reshape(part_rows, n, -1)
-
-    qkv_parts = jnp.concatenate(
-        (w_query.reshape(part_rows, n, q_cols), by_device(w_key), by_device(w_value)), axis=2
-    ).transpose(1, 0, 2)
-    qkv_heads = lax.all_to_all(qkv_parts, "shard", 0, 0, tiled=True).reshape(width, -1)
-
     residual = tokens.astype(f32)
     normed, rms_one = normalize(residual, gain_one)
-    normed_all = gather_rows(normed.astype(bf16))
-    codes = gather_rows(seg_ids.astype(bf16)).astype(jnp.int32)
+    normed_all, codes, qkv_heads = first_gather(
+        normed.astype(bf16), seg_ids, w_query, w_key, w_value
+    )
     qkv = jnp.dot(normed_all, qkv_heads, preferred_element_type=f32).astype(bf16)
     queries = qkv[:, :q_cols].reshape(group_rows, kv_heads, repeat, HEAD_SIZE)
     keys = qkv[:, q_cols : q_cols + k_cols].reshape(group_rows, kv_heads, HEAD_SIZE)
@@ -383,26 +742,22 @@
     probs_b = probs.astype(bf16)
     mixed = jnp.einsum("krts,skh->tkrh", probs_b, values, preferred_element_type=f32)
     mixed = mixed.reshape(group_rows, q_cols).astype(bf16)
-    attn_out = scatter_rows(
-        jnp.dot(mixed, w_out, preferred_element_type=f32).astype(bf16)
-    ).astype(f32)
+    attn_out = scatter_rows(jnp.dot(mixed, w_out, preferred_element_type=f32).astype(bf16), 3)
     post_one, rms_two = normalize(attn_out, gain_two)
     middle = residual + post_one
     normed_two, rms_three = normalize(middle, gain_three)
-    normed_two_all = gather_rows(normed_two.astype(bf16))
+    normed_two_all = gather_rows(normed_two.astype(bf16), 4)
     gate_pre = jnp.dot(normed_two_all, w_gate, preferred_element_type=f32)
     up_pre = jnp.dot(normed_two_all, w_up, preferred_element_type=f32)
     hidden, geglu_back = jax.vjp(geglu, gate_pre, up_pre)
     hidden_b = hidden.astype(bf16)
-    ffn_out = scatter_rows(
-        jnp.dot(hidden_b, w_down, preferred_element_type=f32).astype(bf16)
-    ).astype(f32)
+    ffn_out = scatter_rows(jnp.dot(hidden_b, w_down, preferred_element_type=f32).astype(bf16), 5)
     post_two, rms_four = normalize(ffn_out, gain_four)
     output = (middle + post_two).astype(bf16)
 
     grad_out = cotangent.astype(f32)
     grad_ffn, grad_gain_four = norm_back(ffn_out, rms_four, gain_four, grad_out)
-    grad_ffn_all = gather_rows(grad_ffn.astype(bf16))
+    grad_ffn_all = gather_rows(grad_ffn.astype(bf16), 6)
     down_part = jnp.einsum("tf,td->fd", hidden_b, grad_ffn_all, preferred_element_type=f32)
     grad_hidden = jnp.einsum("td,fd->tf", grad_ffn_all, w_down, preferred_element_type=f32)
     grad_gate, grad_up = geglu_back(grad_hidden)
@@ -410,13 +765,13 @@
     grad_up_b = grad_up.astype(bf16)
     grad_normed_two = jnp.einsum("tf,df->td", grad_gate_b, w_gate, preferred_element_type=f32)
     grad_normed_two += jnp.einsum("tf,df->td", grad_up_b, w_up, preferred_element_type=f32)
-    grad_normed_two = scatter_rows(grad_normed_two.astype(bf16)).astype(f32)
+    grad_normed_two = scatter_rows(grad_normed_two.astype(bf16), 7)
     gate_part = jnp.einsum("td,tf->df", normed_two_all, grad_gate_b, preferred_element_type=f32)
     up_part = jnp.einsum("td,tf->df", normed_two_all, grad_up_b, preferred_element_type=f32)
     grad_middle_part, grad_gain_three = norm_back(middle, rms_three, gain_three, grad_normed_two)
     grad_middle = grad_out + grad_middle_part
     grad_attn, grad_gain_two = norm_back(attn_out, rms_two, gain_two, grad_middle)
-    grad_attn_all = gather_rows(grad_attn.astype(bf16))
+    grad_attn_all = gather_rows(grad_attn.astype(bf16), 8)
     out_part = jnp.einsum("tj,td->jd", mixed, grad_attn_all, preferred_element_type=f32)
     grad_mixed = jnp.einsum("td,jd->tj", grad_attn_all, w_out, preferred_element_type=f32)
     grad_mixed = grad_mixed.astype(bf16).reshape(group_rows, kv_heads, repeat, HEAD_SIZE)
@@ -436,7 +791,7 @@
         ),
         axis=1,
     ).astype(bf16)
-    grad_parts = lax.all_gather(grad_parts, "shard", axis=0)
+    grad_parts = gather_rows(grad_parts, 9).reshape(n, group_rows, -1)
 
     def whole_heads(parts):
         if share > 1:
@@ -453,9 +808,7 @@
     )
     qkv_local = jnp.concatenate((w_query, w_key, w_value), axis=1)
     grad_normed = jnp.einsum("tj,dj->td", grad_qkv, qkv_local, preferred_element_type=f32)
-    grad_normed = lax.all_to_all(
-        grad_normed.astype(bf16).reshape(n, tok_rows, part_rows), "shard", 0, 0, tiled=True
-    )
+    grad_normed = exchange(grad_normed.astype(bf16).reshape(n, tok_rows, part_rows), 10)
     grad_normed = grad_normed.transpose(1, 0, 2).reshape(tok_rows, width).astype(f32)
     normed_cols = lax.dynamic_slice_in_dim(normed_all, me * part_rows, part_rows, axis=1)
     qkv_part = jnp.einsum("td,tj->dj", normed_cols, grad_qkv, preferred_element_type=f32)

time: 1240 us -> 1090 us (0.88)
  waiting for transfers between devices: 328 us -> 0.02 us
  Pallas kernels: 457 us -> 760 us
  blocking collectives: 74.6 us -> 0 us
  local copies, waits for them, and re-layouts: 81.5 us -> 63.4 us
  matrix products: 189 us -> 175 us
  other arithmetic: 79.5 us -> 66.9 us
    pallas_call x0 -> x9, Pallas kernels: none -> 307 us  [the longest x4 138 us: gather4(): pl.pallas_call(gather_kernel, out_shape=jax.ShapeDtypeStruct((4 * rows, w...]
    all_gather x5 -> x0, waiting for transfers between devices: 187 us -> none  [the longest x4 142 us: gather_rows(): return lax.all_gather(block, 'shard', axis=0, tiled=True)]
    reduce_scatter x3 -> x0, waiting for transfers between devices: 140 us -> none  [scatter_rows(): return lax.psum_scatter(partial, 'shard', scatter_dimension=0, tiled=True)]
    unnamed x1 -> x0, blocking collectives: 74.6 us -> none
  transfers between devices with their start and end apart: 11 -> 1, of which waited for: 7 -> 0; matrix products, arithmetic and copies ran while one was open for 12% -> 11% of each run, Pallas kernels for 37% -> 42%
where the time goes in v3:
time: 1090 us; the launch traced here: 1080 us
  Pallas kernels  760 us (70%)
  matrix products  175 us (16%)
  other arithmetic  66.9 us (6%)
  local copies, waits for them, and re-layouts  63.4 us (6%)
  between operations  15.1 us (1%)
    pallas_call x1, Pallas kernels, chain_sum(): pl.pallas_call(functools.partial(chain_kernel, counts, chunk), out_shape=...  453 us
    pallas_call x4, Pallas kernels, gather4(): pl.pallas_call(gather_kernel, out_shape=jax.ShapeDtypeStruct((4 * rows, w...  138 us
    pallas_call x3, Pallas kernels, scatter4(): pl.pallas_call(scatter_kernel, out_shape=jax.ShapeDtypeStruct((rows, widt...  91.4 us
    pallas_call x1, Pallas kernels, prologue4(): pl.pallas_call(functools.partial(prologue_kernel, counts), out_shape=(jax...  68.1 us
    convert_element_type x4, other arithmetic, rep_sum(): total.reshape(grad.shape).astype(jnp.float32)  36 us
    dot_general x1, matrix products, body(): jnp.einsum('td,fd->tf', grad_ffn_all, w_down, preferred_element_type=f32)  22 us
  transfers between devices with their start and end apart: 1, of which 0 were waited for; matrix products, arithmetic and copies ran while one was open for 11% of the time, Pallas kernels for 42%

profile of v3, /device:TPU:0, one launch (start us, length us, event | category | flops | bytes accessed | tf_op | source)
XLA Modules:
  0.0 1080.4 jit_solution(2081804745418389421)
XLA Ops:
  8.1 1.4 fusion.37
  13.4 2.4 fusion.39.x_ref
  15.8 68.1 %shard_map.246 = (bf16[768,2304]{1,0:T(8,128)(2,1)}, bf16[4,16,128]{2,1,0:T(8,128)(2,1)}, bf16[2304,1024]{1,0:T(8,128)(2,1)}) custom-call(bf16[192,2304]{1,0:T(8,128)(2,1)} %fusion.39.x_ref, bf16[16,128]{1,0:T(8,128)(2,1)} %pad_bitcast_fusion.code_ref, bf16[576,2048]{1,0:T(8,128)(2,1)} %query_ref.1, bf16[576,1024]{1,0:T(8,128)(2,1)} %key_ref.1, ...), custom_call_target="tpu_custom_call" | custom-call | bytes 70778880 | tf_op jit(solution)/shard_map/pallas_call | solution.py:572
  84.9 7.2 convolution_convert_fusion.7
  93.4 1.2 copy.109
  94.5 2.0 fusion.28
  96.6 2.8 fusion.19
  99.4 1.4 fusion.18
  100.8 3.2 fusion.50
  105.0 2.0 convolution_convert_fusion.5.part_ref
  107.0 32.0 %shard_map.247 = f32[192,2304]{1,0:T(8,128)S(1)} custom-call(bf16[768,2304]{1,0:T(8,128)(2,1)S(1)} %convolution_convert_fusion.5.part_ref), custom_call_target="tpu_custom_call" | custom-call | bytes 35389440 | tf_op jit(solution)/shard_map/pallas_call | solution.py:397
  140.7 1.2 copy-done.5
  143.1 30.1 %shard_map.248 = bf16[768,2304]{1,0:T(8,128)(2,1)} custom-call(bf16[192,2304]{1,0:T(8,128)(2,1)} %multiply_convert_fusion.2.x_ref), custom_call_target="tpu_custom_call" | custom-call | bytes 35389440 | tf_op jit(solution)/shard_map/pallas_call | solution.py:324
  173.2 16.4 %fusion.74 = f32[768,2304]{1,0:T(8,128)} fusion(bf16[768,2304]{1,0:T(8,128)(2,1)} %shard_map.248, bf16[2304,2304]{1,0:T(8,128)(2,1)} %param.25), kind=kOutput, calls=%fused_computation.136 | convolution fusion | flops 8153726976 | bytes 21233664 | tf_op jit(solution)/shard_map/dot_general | solution.py:750
  189.6 15.4 %multiply_convert_fusion.1 = (bf16[768,2304]{1,0:T(8,128)(2,1)S(1)}, f32[768,2304]{1,0:T(8,128)}) fusion(f32[768,2304]{1,0:T(8,128)} %fusion.74, bf16[768,2304]{1,0:T(8,128)(2,1)S(1)} %copy-done.19, bf16[2304,2304]{1,0:T(8,128)(2,1)} %param.26), kind=kOutput, calls=%fused_computation.14 | convolution fusion | flops 8171421696 | bytes 31850496 | tf_op jit(solution)/shard_map/dot_general | solution.py:751
  205.0 1.8 copy-done.42
  206.8 8.6 convolution_convert_fusion.4.part_ref
  215.4 30.1 %shard_map.249 = f32[192,2304]{1,0:T(8,128)S(1)} custom-call(bf16[768,2304]{1,0:T(8,128)(2,1)S(1)} %convolution_convert_fusion.4.part_ref), custom_call_target="tpu_custom_call" | custom-call | bytes 35389440 | tf_op jit(solution)/shard_map/pallas_call | solution.py:397
  247.1 1.9 fusion.33
  248.9 28.6 %shard_map.250 = bf16[768,2304]{1,0:T(8,128)(2,1)} custom-call(bf16[192,2304]{1,0:T(8,128)(2,1)} %get-tuple-element.50.x_ref), custom_call_target="tpu_custom_call" | custom-call | bytes 35389440 | tf_op jit(solution)/shard_map/pallas_call | solution.py:324
  277.6 22.0 %multiply_convert_fusion = (bf16[768,2304]{1,0:T(8,128)(2,1)}, bf16[768,2304]{1,0:T(8,128)(2,1)}) fusion(f32[768,2304]{1,0:T(8,128)} %fusion.74, f32[768,2304]{1,0:T(8,128)} %get-tuple-element.63, bf16[768,2304]{1,0:T(8,128)(2,1)} %shard_map.250, bf16[2304,2304]{1,0:T(8,128)(2,1)} %param.27), kind=kOutput, calls=%fused_computation.13 | convolution fusion | flops 8196194304 | bytes 35389440 | tf_op jit(solution)/shard_map/td,fd->tf/dot_general | solution.py:762
  299.5 14.9 %fusion.75 = f32[768,2304]{1,0:T(8,128)} fusion(bf16[768,2304]{1,0:T(8,128)(2,1)} %get-tuple-element.45, bf16[2304,2304]{1,0:T(8,128)(2,1)} %param.25), kind=kOutput, calls=%fused_computation.137 | convolution fusion | flops 8153726976 | bytes 21233664 | tf_op jit(solution)/shard_map/tf,df->td/dot_general | solution.py:766
  314.4 15.5 %add_convert_fusion.part_ref = bf16[768,2304]{1,0:T(8,128)(2,1)} fusion(f32[768,2304]{1,0:T(8,128)} %fusion.75, bf16[768,2304]{1,0:T(8,128)(2,1)} %get-tuple-element.44, bf16[2304,2304]{1,0:T(8,128)(2,1)} %param.26), kind=kOutput, calls=%fused_computation.12 | convolution fusion | flops 8157265920 | bytes 24772608 | tf_op jit(solution)/shard_map/tf,df->td/dot_general | solution.py:767
  329.9 2.0 copy-done.4
  331.9 29.3 %shard_map.251 = f32[192,2304]{1,0:T(8,128)S(1)} custom-call(bf16[768,2304]{1,0:T(8,128)(2,1)S(1)} %copy-done.4), custom_call_target="tpu_custom_call" | custom-call | bytes 35389440 | tf_op jit(solution)/shard_map/pallas_call | solution.py:397
  361.2 1.2 multiply_reduce_fusion
  362.4 1.7 multiply_reduce_fusion.1
  364.2 1.2 copy-done.12
  365.4 1.3 subtract_convert_fusion.x_ref
  366.7 29.5 %shard_map.252 = bf16[768,2304]{1,0:T(8,128)(2,1)} custom-call(bf16[192,2304]{1,0:T(8,128)(2,1)} %subtract_convert_fusion.x_ref), custom_call_target="tpu_custom_call" | custom-call | bytes 35389440 | tf_op jit(solution)/shard_map/pallas_call | solution.py:324
  396.3 4.2 convolution_convert_fusion.9
  400.5 1.6 fusion.60
  402.2 2.1 fusion.15
  404.3 2.5 fusion.20
  407.9 1.6 fusion.63
  409.8 2.4 pad_maximum_fusion.3.x_ref
  412.1 49.5 %shard_map.253 = bf16[3072,1024]{1,0:T(8,128)(2,1)} custom-call(bf16[768,1024]{1,0:T(8,128)(2,1)} %pad_maximum_fusion.3.x_ref), custom_call_target="tpu_custom_call" | custom-call | bytes 62914560 | tf_op jit(solution)/shard_map/pallas_call | solution.py:324
  461.6 3.9 slice.60
  466.5 1.4 fusion.73
  467.9 2.6 copy.107
  470.5 4.9 copy.106
  475.4 1.6 copy.108
  476.9 7.7 fusion.47
  484.7 1.3 copy.90
  486.0 10.1 shard_map.254
  496.1 1.3 convert_bitcast_fusion
  497.5 2.5 copy.91
  500.0 2.4 reshape.385
  503.8 13.8 %convolution_convert_fusion.2.refs_0_ = bf16[2304,2304]{1,0:T(8,128)(2,1)} fusion(bf16[768,2304]{1,0:T(8,128)(2,1)} %copy-done.42, bf16[768,2304]{1,0:T(8,128)(2,1)} %shard_map.250), kind=kOutput, calls=%fused_computation.2 | convolution fusion | flops 8159035392 | bytes 17694720 | tf_op jit(solution)/shard_map/tf,td->fd/dot_general | solution.py:761
  517.6 11.0 %convolution_convert_fusion.refs_2_ = bf16[2304,2304]{1,0:T(8,128)(2,1)} fusion(bf16[768,2304]{1,0:T(8,128)(2,1)S(1)} %copy-done.20, bf16[768,2304]{1,0:T(8,128)(2,1)S(1)} %copy-done.41), kind=kOutput, calls=%fused_computation | convolution fusion | flops 8159035392 | bytes 17694720 | tf_op jit(solution)/shard_map/td,tf->df/dot_general | solution.py:770
  528.5 10.7 convolution_convert_fusion.1.refs_1_
  539.3 9.6 convolution_convert_fusion.3
  548.9 9.7 reshape.381.refs_4_
  558.5 4.0 convolution_convert_fusion.6.refs_3_
  562.6 452.7 %shard_map.255 = (bf16[2304,2304]{1,0:T(8,128)(2,1)}, bf16[2304,2304]{1,0:T(8,128)(2,1)}, bf16[2304,2304]{1,0:T(8,128)(2,1)}, bf16[512,2304]{1,0:T(8,128)(2,1)S(1)}, bf16[1024,2304]{1,0:T(8,128)(2,1)}) custom-call(bf16[2304,2304]{1,0:T(8,128)(2,1)} %convolution_convert_fusion.2.refs_0_, bf16[2304,2304]{1,0:T(8,128)(2,1)} %convolution_convert_fusion.1.refs_1_, ...), custom_call_target="tpu_custom_call" | custom-call | bytes 155713536 | tf_op jit(solution)/shard_map/pallas_call | solution.py:244
  1015.3 10.0 reshape.386
  1025.2 5.1 slice.64
  1030.3 2.7 convert_element_type.189
  1033.1 15.6 %convert_element_type.190 = f32[2304,2304]{1,0:T(8,128)} convert(bf16[2304,2304]{1,0:T(8,128)(2,1)} %get-tuple-element.26) | non-fusion elementwise | flops 5308416 | bytes 31850496 | tf_op jit(solution)/shard_map/convert_element_type | solution.py:667
  1048.7 10.2 convert_element_type.191
  1058.9 7.6 convert_element_type.192
  1066.5 3.1 fusion.72
  1069.7 1.4 fusion.43
  1071.1 1.5 reduce_sum.169
  (153 shorter events, 16.8 us)
Async XLA Ops:
  7.2 97.8 %copy-start = (bf16[512,2304]{1,0:T(8,128)(2,1)S(1)}, bf16[512,2304]{1,0:T(8,128)(2,1)}, u32[]{:S(2)}) copy-start(bf16[512,2304]{1,0:T(8,128)(2,1)} %param.22) | copy-start | bytes 7077892
  7.2 1063.9 %all-gather.4.cloned.1.call-start = ((), (), s32[]{:S(2)}) async-start(), calls=%async_computation | async-start | bytes 1216512 | tf_op jit(solution)/shard_map/all_gather | solution.py:818
  10.1 3.4 copy-start.34
  11.3 2.1 copy-start.26
  13.4 71.3 %copy-start.37 = (s32[1,13]{1,0:T(1,128)S(1)}, s32[1,13]{1,0:T(1,128)}, u32[]{:S(2)}) copy-start(s32[1,13]{1,0:T(1,128)} %param.17) | copy-start | bytes 160
  92.1 1.2 copy-start.24
  96.6 4.3 copy-start.17
  99.4 4.7 copy-start.11
  99.4 4.7 copy-start.30
  100.8 3.2 copy-start.32
  104.1 0.9 copy-start.38
  107.0 33.2 %copy-start.9 = (bf16[192,2304]{1,0:T(8,128)(2,1)S(1)}, bf16[192,2304]{1,0:T(8,128)(2,1)}, u32[]{:S(2)}) copy-start(bf16[192,2304]{1,0:T(8,128)(2,1)} %param.15) | copy-start | bytes 2654212
  139.0 1.2 copy-start.2
  140.7 1.2 copy-start.5
  173.2 16.4 %copy-start.19 = (bf16[768,2304]{1,0:T(8,128)(2,1)S(1)}, bf16[768,2304]{1,0:T(8,128)(2,1)}, u32[]{:S(2)}) copy-start(bf16[768,2304]{1,0:T(8,128)(2,1)} %shard_map.248) | copy-start | bytes 10616836
  173.2 33.6 %slice-start.11 = ((s8[10616832]{0:T(1024)(128)(4,1)}), s8[4194304]{0:T(1024)(128)(4,1)S(1)}, s32[]{:S(2)}) async-start(s8[10616832]{0:T(1024)(128)(4,1)} %bitcast.188), calls=%async_computation.12 | async-start | bytes 8388608
  173.2 33.6 %slice-start.12 = ((s8[10616832]{0:T(1024)(128)(4,1)}), s8[4194304]{0:T(1024)(128)(4,1)S(1)}, s32[]{:S(2)}) async-start(s8[10616832]{0:T(1024)(128)(4,1)} %bitcast.188), calls=%async_computation.13 | async-start | bytes 8388608
  189.6 17.2 %slice-start.13 = ((s8[10616832]{0:T(1024)(128)(4,1)}), s8[2228224]{0:T(1024)(128)(4,1)S(1)}, s32[]{:S(2)}) async-start(s8[10616832]{0:T(1024)(128)(4,1)} %bitcast.188), calls=%async_computation.14 | async-start | bytes 4456448
  205.0 1.8 copy-start.42
  215.4 30.4 %copy-start.16 = (bf16[192,2304]{1,0:T(8,128)(2,1)S(1)}, bf16[192,2304]{1,0:T(8,128)(2,1)}, u32[]{:S(2)}) copy-start(bf16[192,2304]{1,0:T(8,128)(2,1)} %param.29) | copy-start | bytes 2654212
  245.6 1.5 copy-start.6
  329.9 2.0 copy-start.4
  331.9 29.3 %copy-start.7 = (f32[192,2304]{1,0:T(8,128)S(1)}, f32[192,2304]{1,0:T(8,128)}, u32[]{:S(2)}) copy-start(f32[192,2304]{1,0:T(8,128)} %copy-done.5) | copy-start | bytes 5308420
  331.9 30.6 %copy-start.3 = (f32[192,2304]{1,0:T(8,128)S(1)}, f32[192,2304]{1,0:T(8,128)}, u32[]{:S(2)}) copy-start(f32[192,2304]{1,0:T(8,128)} %copy-done.2) | copy-start | bytes 5308420
  364.2 1.3 copy-start.12
  365.4 35.0 %slice-start.3 = ((s8[4718592]{0:T(1024)(128)(4,1)}), s8[524288]{0:T(1024)(128)(4,1)S(1)}, s32[]{:S(2)}) async-start(s8[4718592]{0:T(1024)(128)(4,1)} %bitcast.168), calls=%async_computation.4 | async-start | bytes 1048576
  396.2 4.2 slice-start.4
  396.2 4.2 copy-start.18
  396.2 4.2 copy-start.31
  396.3 4.2 copy-start.33
  400.5 1.7 copy-start.25
  406.8 1.1 copy-start.23
  461.6 4.9 copy-start.8
  466.5 1.4 copy-start.28
  466.5 1.4 copy-start.29
  470.5 6.5 copy-start.22
  497.4 4.9 copy-start.10
  497.5 4.9 copy-start.27
  497.5 4.9 copy-start.35
  502.4 15.2 %copy-start.14 = (f32[192,2304]{1,0:T(8,128)}, f32[192,2304]{1,0:T(8,128)S(1)}, u32[]{:S(2)}) copy-start(f32[192,2304]{1,0:T(8,128)S(1)} %reshape.385) | copy-start | bytes 5308420
  503.8 13.8 %copy-start.20 = (bf16[768,2304]{1,0:T(8,128)(2,1)S(1)}, bf16[768,2304]{1,0:T(8,128)(2,1)}, u32[]{:S(2)}) copy-start(bf16[768,2304]{1,0:T(8,128)(2,1)} %shard_map.248) | copy-start | bytes 10616836
  503.8 13.8 %copy-start.41 = (bf16[768,2304]{1,0:T(8,128)(2,1)S(1)}, bf16[768,2304]{1,0:T(8,128)(2,1)}, u32[]{:S(2)}) copy-start(bf16[768,2304]{1,0:T(8,128)(2,1)} %get-tuple-element.44) | copy-start | bytes 10616836
  517.6 11.0 %copy-start.40 = (bf16[768,2304]{1,0:T(8,128)(2,1)S(1)}, bf16[768,2304]{1,0:T(8,128)(2,1)}, u32[]{:S(2)}) copy-start(bf16[768,2304]{1,0:T(8,128)(2,1)} %get-tuple-element.45) | copy-start | bytes 10616836
  528.5 10.7 copy-start.21
  548.9 9.7 copy-start.39
  1030.3 18.3 %slice-start.8 = ((s8[10616832]{0:T(1024)(128)(4,1)}), s8[4194304]{0:T(1024)(128)(4,1)S(1)}, s32[]{:S(2)}) async-start(s8[10616832]{0:T(1024)(128)(4,1)} %bitcast.172), calls=%async_computation.9 | async-start | bytes 8388608
  1033.1 15.6 %slice-start.9 = ((s8[10616832]{0:T(1024)(128)(4,1)}), s8[4194304]{0:T(1024)(128)(4,1)S(1)}, s32[]{:S(2)}) async-start(s8[10616832]{0:T(1024)(128)(4,1)} %bitcast.172), calls=%async_computation.10 | async-start | bytes 8388608
  1033.1 15.6 %slice-start.10 = ((s8[10616832]{0:T(1024)(128)(4,1)}), s8[2228224]{0:T(1024)(128)(4,1)S(1)}, s32[]{:S(2)}) async-start(s8[10616832]{0:T(1024)(128)(4,1)} %bitcast.172), calls=%async_computation.11 | async-start | bytes 4456448
  1033.1 25.8 %slice-start.5 = ((s8[10616832]{0:T(1024)(128)(4,1)}), s8[4194304]{0:T(1024)(128)(4,1)S(1)}, s32[]{:S(2)}) async-start(s8[10616832]{0:T(1024)(128)(4,1)} %bitcast.170), calls=%async_computation.6 | async-start | bytes 8388608
  1033.1 25.8 %slice-start.6 = ((s8[10616832]{0:T(1024)(128)(4,1)}), s8[4194304]{0:T(1024)(128)(4,1)S(1)}, s32[]{:S(2)}) async-start(s8[10616832]{0:T(1024)(128)(4,1)} %bitcast.170), calls=%async_computation.7 | async-start | bytes 8388608
  1048.7 10.2 slice-start.7
  1048.7 17.8 %slice-start = ((s8[9437184]{0:T(1024)(128)(4,1)}), s8[4194304]{0:T(1024)(128)(4,1)S(1)}, s32[]{:S(2)}) async-start(s8[9437184]{0:T(1024)(128)(4,1)} %bitcast.164), calls=%async_computation.1 | async-start | bytes 8388608
  1048.7 17.8 %slice-start.1 = ((s8[9437184]{0:T(1024)(128)(4,1)}), s8[4194304]{0:T(1024)(128)(4,1)S(1)}, s32[]{:S(2)}) async-start(s8[9437184]{0:T(1024)(128)(4,1)} %bitcast.164), calls=%async_computation.2 | async-start | bytes 8388608
  1058.9 7.6 slice-start.2
  1066.5 3.2 copy-start.13
  1066.5 3.2 copy-start.15
  1066.5 3.2 copy-start.36
  1066.5 6.7 copy-start.1
Sparse Core Ops, SparseCore 0:
  503.9 54.3 all-gather.3

commit v4 on v3

--- a/solution.py
+++ b/solution.py
@@ -1,4 +1,6 @@
 import functools
+import math
+import types
 
 import jax
 import jax.numpy as jnp
@@ -589,6 +591,881 @@
     )(block, codes, w_query, w_key, w_value)
 
 
+TILE = 256
+PAIR = 2 * CHUNK
+DEEP = 8
+ROOT_TWO_PI = math.sqrt(2.0 / math.pi)
+
+
+def dot_rows(left, right):
+    return lax.dot_general(left, right, (((1,), (1,)), ((), ())), preferred_element_type=jnp.float32)
+
+
+def dot_plain(left, right):
+    return lax.dot_general(left, right, (((1,), (0,)), ((), ())), preferred_element_type=jnp.float32)
+
+
+def dot_columns(left, right):
+    return lax.dot_general(left, right, (((0,), (0,)), ((), ())), preferred_element_type=jnp.float32)
+
+
+def backward_kernel(dims, names, *refs):
+    r = types.SimpleNamespace(**dict(zip(names, refs)))
+    tokens, local, width, inner_width, head_cols = dims
+    f32, bf16 = jnp.float32, jnp.bfloat16
+    half = local // 2
+    q_cols = head_cols // 2
+    k_cols = head_cols // 4
+    heads = q_cols // HEAD_SIZE
+    part = width // 4
+    part_wide = r.gain_one.shape[1]
+    side = 2 * head_cols
+    n_a = inner_width // TILE
+    n_b = width // TILE
+    block = min(TILE, tokens)
+    n_blocks = tokens // block
+
+    counts = (
+        inner_width // PAIR, width // PAIR, width // PAIR, r.w_out.shape[0] // PAIR, part // CHUNK
+    )
+    first = [sum(counts[:job]) for job in range(6)]
+    steps = first[5]
+    b_at = (n_a + 1) // 2
+    c_at = b_at + n_b
+    d_at = c_at + 5
+    f_at = d_at + 5
+    g_at = f_at + 1
+    h_at = g_at + heads * n_blocks
+    i_at = h_at + 9
+    k_at = i_at + 3
+    assert b_at <= first[1] and f_at < first[3] and i_at < first[4] and first[1] <= i_at
+    assert first[2] <= i_at and k_at + 5 <= steps + 8
+
+    place = lax.axis_index("rep")
+    chips = lax.axis_size("rep") // 2
+    chip, core = place // 2, place % 2
+    left = chip < chips // 2
+    is_end = (chip == 0) | (chip == chips - 1)
+    is_mid = (chip == chips // 2 - 1) | (chip == chips // 2)
+    twin = {"rep": place + 1 - 2 * core}
+    inner = {"rep": jnp.where(left, place + 2, place - 2)}
+    outer = {"rep": jnp.where(is_end, place, jnp.where(left, place - 2, place + 2))}
+    next_chip = {"rep": place + 2 - 4 * (chip % 2)}
+    far_chip = {"rep": (place + 4) % 8}
+    me, x_place, y_place, far_place = plane_places()
+    x_other, y_other = {"shard": x_place}, {"shard": y_place}
+    plane = [{"shard": (me + step) % 4} for step in (1, 2, 3)]
+
+    def tell(sem, where):
+        pl.semaphore_signal(sem, inc=1, device_id=where, device_id_type=pl.DeviceIdType.MESH)
+
+    def load(src, dst, index):
+        return pltpu.make_async_copy(src, dst, r.load_sem.at[index])
+
+    load_ffn = load(r.grad_ffn, r.ffn_buf.at[:, pl.ds(0, width)], 0)
+    load_hidden = load(r.hidden, r.hidden_buf.at[:, pl.ds(0, inner_width)], 1)
+    load_two = load(r.normed_two, r.two_buf, 2)
+    load_small = (
+        load(r.middle, r.middle_buf, 3),
+        load(r.attn_out, r.attn_buf, 4),
+        load(r.cotangent, r.cot_buf, 5),
+        load(r.qkv, r.qkv_buf, 6),
+        load(r.mixed, r.mixed_buf, 7),
+        load(r.normed_cols, r.cols_buf, 8),
+        load(r.token_blocks, r.token_buf, 9),
+    )
+
+    def weight_tile(index):
+        return r.weights.at[pl.ds(pl.multiple_of(index * TILE, TILE), TILE)]
+
+    def a_loads(tile, buf):
+        rows = pl.ds(pl.multiple_of(tile * TILE, TILE), TILE)
+        return (
+            load(r.w_down.at[rows], weight_tile(buf).at[:, pl.ds(0, width)], 10 + buf),
+            load(r.gate.at[:, rows], r.gate_buf.at[buf], 12 + buf),
+            load(r.up.at[:, rows], r.up_buf.at[buf], 14 + buf),
+        )
+
+    def b_loads(tile):
+        rows = pl.ds(pl.multiple_of(tile * TILE, TILE), TILE)
+        buf = 2 - 2 * (tile % 2)
+        sem = 16 + 2 * (tile % 2)
+        return (
+            load(r.w_gate.at[rows], weight_tile(buf).at[:, pl.ds(0, inner_width)], sem),
+            load(r.w_up.at[rows], weight_tile(buf + 1).at[:, pl.ds(0, inner_width)], sem + 1),
+        )
+
+    def b_store(tile):
+        columns = pl.ds(pl.multiple_of(tile * TILE, TILE), TILE)
+        return pltpu.make_async_copy(
+            r.stage.at[tile % 2], r.partial.at[:, columns], r.stage_sem.at[tile % 2]
+        )
+
+    load_ffn.start()
+    for buf in range(2):
+        for copy in a_loads(buf, buf):
+            copy.start()
+    load_hidden.start()
+    load_two.start()
+    for copy in load_small:
+        copy.start()
+    for copy in b_loads(0):
+        copy.start()
+
+    barrier = pltpu.get_barrier_semaphore()
+    for where in [twin, inner, far_chip] + plane:
+        tell(barrier, where)
+
+    @pl.when(is_end)
+    def _():
+        pl.semaphore_wait(barrier, 6)
+
+    @pl.when(jnp.logical_not(is_end))
+    def _():
+        tell(barrier, outer)
+        pl.semaphore_wait(barrier, 7)
+
+    load_ffn.wait()
+
+    def a_tile(tile, buf):
+        for copy in a_loads(tile, buf):
+            copy.wait()
+        r.wide[...] = dot_rows(r.ffn_buf[:, pl.ds(0, width)], weight_tile(buf)[:, pl.ds(0, width)])
+        columns = pl.ds(pl.multiple_of(tile * TILE, TILE), TILE)
+
+        def rows_of(index, carry):
+            rows = pl.ds(pl.multiple_of(index * 32, 32), 32)
+            grad = r.wide[rows]
+            gate = r.gate_buf[buf, rows].astype(f32)
+            up = r.up_buf[buf, rows].astype(f32)
+            curve = jnp.tanh(ROOT_TWO_PI * (gate + 0.044715 * gate * gate * gate))
+            slope = (1.0 - curve * curve) * (ROOT_TWO_PI * (1.0 + 3.0 * 0.044715 * gate * gate))
+            gelu_slope = 0.5 * (1.0 + curve) + 0.5 * gate * slope
+            r.gate_grad[rows, columns] = (grad * up * gelu_slope).astype(bf16)
+            r.up_grad[rows, columns] = (grad * (0.5 * gate * (1.0 + curve))).astype(bf16)
+            return carry
+
+        lax.fori_loop(0, tokens // 32, rows_of, 0)
+
+        @pl.when(tile + 2 < n_a)
+        def _():
+            for copy in a_loads(tile + 2, buf):
+                copy.start()
+
+    def b_tile(tile):
+        for copy in b_loads(tile):
+            copy.wait()
+
+        @pl.when(tile >= 2)
+        def _():
+            b_store(tile - 2).wait()
+
+        buf = 2 - 2 * (tile % 2)
+        some = dot_rows(r.gate_grad[:, pl.ds(0, inner_width)], weight_tile(buf)[:, pl.ds(0, inner_width)])
+        some += dot_rows(r.up_grad[...], weight_tile(buf + 1)[:, pl.ds(0, inner_width)])
+        r.stage[tile % 2] = some.astype(bf16)
+        b_store(tile).start()
+
+        @pl.when(tile + 2 < n_b)
+        def _():
+            for copy in b_loads(tile + 2):
+                copy.start()
+
+    def partial_rows(owner, which):
+        return r.partial.at[pl.ds(pl.multiple_of(owner * local + which * half, 16), half)]
+
+    c_own = (
+        load(partial_rows(y_place, 0), r.c_mine.at[0], 20),
+        load(partial_rows(x_place, 1), r.c_mine.at[1], 21),
+        load(partial_rows(me, 0), r.c_mine.at[2], 22),
+        load(partial_rows(me, 1), r.c_mine.at[3], 23),
+    )
+
+    def c_send(src, index, where):
+        return remote(src, r.c_landed.at[index], r.c_send.at[index], r.c_recv.at[index], where)
+
+    c_first = (
+        c_send(partial_rows(far_place, 0), 0, x_other),
+        c_send(partial_rows(far_place, 1), 1, y_other),
+        c_send(partial_rows(x_place, 0), 2, x_other),
+        c_send(partial_rows(y_place, 1), 3, y_other),
+    )
+    c_on = (c_send(r.c_mine.at[0], 4, y_other), c_send(r.c_mine.at[1], 5, x_other))
+
+    def c_start():
+        b_store(n_b - 2).wait()
+        b_store(n_b - 1).wait()
+        for copy in c_first + c_own:
+            copy.start()
+
+    def c_pass():
+        for copy in c_own:
+            copy.wait()
+        for index in range(2):
+            c_first[index].wait_recv()
+            r.c_mine[index] = add_low(r.c_mine[index], r.c_landed[index])
+            c_on[index].start()
+
+    def d_norms():
+        for copy in load_small:
+            copy.wait()
+        for copy in c_first:
+            copy.wait_send()
+        for copy in c_first[2:] + c_on:
+            copy.wait_recv()
+        r.gain_own[...] = r.gain_parts[...]
+
+        def rows_of(which, index, carry):
+            here = pl.ds(pl.multiple_of(index * 16, 16), 16)
+            rows = pl.ds(pl.multiple_of(which * half + index * 16, 16), 16)
+            grad = (
+                r.c_mine[2 + which, here].astype(f32)
+                + r.c_landed[2 + which, here].astype(f32)
+                + r.c_landed[4 + which, here].astype(f32)
+            )
+            middle = r.middle_buf[rows]
+            inv = lax.rsqrt(jnp.mean(middle * middle, axis=-1, keepdims=True) + norm_eps)
+            weighted = grad * r.gains[1:2]
+            mean = jnp.mean(weighted * middle, axis=-1, keepdims=True)
+            r.gain_own[2:3, 0:width] += jnp.sum(grad * middle * inv, axis=0, keepdims=True)
+            grad_mid = (
+                r.cot_buf[rows].astype(f32) + inv * weighted - middle * (inv * inv * inv) * mean
+            )
+            r.middle_buf[rows] = grad_mid
+            attn = r.attn_buf[rows]
+            inv = lax.rsqrt(jnp.mean(attn * attn, axis=-1, keepdims=True) + norm_eps)
+            weighted = grad_mid * r.gains[0:1]
+            mean = jnp.mean(weighted * attn, axis=-1, keepdims=True)
+            r.gain_own[1:2, 0:width] += jnp.sum(grad_mid * attn * inv, axis=0, keepdims=True)
+            grad_attn = inv * weighted - attn * (inv * inv * inv) * mean
+            r.all_grad[pl.ds(pl.multiple_of(me * local + which * half + index * 16, 16), 16)] = (
+                grad_attn.astype(bf16)
+            )
+            return carry
+
+        for which in range(2):
+            lax.fori_loop(0, half // 16, functools.partial(rows_of, which), 0)
+        for copy in c_on:
+            copy.wait_send()
+        keep_middle.start()
+
+    keep_middle = pltpu.make_async_copy(r.middle_buf, r.grad_middle, r.keep_sem.at[0])
+
+    def gather_copies(rows, source, target, send_sem, recv_sem):
+        def send(owner, which, index, where, src):
+            here = pl.ds(pl.multiple_of(owner * 2 * rows + which * rows, 16), rows)
+            return remote(
+                src.at[here] if src is target else src.at[pl.ds(which * rows, rows)],
+                target.at[here], send_sem.at[index], recv_sem.at[index], where,
+            )
+
+        starts = (
+            send(me, 0, 0, x_other, source),
+            send(me, 1, 1, y_other, source),
+            send(me, 1, 2, x_other, source),
+            send(me, 0, 3, y_other, source),
+        )
+        passes = (
+            send(x_place, 0, 4, y_other, target), send(y_place, 1, 5, x_other, target)
+        )
+        return starts, passes
+
+    e_first, e_on = gather_copies(half, r.all_grad, r.all_grad, r.e_send, r.e_recv)
+    h_first, h_on = gather_copies(tokens // 2, r.head_grad, r.grad_qkv, r.h_send, r.h_recv)
+    h_own = pltpu.make_async_copy(
+        r.head_grad, r.grad_qkv.at[pl.ds(pl.multiple_of(me * tokens, 16), tokens)], r.keep_sem.at[1]
+    )
+
+    def pass_on(starts, passes):
+        for index in range(2):
+            starts[index].wait_recv()
+            passes[index].start()
+
+    def gathered(starts, passes):
+        for copy in starts[2:] + passes:
+            copy.wait_recv()
+        for copy in starts + passes:
+            copy.wait_send()
+
+    load_out = load(r.w_out, r.weights.at[pl.ds(0, r.w_out.shape[0]), pl.ds(0, width)], 24)
+
+    def g_loads(item):
+        head, rows = item // n_blocks, pl.ds(pl.multiple_of((item % n_blocks) * block, block), block)
+        return (
+            load(r.probs.at[head, rows], r.probs_buf, 25),
+            load(r.tanh.at[head, rows], r.tanh_buf, 26),
+        )
+
+    def f_mixed():
+        gathered(e_first, e_on)
+        load_out.wait()
+        r.mixed_grad[...] = dot_rows(
+            r.all_grad[...], r.weights[pl.ds(0, r.w_out.shape[0]), pl.ds(0, width)]
+        ).astype(bf16)
+        r.kv_grad[...] = jnp.zeros_like(r.kv_grad)
+        for copy in g_loads(0):
+            copy.start()
+
+    def g_attention(item):
+        head = item // n_blocks
+        rows = pl.ds(pl.multiple_of((item % n_blocks) * block, block), block)
+        columns = pl.ds(pl.multiple_of(head * HEAD_SIZE, HEAD_SIZE), HEAD_SIZE)
+        for copy in g_loads(item):
+            copy.wait()
+        grad_out = r.mixed_grad[rows, columns]
+        values = r.qkv_buf[:, pl.ds(q_cols + k_cols, k_cols)]
+        r.score_grad[...] = dot_rows(grad_out, values)
+
+        def rows_of(index, carry):
+            here = pl.ds(pl.multiple_of(index * 16, 16), 16)
+            probs = r.probs_buf[here]
+            grad = r.score_grad[here]
+            curve = r.tanh_buf[here]
+            total = jnp.sum(probs * grad, axis=-1, keepdims=True)
+            grad = probs * (grad - total) * (1.0 - curve * curve) * (HEAD_SIZE ** (-0.5))
+            r.dots_grad[here] = grad.astype(bf16)
+            r.probs_low[here] = probs.astype(bf16)
+            return carry
+
+        lax.fori_loop(0, block // 16, rows_of, 0)
+
+        @pl.when(item + 1 < heads * n_blocks)
+        def _():
+            for copy in g_loads(item + 1):
+                copy.start()
+
+        keys = r.qkv_buf[:, pl.ds(q_cols, k_cols)]
+        r.head_grad[rows, columns] = dot_plain(r.dots_grad[...], keys).astype(bf16)
+        r.kv_grad[0] += dot_columns(r.dots_grad[...], r.qkv_buf[rows, columns])
+        r.kv_grad[1] += dot_columns(r.probs_low[...], grad_out)
+
+    def h_start():
+        r.head_grad[:, pl.ds(q_cols, k_cols)] = r.kv_grad[0].astype(bf16)
+        r.head_grad[:, pl.ds(q_cols + k_cols, k_cols)] = r.kv_grad[1].astype(bf16)
+        for copy in h_first:
+            copy.start()
+        h_own.start()
+
+    def side_of(owner, kind):
+        buf = r.hidden_buf if owner < 2 else r.ffn_buf
+        size = (q_cols, k_cols, k_cols)[kind]
+        start = (0, 2 * q_cols, 2 * q_cols + 2 * k_cols)[kind] + (owner % 2) * size
+        return buf.at[:, pl.ds(start, size)]
+
+    i_loads = [
+        load(
+            r.grad_qkv.at[
+                pl.ds(owner * tokens, tokens),
+                pl.ds((0, q_cols, q_cols + k_cols)[kind], (q_cols, k_cols, k_cols)[kind]),
+            ],
+            side_of(owner, kind),
+            27 + 3 * owner + kind,
+        )
+        for owner in range(4)
+        for kind in range(3)
+    ] + [
+        load(r.w_query, r.gate_grad.at[pl.ds(0, part), pl.ds(0, 4 * q_cols)], 39),
+        load(r.w_key, r.weights.at[pl.ds(0, part), pl.ds(0, 4 * k_cols)], 40),
+        load(r.w_value, r.weights.at[pl.ds(0, part), pl.ds(4 * k_cols, 4 * k_cols)], 41),
+    ]
+    i_copies = [
+        remote(
+            r.head_grad.at[pl.ds(pl.multiple_of(((me + step) % 4) * local, 16), local), pl.ds(0, part_wide)],
+            r.norm_grad.at[me], r.i_send.at[step - 1], r.i_recv.at[step - 1], plane[step - 1],
+        )
+        for step in (1, 2, 3)
+    ]
+
+    def i_start():
+        gathered(h_first, h_on)
+        h_own.wait()
+        for copy in i_loads:
+            copy.start()
+        for copy in i_loads:
+            copy.wait()
+
+    def i_norm():
+        def rows_of(index, carry):
+            rows = pl.ds(pl.multiple_of(index * block, block), block)
+            some = jnp.zeros((block, part_wide), f32)
+            for owner in range(4):
+                for kind, size in enumerate((q_cols, k_cols, k_cols)):
+                    held = r.gate_grad if kind == 0 else r.weights
+                    start = (0, 0, 4 * k_cols)[kind] + owner * size
+                    some += dot_rows(
+                        side_of(owner, kind)[rows], held[pl.ds(0, part_wide), pl.ds(start, size)]
+                    )
+            r.head_grad[rows, pl.ds(0, part_wide)] = some.astype(bf16)
+            return carry
+
+        lax.fori_loop(0, n_blocks, rows_of, 0)
+        for copy in i_copies:
+            copy.start()
+        r.norm_grad[me] = r.head_grad[
+            pl.ds(pl.multiple_of(me * local, 16), local), pl.ds(0, part_wide)
+        ]
+
+    def k_norm():
+        for copy in i_copies:
+            copy.wait()
+
+        def rows_of(index, carry):
+            rows = pl.ds(pl.multiple_of(index * 16, 16), 16)
+            squares = jnp.zeros((16, 1), f32)
+            mean = jnp.zeros((16, 1), f32)
+            for owner in range(4):
+                tokens_in = r.token_buf[owner, rows].astype(f32)
+                weighted = r.norm_grad[owner, rows].astype(f32) * r.gain_one[owner : owner + 1]
+                squares += jnp.sum(tokens_in * tokens_in, axis=-1, keepdims=True)
+                mean += jnp.sum(weighted * tokens_in, axis=-1, keepdims=True)
+            inv = lax.rsqrt(squares * (1.0 / width) + norm_eps)
+            mean = mean * (1.0 / width)
+            for owner in range(4):
+                tokens_in = r.token_buf[owner, rows].astype(f32)
+                grad = r.norm_grad[owner, rows].astype(f32)
+                r.gain_own[4 + owner : 5 + owner, 0:part_wide] += jnp.sum(
+                    grad * tokens_in * inv, axis=0, keepdims=True
+                )
+                weighted = grad * r.gain_one[owner : owner + 1]
+                r.norm_grad[owner, rows] = (
+                    inv * weighted - tokens_in * (inv * inv * inv) * mean
+                ).astype(bf16)
+            return carry
+
+        lax.fori_loop(0, local // 16, rows_of, 0)
+        keep_part.start()
+        for copy in gain_plane:
+            copy.start()
+
+    keep_part = pltpu.make_async_copy(r.norm_grad, r.resid_part, r.keep_sem.at[2])
+    gain_plane = [
+        remote(r.gain_own, r.gain_plane.at[me], r.gain_send.at[i], r.gain_recv.at[i], where)
+        for i, where in enumerate(plane)
+    ]
+    gain_rep = [
+        remote(r.gain_mine.at[i], r.gain_theirs.at[i], r.gain_send.at[3 + i], r.gain_recv.at[3 + i], where)
+        for i, where in enumerate((twin, next_chip, far_chip))
+    ]
+
+    def k_plane():
+        for copy in gain_plane:
+            copy.wait()
+        r.gain_plane[me] = r.gain_own[...]
+        r.gain_mine[0] = (r.gain_plane[0] + r.gain_plane[1]) + (r.gain_plane[2] + r.gain_plane[3])
+        gain_rep[0].start()
+
+    def k_rep(index):
+        gain_rep[index].wait()
+        total = r.gain_mine[index] + r.gain_theirs[index]
+        if index < 2:
+            r.gain_mine[index + 1] = total
+            gain_rep[index + 1].start()
+        else:
+            r.gain_total[...] = total
+            keep_gains.start()
+
+    keep_gains = pltpu.make_async_copy(r.gain_total, r.gain_sums, r.keep_sem.at[3])
+
+    sums = (r.down_sum, r.gate_sum, r.up_sum, r.out_sum)
+
+    def by_job(step, use):
+        for job in range(5):
+
+            @pl.when((step >= first[job]) & (step < first[job + 1]))
+            def _():
+                use(job, step - first[job])
+
+    def results(job, index, slot):
+        if job < 4:
+            rows = pl.ds(pl.multiple_of((2 * index + core) * CHUNK, CHUNK), CHUNK)
+            return [(r.total.at[slot, :, pl.ds(0, sums[job].shape[1])], sums[job].at[rows])]
+        rows = pl.ds(pl.multiple_of(index * CHUNK, CHUNK), CHUNK)
+        pairs, start = [], 0
+        for ref in (r.query_sum, r.key_sum, r.value_sum):
+            size = ref.shape[1] // 2
+            columns = pl.ds(pl.multiple_of(core * size, 128), size)
+            pairs.append((r.total.at[slot, :, pl.ds(start, size)], ref.at[rows, columns]))
+            start += size
+        return pairs
+
+    def pair_copies(job, index, step):
+        slot = step % 4
+        return [
+            remote(src, dst, r.pair_send.at[slot, i], r.pair_recv.at[step, i], twin)
+            for i, (src, dst) in enumerate(results(job, index, slot))
+        ]
+
+    def store_copies(job, index, step):
+        slot = step % 4
+        return [
+            pltpu.make_async_copy(src, dst, r.store_sem.at[slot, i])
+            for i, (src, dst) in enumerate(results(job, index, slot))
+        ]
+
+    def sib_copy(step):
+        give = pl.ds(pl.multiple_of((1 - core) * CHUNK, CHUNK), CHUNK)
+        return remote(
+            r.made.at[step % 2, give], r.sib.at[step % 4],
+            r.sib_send.at[step % 4], r.sib_recv.at[step % 4], twin,
+        )
+
+    def up_copy(step, dst, sem):
+        slot = step % DEEP
+        return remote(r.acc.at[slot], dst.at[slot], r.up_send.at[slot], sem.at[slot], inner)
+
+    def down_copy(step):
+        return remote(
+            r.total.at[step % 4], r.inner_in.at[step % DEEP],
+            r.down_send.at[step % 4], r.inner_recv.at[step % DEEP], outer,
+        )
+
+    def make(step):
+        slot = step % 2
+
+        def product(job, index):
+            if job < 4:
+                left_buf = (r.hidden_buf, r.two_buf, r.two_buf, r.mixed_buf)[job]
+                right_buf = (r.ffn_buf, r.gate_grad, r.up_grad, r.all_grad)[job]
+                columns = pl.ds(pl.multiple_of(index * PAIR, PAIR), PAIR)
+                across = pl.ds(0, sums[job].shape[1])
+                r.made[slot, :, across] = dot_columns(
+                    left_buf[:, columns], right_buf[:, across]
+                ).astype(bf16)
+                return
+            columns = pl.ds(pl.multiple_of((index // 2) * PAIR, PAIR), PAIR)
+            for which, buf in enumerate((r.hidden_buf, r.ffn_buf)):
+                r.both[...] = dot_columns(r.cols_buf[:, columns], buf[:, pl.ds(0, side)]).astype(bf16)
+                r.made[slot, pl.ds(which * CHUNK, CHUNK), pl.ds(0, side)] = r.both[
+                    pl.ds(pl.multiple_of((index % 2) * CHUNK, CHUNK), CHUNK)
+                ]
+
+        by_job(step, product)
+
+        @pl.when(step >= 4)
+        def _():
+            pl.semaphore_wait(r.sib_credit, 1)
+
+        sib_copy(step).start()
+
+    def send_up(step):
+        @pl.when(step >= DEEP)
+        def _():
+            pl.semaphore_wait(r.up_credit, 1)
+
+        @pl.when(is_mid)
+        def _():
+            up_copy(step, r.inner_in, r.inner_recv).start()
+
+        @pl.when(jnp.logical_not(is_mid))
+        def _():
+            up_copy(step, r.outer_in, r.outer_recv).start()
+
+    def pair_up(step):
+        slot = step % DEEP
+        sib_copy(step).wait()
+
+        @pl.when(step >= DEEP)
+        def _():
+            up_copy(step, r.outer_in, r.outer_recv).wait_send()
+
+        mine = pl.ds(pl.multiple_of(core * CHUNK, CHUNK), CHUNK)
+        r.acc[slot] = add_low(r.made[step % 2, mine], r.sib[step % 4])
+
+        @pl.when(step + 4 < steps)
+        def _():
+            tell(r.sib_credit, twin)
+
+        @pl.when(is_end)
+        def _():
+            send_up(step)
+
+    def from_outer(step):
+        slot = step % DEEP
+        up_copy(step, r.outer_in, r.outer_recv).wait_recv()
+        r.acc[slot] = add_low(r.acc[slot], r.outer_in[slot])
+
+        @pl.when(step + DEEP < steps)
+        def _():
+            tell(r.up_credit, outer)
+
+        send_up(step)
+
+    def sends_done(step):
+        def use(job, index):
+            for copy in pair_copies(job, index, step):
+                copy.wait_send()
+            for copy in store_copies(job, index, step):
+                copy.wait()
+
+        by_job(step, use)
+
+        @pl.when(jnp.logical_not(is_end))
+        def _():
+            down_copy(step).wait_send()
+
+    def from_inner(step):
+        slot = step % DEEP
+        down_copy(step).wait_recv()
+
+        @pl.when(step >= 4)
+        def _():
+            sends_done(step - 4)
+
+        @pl.when(is_mid)
+        def _():
+            r.total[step % 4] = add_low(r.acc[slot], r.inner_in[slot])
+
+            @pl.when(step + DEEP < steps)
+            def _():
+                tell(r.up_credit, inner)
+
+        @pl.when(jnp.logical_not(is_mid))
+        def _():
+            r.total[step % 4] = r.inner_in[slot]
+
+            @pl.when(step + DEEP < steps)
+            def _():
+                tell(r.down_credit, inner)
+
+        @pl.when(jnp.logical_not(is_end))
+        def _():
+            @pl.when(step >= DEEP)
+            def _():
+                pl.semaphore_wait(r.down_credit, 1)
+
+            down_copy(step).start()
+
+        def use(job, index):
+            for copy in pair_copies(job, index, step) + store_copies(job, index, step):
+                copy.start()
+
+        by_job(step, use)
+
+    lag_outer = 3
+    lag_inner = jnp.where(is_end, 8, 6)
+    load_hidden.wait()
+    load_two.wait()
+
+    def at(now, step, use):
+        @pl.when(now == step)
+        def _():
+            use()
+
+    def tick(now, carry):
+        @pl.when(now < steps)
+        def _():
+            make(now)
+
+        @pl.when((now >= 1) & (now - 1 < steps))
+        def _():
+            pair_up(now - 1)
+
+        @pl.when(jnp.logical_not(is_end) & (now >= lag_outer) & (now - lag_outer < steps))
+        def _():
+            from_outer(now - lag_outer)
+
+        @pl.when((now >= lag_inner) & (now - lag_inner < steps))
+        def _():
+            from_inner(now - lag_inner)
+
+        for buf in range(2):
+
+            @pl.when(2 * now + buf < n_a)
+            def _():
+                a_tile(2 * now + buf, buf)
+
+        @pl.when(now == b_at - 1)
+        def _():
+            for copy in b_loads(1):
+                copy.start()
+
+        @pl.when((now >= b_at) & (now < c_at))
+        def _():
+            b_tile(now - b_at)
+
+        at(now, c_at, c_start)
+        at(now, c_at + 1, load_out.start)
+        at(now, c_at + 2, c_pass)
+
+        @pl.when(now == d_at)
+        def _():
+            d_norms()
+            for copy in e_first:
+                copy.start()
+
+        at(now, d_at + 2, lambda: pass_on(e_first, e_on))
+        at(now, f_at, f_mixed)
+
+        @pl.when((now >= g_at) & (now < h_at))
+        def _():
+            g_attention(now - g_at)
+
+        at(now, h_at, h_start)
+        at(now, h_at + 4, lambda: pass_on(h_first, h_on))
+        at(now, i_at, i_start)
+        at(now, i_at + 1, i_norm)
+        at(now, k_at, k_norm)
+        at(now, k_at + 1, k_plane)
+        for index in range(3):
+            at(now, k_at + 2 + index, functools.partial(k_rep, index))
+        return carry
+
+    lax.fori_loop(0, steps + 8, tick, 0)
+
+    def finish(step, carry):
+        sends_done(step)
+        return carry
+
+    lax.fori_loop(steps - 4, steps, finish, 0)
+
+    def finish_up(step, carry):
+        up_copy(step, r.outer_in, r.outer_recv).wait_send()
+        return carry
+
+    lax.fori_loop(steps - DEEP, steps, finish_up, 0)
+
+    def arrived(step, carry):
+        def use(job, index):
+            for copy in pair_copies(job, index, step):
+                copy.wait_recv()
+
+        by_job(step, use)
+        return carry
+
+    lax.fori_loop(0, steps, arrived, 0)
+    for copy in (keep_middle, keep_part, keep_gains):
+        copy.wait()
+
+
+def backward(collective_id, **args):
+    f32, bf16 = jnp.float32, jnp.bfloat16
+    given = types.SimpleNamespace(**args)
+    tokens, width = given.grad_ffn.shape
+    inner_width = given.hidden.shape[1]
+    local = tokens // 4
+    half = local // 2
+    head_cols = given.qkv.shape[1]
+    part = width // 4
+    part_wide = given.gain_one.shape[1]
+    out_rows = given.w_out.shape[0]
+    side = 2 * head_cols
+    slot_width = max(width, inner_width, side)
+    block = min(TILE, tokens)
+    steps = (inner_width + 2 * width + out_rows) // PAIR + part // CHUNK
+    vmem, dma, credit = pltpu.VMEM, pltpu.SemaphoreType.DMA, pltpu.SemaphoreType.REGULAR
+    shape = jax.ShapeDtypeStruct
+    outs = dict(
+        down_sum=shape((inner_width, width), bf16),
+        gate_sum=shape((width, inner_width), bf16),
+        up_sum=shape((width, inner_width), bf16),
+        out_sum=shape((out_rows, width), bf16),
+        query_sum=shape((part, side), bf16),
+        key_sum=shape((part, side // 2), bf16),
+        value_sum=shape((part, side // 2), bf16),
+        grad_middle=shape((local, width), f32),
+        resid_part=shape((4, local, part_wide), bf16),
+        gain_sums=shape((8, width), f32),
+        partial=shape((tokens, width), bf16),
+        grad_qkv=shape((4 * tokens, head_cols), bf16),
+    )
+    scratch = dict(
+        ffn_buf=vmem((tokens, slot_width), bf16),
+        hidden_buf=vmem((tokens, slot_width), bf16),
+        two_buf=vmem((tokens, width), bf16),
+        gate_grad=vmem((tokens, slot_width), bf16),
+        up_grad=vmem((tokens, inner_width), bf16),
+        weights=vmem((4 * TILE, slot_width), bf16),
+        gate_buf=vmem((2, tokens, TILE), bf16),
+        up_buf=vmem((2, tokens, TILE), bf16),
+        wide=vmem((tokens, TILE), f32),
+        stage=vmem((2, tokens, TILE), bf16),
+        c_mine=vmem((4, half, width), bf16),
+        c_landed=vmem((6, half, width), bf16),
+        middle_buf=vmem((local, width), f32),
+        attn_buf=vmem((local, width), f32),
+        cot_buf=vmem((local, width), bf16),
+        qkv_buf=vmem((tokens, head_cols), bf16),
+        mixed_buf=vmem((tokens, out_rows), bf16),
+        cols_buf=vmem((tokens, -(-part // PAIR) * PAIR), bf16),
+        token_buf=vmem((4, local, part_wide), bf16),
+        all_grad=vmem((tokens, width), bf16),
+        mixed_grad=vmem((tokens, out_rows), bf16),
+        probs_buf=vmem((block, tokens), f32),
+        tanh_buf=vmem((block, tokens), f32),
+        score_grad=vmem((block, tokens), f32),
+        dots_grad=vmem((block, tokens), bf16),
+        probs_low=vmem((block, tokens), bf16),
+        kv_grad=vmem((2, tokens, head_cols // 4), f32),
+        head_grad=vmem((tokens, head_cols), bf16),
+        norm_grad=vmem((4, local, part_wide), bf16),
+        gain_own=vmem((8, width), f32),
+        gain_plane=vmem((4, 8, width), f32),
+        gain_mine=vmem((3, 8, width), f32),
+        gain_theirs=vmem((3, 8, width), f32),
+        gain_total=vmem((8, width), f32),
+        made=vmem((2, PAIR, slot_width), bf16),
+        both=vmem((PAIR, side), bf16),
+        sib=vmem((4, CHUNK, slot_width), bf16),
+        acc=vmem((DEEP, CHUNK, slot_width), bf16),
+        outer_in=vmem((DEEP, CHUNK, slot_width), bf16),
+        inner_in=vmem((DEEP, CHUNK, slot_width), bf16),
+        total=vmem((4, CHUNK, slot_width), bf16),
+        load_sem=dma((42,)),
+        stage_sem=dma((2,)),
+        keep_sem=dma((4,)),
+        c_send=dma((6,)),
+        c_recv=dma((6,)),
+        e_send=dma((6,)),
+        e_recv=dma((6,)),
+        h_send=dma((6,)),
+        h_recv=dma((6,)),
+        i_send=dma((3,)),
+        i_recv=dma((3,)),
+        gain_send=dma((6,)),
+        gain_recv=dma((6,)),
+        sib_send=dma((4,)),
+        sib_recv=dma((4,)),
+        up_send=dma((DEEP,)),
+        outer_recv=dma((DEEP,)),
+        inner_recv=dma((DEEP,)),
+        down_send=dma((4,)),
+        pair_send=dma((4, 3)),
+        pair_recv=dma((steps, 3)),
+        store_sem=dma((4, 3)),
+        sib_credit=credit,
+        up_credit=credit,
+        down_credit=credit,
+    )
+    any_space = pl.BlockSpec(memory_space=pl.ANY)
+    small = pl.BlockSpec(memory_space=pltpu.VMEM)
+    in_specs = [
+        small if value.ndim == 2 and value.shape[0] <= 8 else any_space for value in args.values()
+    ]
+    results = pl.pallas_call(
+        functools.partial(
+            backward_kernel,
+            (tokens, local, width, inner_width, head_cols),
+            tuple(args) + tuple(outs) + tuple(scratch),
+        ),
+        out_shape=list(outs.values()),
+        in_specs=in_specs,
+        out_specs=[any_space] * len(outs),
+        scratch_shapes=list(scratch.values()),
+        compiler_params=pltpu.CompilerParams(
+            collective_id=collective_id,
+            has_side_effects=True,
+            vmem_limit_bytes=VMEM_LIMIT,
+        ),
+        cost_estimate=pl.CostEstimate(
+            flops=80 * tokens * width * width, bytes_accessed=400 * 2**20, transcendentals=0
+        ),
+    )(*args.values())
+    return types.SimpleNamespace(**dict(zip(outs, results)))
+
+
+VMEM_LIMIT = 63 * 2**20
+
+
 QUERY_HEADS = 8
 KV = 4
 HEAD_SIZE = 256
@@ -758,6 +1635,56 @@
     grad_out = cotangent.astype(f32)
     grad_ffn, grad_gain_four = norm_back(ffn_out, rms_four, gain_four, grad_out)
     grad_ffn_all = gather_rows(grad_ffn.astype(bf16), 6)
+    if n == 4 and lax.axis_size("rep") == 8:
+        part_wide = -(-part_rows // 128) * 128
+        widen = lambda array: jnp.pad(array, [(0, 0)] * (array.ndim - 1) + [(0, part_wide - part_rows)])
+        normed_cols = lax.dynamic_slice_in_dim(normed_all, me * part_rows, part_rows, axis=1)
+        nothing = jnp.zeros((width,), f32)
+        found = backward(
+            7,
+            grad_ffn=grad_ffn_all,
+            hidden=hidden_b,
+            gate=gate_pre.astype(bf16),
+            up=up_pre.astype(bf16),
+            normed_two=normed_two_all,
+            w_down=w_down,
+            w_gate=w_gate,
+            w_up=w_up,
+            w_out=w_out,
+            middle=middle,
+            attn_out=attn_out,
+            cotangent=cotangent,
+            gains=jnp.stack([gain_two, gain_three] + [nothing] * 6),
+            gain_parts=jnp.stack([grad_gain_four] + [nothing] * 7),
+            gain_one=widen(gain_one.reshape(4, part_rows)),
+            qkv=qkv,
+            mixed=mixed,
+            probs=probs.reshape(q_heads, group_rows, group_rows),
+            tanh=tanh_part.reshape(q_heads, group_rows, group_rows),
+            normed_cols=widen(normed_cols),
+            w_query=w_query,
+            w_key=w_key,
+            w_value=w_value,
+            token_blocks=widen(tokens.reshape(tok_rows, 4, part_rows).transpose(1, 0, 2)),
+        )
+        resid = found.resid_part[:, :, :part_rows].transpose(1, 0, 2).reshape(tok_rows, width)
+        grad_tokens = (found.grad_middle + resid.astype(f32)).astype(bf16)
+        gains = found.gain_sums
+        return (
+            output,
+            grad_tokens,
+            gains[4:, :part_rows].reshape(width),
+            found.query_sum.astype(f32),
+            found.key_sum.astype(f32),
+            found.value_sum.astype(f32),
+            found.out_sum.astype(f32),
+            gains[1],
+            gains[2],
+            found.gate_sum.astype(f32),
+            found.up_sum.astype(f32),
+            found.down_sum.astype(f32),
+            gains[0],
+        )
     down_part = jnp.einsum("tf,td->fd", hidden_b, grad_ffn_all, preferred_element_type=f32)
     grad_hidden = jnp.einsum("td,fd->tf", grad_ffn_all, w_down, preferred_element_type=f32)
     grad_gate, grad_up = geglu_back(grad_hidden)

time: 1090 us -> 810 us (0.74)
  matrix products: 175 us -> 57.1 us
  Pallas kernels: 760 us -> 663 us
  local copies, waits for them, and re-layouts: 63.4 us -> 14.7 us
  between operations: 15.1 us -> 1.32 us
    dot_general x14 -> x0, matrix products: 119 us -> none  [the longest x1 22 us: body(): jnp.einsum('td,fd->tf', grad_ffn_all, w_down, preferred_element_type=f32)]
    pallas_call x4 -> x2, Pallas kernels: 138 us -> 58.7 us  [gather4(): pl.pallas_call(gather_kernel, out_shape=jax.ShapeDtypeStruct((4 * rows, w...]
    pallas_call x3 -> x2, Pallas kernels: 91.4 us -> 62.1 us  [scatter4(): pl.pallas_call(scatter_kernel, out_shape=jax.ShapeDtypeStruct((rows, widt...]
    unnamed x118 -> x53, local copies, waits for them, and re-layouts: 21.1 us -> 1.8 us
    slice x5 -> x2, local copies, waits for them, and re-layouts: 14.2 us -> 0.68 us  [the longest x1 0.67 us: body(): gains[0]]
    convert_element_type x4 -> x3, local copies, waits for them, and re-layouts: 16.2 us -> 4.8 us  [the longest x2 3.65 us: body(): grad_tokens = (found.grad_middle + resid.astype(f32)).astype(bf16)]
    pallas_call x2 -> x1, Pallas kernels: 463 us -> 474 us  [backward(): pl.pallas_call(functools.partial(backward_kernel, (tokens, local, width,...]
    convert_element_type x7 -> x9, other arithmetic: 40.2 us -> 43 us  [the longest x1 15.8 us: body(): found.gate_sum.astype(f32)]
  transfers between devices with their start and end apart: 1 -> 0, of which waited for: 0 -> 0; matrix products, arithmetic and copies ran while one was open for 11% -> 0% of each run, Pallas kernels for 42% -> 0%
where the time goes in v4:
time: 810 us; the launch traced here: 801 us
  Pallas kernels  663 us (82%)
  other arithmetic  65.3 us (8%)
  matrix products  57.1 us (7%)
  local copies, waits for them, and re-layouts  14.7 us (2%)
    pallas_call x1, Pallas kernels, backward(): pl.pallas_call(functools.partial(backward_kernel, (tokens, local, width,...  474 us
    pallas_call x1, Pallas kernels, prologue4(): pl.pallas_call(functools.partial(prologue_kernel, counts), out_shape=(jax...  68.1 us
    pallas_call x2, Pallas kernels, scatter4(): pl.pallas_call(scatter_kernel, out_shape=jax.ShapeDtypeStruct((rows, widt...  62.1 us
    pallas_call x2, Pallas kernels, gather4(): pl.pallas_call(gather_kernel, out_shape=jax.ShapeDtypeStruct((4 * rows, w...  58.7 us
    dot_general x1, matrix products, body(): up_pre = jnp.dot(normed_two_all, w_up, preferred_element_type=f32)  17.1 us
    dot_general x1, matrix products, body(): gate_pre = jnp.dot(normed_two_all, w_gate, preferred_element_type=f32)  16.5 us

profile of v4, /device:TPU:0, one launch (start us, length us, event | category | flops | bytes accessed | tf_op | source)
XLA Modules:
  0.0 801.0 jit_solution(9810162708145551367)
XLA Ops:
  0.6 0.7 convert_element_type.125
  1.3 1.4 fusion.30
  2.8 2.4 fusion.32.x_ref
  5.1 0.7 convert_element_type.127
  5.8 0.6 pad_bitcast_fusion.code_ref
  6.4 68.1 %shard_map.246 = (bf16[768,2304]{1,0:T(8,128)(2,1)}, bf16[4,16,128]{2,1,0:T(8,128)(2,1)}, bf16[2304,1024]{1,0:T(8,128)(2,1)}) custom-call(bf16[192,2304]{1,0:T(8,128)(2,1)} %fusion.32.x_ref, bf16[16,128]{1,0:T(8,128)(2,1)} %pad_bitcast_fusion.code_ref, bf16[576,2048]{1,0:T(8,128)(2,1)} %refs_20_.1, bf16[576,1024]{1,0:T(8,128)(2,1)} %refs_21_.1, ...), custom_call_target="tpu_custom_call" | custom-call | bytes 70778880 | tf_op jit(solution)/shard_map/pallas_call | solution.py:574
  74.5 0.7 copy.59
  75.2 0.1 reshape.295
  75.3 0.1 select_reduce_fusion.1
  75.4 0.1 select_reduce_fusion
  75.5 1.6 fusion.20
  77.1 7.2 convolution_convert_fusion.2.refs_15_
  84.4 0.1 slice.39
  84.5 1.5 fusion.13
  86.0 1.7 fusion.12
  87.7 2.9 fusion.21.refs_17_
  90.6 2.6 fusion.33
  93.3 2.0 convolution_convert_fusion.1.part_ref
  95.3 0.0 copy-start.13
  95.3 32.0 %shard_map.247.refs_10_ = f32[192,2304]{1,0:T(8,128)S(1)} custom-call(bf16[768,2304]{1,0:T(8,128)(2,1)S(1)} %convolution_convert_fusion.1.part_ref), custom_call_target="tpu_custom_call" | custom-call | bytes 35389440 | tf_op jit(solution)/shard_map/pallas_call | solution.py:399
  127.3 0.0 copy-start
  127.3 0.0 copy-start.14
  127.3 0.2 multiply_reduce_fusion.2
  127.6 1.0 copy-done
  128.5 0.5 multiply_reduce_fusion.1
  129.1 1.3 multiply_convert_fusion.x_ref
  130.4 30.1 %shard_map.248.refs_4_ = bf16[768,2304]{1,0:T(8,128)(2,1)} custom-call(bf16[192,2304]{1,0:T(8,128)(2,1)} %multiply_convert_fusion.x_ref), custom_call_target="tpu_custom_call" | custom-call | bytes 35389440 | tf_op jit(solution)/shard_map/pallas_call | solution.py:326
  160.6 0.0 slice-start.3
  160.6 16.5 %fusion.43 = f32[768,2304]{1,0:T(8,128)} fusion(bf16[768,2304]{1,0:T(8,128)(2,1)} %shard_map.248.refs_4_, bf16[2304,2304]{1,0:T(8,128)(2,1)} %refs_6_.1), kind=kOutput, calls=%fused_computation.84 | convolution fusion | flops 8153726976 | bytes 21233664 | tf_op jit(solution)/shard_map/dot_general | solution.py:1627
  177.1 17.1 %fusion.42 = (bf16[768,2304]{1,0:T(8,128)(2,1)}, bf16[768,2304]{1,0:T(8,128)(2,1)}, bf16[768,2304]{1,0:T(8,128)(2,1)}) fusion(f32[768,2304]{1,0:T(8,128)} %fusion.43, bf16[768,2304]{1,0:T(8,128)(2,1)S(1)} %copy-done.5, bf16[2304,2304]{1,0:T(8,128)(2,1)} %refs_7_.1), kind=kOutput, calls=%fused_computation.83 | convolution fusion | flops 8174960640 | bytes 31850496 | tf_op jit(solution)/shard_map/dot_general | solution.py:1628
  194.2 10.1 %convolution_convert_fusion.part_ref = bf16[768,2304]{1,0:T(8,128)(2,1)S(1)} fusion(bf16[768,2304]{1,0:T(8,128)(2,1)} %get-tuple-element.47.refs_1_, bf16[2304,2304]{1,0:T(8,128)(2,1)S(1)} %bitcast.82), kind=kOutput, calls=%fused_computation.10 | convolution fusion | flops 8155496448 | bytes 17694720 | tf_op jit(solution)/shard_map/dot_general | solution.py:1631
  204.3 0.0 copy-start.17
  204.3 30.1 %shard_map.249 = f32[192,2304]{1,0:T(8,128)S(1)} custom-call(bf16[768,2304]{1,0:T(8,128)(2,1)S(1)} %convolution_convert_fusion.part_ref), custom_call_target="tpu_custom_call" | custom-call | bytes 35389440 | tf_op jit(solution)/shard_map/pallas_call | solution.py:399
  234.5 0.2 multiply_reduce_fusion
  234.7 0.7 fusion.29
  235.5 1.9 fusion.26
  237.3 28.6 %shard_map.250.refs_0_ = bf16[768,2304]{1,0:T(8,128)(2,1)} custom-call(bf16[192,2304]{1,0:T(8,128)(2,1)} %get-tuple-element.49.x_ref), custom_call_target="tpu_custom_call" | custom-call | bytes 35389440 | tf_op jit(solution)/shard_map/pallas_call | solution.py:326
  266.0 0.1 pad.26.clone
  266.1 0.1 pad.27.clone
  266.1 0.1 pad.21.clone
  266.2 0.7 maximum_maximum_fusion.1
  266.9 1.2 copy.47.refs_16_
  268.1 5.1 fusion.10.refs_18_
  273.2 1.7 constant_dynamic-slice_fusion
  275.0 1.0 pad.18.refs_19_
  276.0 1.1 reshape.293
  277.1 0.1 copy.58
  277.2 1.1 pad.19.refs_23_
  278.3 0.1 reshape.290
  278.4 0.6 pad.17.refs_14_
  279.0 473.6 %shard_map.251 = (bf16[2304,2304]{1,0:T(8,128)(2,1)}, bf16[2304,2304]{1,0:T(8,128)(2,1)}, bf16[2304,2304]{1,0:T(8,128)(2,1)}, bf16[512,2304]{1,0:T(8,128)(2,1)},...) custom-call(bf16[768,2304]{1,0:T(8,128)(2,1)} %shard_map.250.refs_0_, ...), custom_call_target="tpu_custom_call" | custom-call | flops 326149079040 | bytes 419430400 | tf_op jit(solution)/shard_map/pallas_call | solution.py:1444
  752.6 15.8 %convert_element_type.156 = f32[2304,2304]{1,0:T(8,128)} convert(bf16[2304,2304]{1,0:T(8,128)(2,1)} %get-tuple-element.36) | non-fusion elementwise | flops 5308416 | bytes 31850496 | tf_op jit(solution)/shard_map/convert_element_type | solution.py:1683
  768.5 7.5 convert_element_type.157
  776.1 7.6 convert_element_type.158
  783.6 0.1 convert_bitcast_fusion
  783.8 1.3 copy.43
  785.0 2.4 reshape.296
  787.4 3.2 add_convert_fusion
  790.6 2.8 convert_element_type.152
  793.4 2.5 convert_element_type.155
  796.0 1.7 convert_element_type.153
  797.7 1.7 convert_element_type.154
  799.4 0.7 slice_reduce_fusion
  800.1 0.7 reshape.294
  (64 shorter events, 0.2 us)
Async XLA Ops:
  2.8 72.6 %copy-start.18 = (s32[1,13]{1,0:T(1,128)S(1)}, s32[1,13]{1,0:T(1,128)}, u32[]{:S(2)}) copy-start(s32[1,13]{1,0:T(1,128)} %param.17) | copy-start | bytes 160
  84.4 6.3 copy-start.12
  86.0 4.6 copy-start.1
  90.6 2.6 copy-start.19
  95.3 32.2 %copy-start.13 = (bf16[2304]{0:T(1024)(128)(2,1)S(1)}, bf16[2304]{0:T(1024)(128)(2,1)}, u32[]{:S(2)}) copy-start(bf16[2304]{0:T(1024)(128)(2,1)} %param.23) | copy-start | bytes 13828
  95.3 33.2 %copy-start.3 = (bf16[192,2304]{1,0:T(8,128)(2,1)S(1)}, bf16[192,2304]{1,0:T(8,128)(2,1)}, u32[]{:S(2)}) copy-start(bf16[192,2304]{1,0:T(8,128)(2,1)} %param.15) | copy-start | bytes 2654212
  127.3 1.2 copy-start
  127.3 1.7 copy-start.14
  129.0 106.4 %copy-start.2 = (f32[192,2304]{1,0:T(8,128)}, f32[192,2304]{1,0:T(8,128)S(1)}, u32[]{:S(2)}) copy-start(f32[192,2304]{1,0:T(8,128)S(1)} %get-tuple-element.45.refs_9_) | copy-start | bytes 5308420
  160.5 16.5 %copy-start.5 = (bf16[768,2304]{1,0:T(8,128)(2,1)S(1)}, bf16[768,2304]{1,0:T(8,128)(2,1)}, u32[]{:S(2)}) copy-start(bf16[768,2304]{1,0:T(8,128)(2,1)} %shard_map.248.refs_4_) | copy-start | bytes 10616836
  160.6 33.6 %slice-start.3 = ((s8[10616832]{0:T(1024)(128)(4,1)}), s8[4194304]{0:T(1024)(128)(4,1)S(1)}, s32[]{:S(2)}) async-start(s8[10616832]{0:T(1024)(128)(4,1)} %bitcast.81), calls=%async_computation.3 | async-start | bytes 8388608
  160.6 33.6 %slice-start.4 = ((s8[10616832]{0:T(1024)(128)(4,1)}), s8[4194304]{0:T(1024)(128)(4,1)S(1)}, s32[]{:S(2)}) async-start(s8[10616832]{0:T(1024)(128)(4,1)} %bitcast.81), calls=%async_computation.4 | async-start | bytes 8388608
  177.1 17.1 %slice-start.5 = ((s8[10616832]{0:T(1024)(128)(4,1)}), s8[2228224]{0:T(1024)(128)(4,1)S(1)}, s32[]{:S(2)}) async-start(s8[10616832]{0:T(1024)(128)(4,1)} %bitcast.81), calls=%async_computation.5 | async-start | bytes 4456448
  204.3 30.4 %copy-start.17 = (bf16[2304]{0:T(1024)(128)(2,1)S(1)}, bf16[2304]{0:T(1024)(128)(2,1)}, u32[]{:S(2)}) copy-start(bf16[2304]{0:T(1024)(128)(2,1)} %param.28) | copy-start | bytes 13828
  204.3 30.4 %copy-start.6 = (bf16[192,2304]{1,0:T(8,128)(2,1)S(1)}, bf16[192,2304]{1,0:T(8,128)(2,1)}, u32[]{:S(2)}) copy-start(bf16[192,2304]{1,0:T(8,128)(2,1)} %refs_11_.1) | copy-start | bytes 2654212
  274.9 3.4 copy-start.15
  752.6 15.9 %copy-start.4 = (bf16[2304,2304]{1,0:T(8,128)(2,1)S(1)}, bf16[2304,2304]{1,0:T(8,128)(2,1)}, u32[]{:S(2)}) copy-start(bf16[2304,2304]{1,0:T(8,128)(2,1)} %get-tuple-element.37) | copy-start | bytes 31850500
  752.6 23.4 %slice-start = ((s8[10616832]{0:T(1024)(128)(4,1)}), s8[4194304]{0:T(1024)(128)(4,1)S(1)}, s32[]{:S(2)}) async-start(s8[10616832]{0:T(1024)(128)(4,1)} %bitcast.71), calls=%async_computation | async-start | bytes 8388608
  752.6 23.4 %slice-start.1 = ((s8[10616832]{0:T(1024)(128)(4,1)}), s8[4194304]{0:T(1024)(128)(4,1)S(1)}, s32[]{:S(2)}) async-start(s8[10616832]{0:T(1024)(128)(4,1)} %bitcast.71), calls=%async_computation.1 | async-start | bytes 8388608
  768.5 7.5 slice-start.2
  776.0 7.6 copy-start.11
  787.4 3.2 copy-start.8
  790.6 2.8 copy-start.7
  793.4 2.5 copy-start.10
  796.0 1.7 copy-start.9
  796.0 3.4 copy-start.16

commit v5 on v4

--- a/solution.py
+++ b/solution.py
@@ -1466,6 +1466,324 @@
 VMEM_LIMIT = 63 * 2**20
 
 
+def forward_kernel(names, *refs):
+    r = types.SimpleNamespace(**dict(zip(names, refs)))
+    f32, bf16 = jnp.float32, jnp.bfloat16
+    tokens, inner_width = r.hidden.shape
+    local, width = r.tokens.shape
+    half = local // 2
+    me, x_place, y_place, far_place = plane_places()
+    x_other, y_other = {"shard": x_place}, {"shard": y_place}
+
+    def load(src, dst, index):
+        return pltpu.make_async_copy(src, dst, r.load_sem.at[index])
+
+    def block_rows(owner):
+        return pl.ds(pl.multiple_of(owner * local, 16), local)
+
+    def half_rows(owner, which):
+        return pl.ds(pl.multiple_of(owner * local + which * half, 16), half)
+
+    early = (load(r.mixed, r.mixed_buf, 0), load(r.w_out, r.out_buf, 1))
+    small = (load(r.tokens, r.token_buf, 2), load(r.cotangent, r.cot_buf, 3))
+    big = (
+        load(r.w_gate, r.gate_weight, 4),
+        load(r.w_up, r.up_weight, 5),
+        load(r.w_down, r.down_weight, 6),
+    )
+    for copy in early + small + big:
+        copy.start()
+    greet((x_place, y_place))
+
+    def summing(landed, send_sem, recv_sem):
+        def send(src, index, where):
+            return remote(src, landed.at[index], send_sem.at[index], recv_sem.at[index], where)
+
+        far = (
+            send(r.partial.at[half_rows(far_place, 0)], 0, x_other),
+            send(r.partial.at[half_rows(far_place, 1)], 1, y_other),
+        )
+        near = (
+            send(r.partial.at[half_rows(x_place, 0)], 2, x_other),
+            send(r.partial.at[half_rows(y_place, 1)], 3, y_other),
+        )
+        on = (send(r.passed.at[0], 4, y_other), send(r.passed.at[1], 5, x_other))
+        return far, near, on
+
+    def pass_sums(landed, far, on):
+        for index, owner in enumerate((y_place, x_place)):
+            far[index].wait_recv()
+            r.passed[index] = add_low(r.partial[half_rows(owner, index)], landed[index])
+            on[index].start()
+
+    def gathering(source, target, send_sem, recv_sem):
+        def send(owner, which, index, where, src):
+            return remote(
+                src, target.at[half_rows(owner, which)],
+                send_sem.at[index], recv_sem.at[index], where,
+            )
+
+        starts = [
+            [send(me, which, 2 * which + i, where, source(which)) for i, where in enumerate((x_other, y_other))]
+            for which in range(2)
+        ]
+        on = (
+            send(x_place, 0, 4, y_other, target.at[half_rows(x_place, 0)]),
+            send(y_place, 1, 5, x_other, target.at[half_rows(y_place, 1)]),
+        )
+        return starts, on
+
+    a_far, a_near, a_on = summing(r.a_landed, r.a_send, r.a_recv)
+    c_far, c_near, c_on = summing(r.c_landed, r.c_send, r.c_recv)
+    b_starts, b_on = gathering(
+        lambda which: r.two_buf.at[half_rows(me, which)], r.two_buf, r.b_send, r.b_recv
+    )
+    d_starts, d_on = gathering(
+        lambda which: r.cot_buf.at[pl.ds(which * half, half)], r.grad_ffn, r.d_send, r.d_recv
+    )
+
+    for copy in early:
+        copy.wait()
+
+    def project(owner):
+        rows = block_rows(owner)
+        r.partial[rows] = dot_plain(r.mixed_buf[rows], r.out_buf[...]).astype(bf16)
+
+    project(far_place)
+    for copy in a_far:
+        copy.start()
+    project(x_place)
+    a_near[0].start()
+    project(y_place)
+    a_near[1].start()
+    project(me)
+    pass_sums(r.a_landed, a_far, a_on)
+    for copy in small:
+        copy.wait()
+
+    def sum_rows(landed, which, index):
+        rows = pl.ds(pl.multiple_of(me * local + which * half + index * 16, 16), 16)
+        here = pl.ds(pl.multiple_of(index * 16, 16), 16)
+        return (
+            r.partial[rows].astype(f32)
+            + landed[2 + which, here].astype(f32)
+            + landed[4 + which, here].astype(f32)
+        )
+
+    def middle_rows(which, index, carry):
+        rows = pl.ds(pl.multiple_of(which * half + index * 16, 16), 16)
+        attn = sum_rows(r.a_landed, which, index)
+        r.attn_buf[rows] = attn
+        inv = lax.rsqrt(jnp.mean(attn * attn, axis=-1, keepdims=True) + norm_eps)
+        middle = r.token_buf[rows].astype(f32) + attn * inv * r.gains[0:1]
+        r.middle_buf[rows] = middle
+        inv = lax.rsqrt(jnp.mean(middle * middle, axis=-1, keepdims=True) + norm_eps)
+        r.two_buf[pl.ds(pl.multiple_of(me * local + which * half + index * 16, 16), 16)] = (
+            middle * inv * r.gains[1:2]
+        ).astype(bf16)
+        return carry
+
+    for which in range(2):
+        a_near[which].wait_recv()
+        a_on[which].wait_recv()
+        lax.fori_loop(0, half // 16, functools.partial(middle_rows, which), 0)
+        for copy in b_starts[which]:
+            copy.start()
+    keep = [
+        pltpu.make_async_copy(r.attn_buf, r.attn_out, r.keep_sem.at[0]),
+        pltpu.make_async_copy(r.middle_buf, r.middle, r.keep_sem.at[1]),
+    ]
+    for copy in keep:
+        copy.start()
+    for copy in a_far + a_near + a_on:
+        copy.wait_send()
+
+    def keep_block(owner):
+        rows = block_rows(owner)
+        return [
+            pltpu.make_async_copy(buf, dst.at[rows], r.keep_sem.at[2 + i])
+            for i, (buf, dst) in enumerate(
+                ((r.gate_stage, r.gate), (r.up_stage, r.up), (r.hidden_buf.at[rows], r.hidden))
+            )
+        ]
+
+    def feed(owner, before):
+        rows = block_rows(owner)
+        if before is not None:
+            for copy in keep_block(before):
+                copy.wait()
+
+        def tile(index, carry):
+            columns = pl.ds(pl.multiple_of(index * TILE, TILE), TILE)
+            block = r.two_buf[rows]
+            r.gate_wide[...] = dot_plain(block, r.gate_weight[:, columns])
+            r.up_wide[...] = dot_plain(block, r.up_weight[:, columns])
+
+            def rows_of(index, carry):
+                here = pl.ds(pl.multiple_of(index * 32, 32), 32)
+                gate, up = r.gate_wide[here], r.up_wide[here]
+                r.gate_stage[here, columns] = gate.astype(bf16)
+                r.up_stage[here, columns] = up.astype(bf16)
+                curve = jnp.tanh(ROOT_TWO_PI * (gate + 0.044715 * (gate * gate * gate)))
+                r.hidden_buf[
+                    pl.ds(pl.multiple_of(owner * local + index * 32, 32), 32), columns
+                ] = (0.5 * gate * (1.0 + curve) * up).astype(bf16)
+                return carry
+
+            lax.fori_loop(0, local // 32, rows_of, 0)
+            return carry
+
+        lax.fori_loop(0, inner_width // TILE, tile, 0)
+        for copy in keep_block(owner):
+            copy.start()
+
+    def shrink(owner):
+        rows = block_rows(owner)
+
+        def tile(index, carry):
+            columns = pl.ds(pl.multiple_of(index * TILE, TILE), TILE)
+            r.partial[rows, columns] = dot_plain(
+                r.hidden_buf[rows], r.down_weight[:, columns]
+            ).astype(bf16)
+            return carry
+
+        lax.fori_loop(0, width // TILE, tile, 0)
+
+    big[0].wait()
+    big[1].wait()
+    feed(me, None)
+    big[2].wait()
+    b_starts[0][0].wait_recv()
+    b_on[0].start()
+    b_starts[1][1].wait_recv()
+    b_on[1].start()
+    shrink(me)
+    b_starts[1][0].wait_recv()
+    feed(x_place, me)
+    shrink(x_place)
+    c_near[0].start()
+    b_starts[0][1].wait_recv()
+    feed(y_place, x_place)
+    shrink(y_place)
+    c_near[1].start()
+    for copy in b_on:
+        copy.wait_recv()
+    feed(far_place, y_place)
+    shrink(far_place)
+    for copy in c_far:
+        copy.start()
+    keep_two = pltpu.make_async_copy(r.two_buf, r.normed_two, r.keep_sem.at[5])
+    keep_two.start()
+    r.gain_part[...] = jnp.zeros_like(r.gain_part)
+    pass_sums(r.c_landed, c_far, c_on)
+
+    def last_rows(which, index, carry):
+        rows = pl.ds(pl.multiple_of(which * half + index * 16, 16), 16)
+        ffn = sum_rows(r.c_landed, which, index)
+        inv = lax.rsqrt(jnp.mean(ffn * ffn, axis=-1, keepdims=True) + norm_eps)
+        r.token_buf[rows] = (r.middle_buf[rows] + ffn * inv * r.gains[2:3]).astype(bf16)
+        grad = r.cot_buf[rows].astype(f32)
+        weighted = grad * r.gains[2:3]
+        mean = jnp.mean(weighted * ffn, axis=-1, keepdims=True)
+        r.gain_part[0:1] += jnp.sum(grad * ffn * inv, axis=0, keepdims=True)
+        r.cot_buf[rows] = (inv * weighted - ffn * (inv * inv * inv) * mean).astype(bf16)
+        return carry
+
+    for which in range(2):
+        c_near[which].wait_recv()
+        c_on[which].wait_recv()
+        lax.fori_loop(0, half // 16, functools.partial(last_rows, which), 0)
+        for copy in d_starts[which]:
+            copy.start()
+    keep_own = pltpu.make_async_copy(r.cot_buf, r.grad_ffn.at[block_rows(me)], r.keep_sem.at[6])
+    keep_out = pltpu.make_async_copy(r.token_buf, r.output, r.keep_sem.at[7])
+    keep_own.start()
+    keep_out.start()
+    d_starts[0][0].wait_recv()
+    d_on[0].start()
+    d_starts[1][1].wait_recv()
+    d_on[1].start()
+    d_starts[1][0].wait_recv()
+    d_starts[0][1].wait_recv()
+    for copy in d_on:
+        copy.wait_recv()
+    for copy in b_starts[0] + b_starts[1] + list(b_on + c_far + c_near + c_on) + d_starts[0] + d_starts[1] + list(d_on):
+        copy.wait_send()
+    for copy in keep + keep_block(far_place) + [keep_two, keep_own, keep_out]:
+        copy.wait()
+
+
+def forward(collective_id, **args):
+    f32, bf16 = jnp.float32, jnp.bfloat16
+    given = types.SimpleNamespace(**args)
+    local, width = given.tokens.shape
+    tokens = 4 * local
+    half = local // 2
+    inner_width = given.w_down.shape[0]
+    vmem, dma, shape = pltpu.VMEM, pltpu.SemaphoreType.DMA, jax.ShapeDtypeStruct
+    outs = dict(
+        grad_ffn=shape((tokens, width), bf16),
+        hidden=shape((tokens, inner_width), bf16),
+        gate=shape((tokens, inner_width), bf16),
+        up=shape((tokens, inner_width), bf16),
+        normed_two=shape((tokens, width), bf16),
+        middle=shape((local, width), f32),
+        attn_out=shape((local, width), f32),
+        output=shape((local, width), bf16),
+        gain_part=shape((8, width), f32),
+    )
+    scratch = dict(
+        mixed_buf=vmem(given.mixed.shape, bf16),
+        out_buf=vmem(given.w_out.shape, bf16),
+        token_buf=vmem((local, width), bf16),
+        cot_buf=vmem((local, width), bf16),
+        gate_weight=vmem((width, inner_width), bf16),
+        up_weight=vmem((width, inner_width), bf16),
+        down_weight=vmem((inner_width, width), bf16),
+        partial=vmem((tokens, width), bf16),
+        passed=vmem((2, half, width), bf16),
+        a_landed=vmem((6, half, width), bf16),
+        c_landed=vmem((6, half, width), bf16),
+        attn_buf=vmem((local, width), f32),
+        middle_buf=vmem((local, width), f32),
+        two_buf=vmem((tokens, width), bf16),
+        hidden_buf=vmem((tokens, inner_width), bf16),
+        gate_stage=vmem((local, inner_width), bf16),
+        up_stage=vmem((local, inner_width), bf16),
+        gate_wide=vmem((local, TILE), f32),
+        up_wide=vmem((local, TILE), f32),
+        load_sem=dma((7,)),
+        keep_sem=dma((8,)),
+        a_send=dma((6,)),
+        a_recv=dma((6,)),
+        b_send=dma((6,)),
+        b_recv=dma((6,)),
+        c_send=dma((6,)),
+        c_recv=dma((6,)),
+        d_send=dma((6,)),
+        d_recv=dma((6,)),
+    )
+    any_space = pl.BlockSpec(memory_space=pl.ANY)
+    small = pl.BlockSpec(memory_space=pltpu.VMEM)
+    results = pl.pallas_call(
+        functools.partial(forward_kernel, tuple(args) + tuple(outs) + tuple(scratch)),
+        out_shape=list(outs.values()),
+        in_specs=[
+            small if value.ndim == 2 and value.shape[0] <= 8 else any_space
+            for value in args.values()
+        ],
+        out_specs=[small if value.shape[0] <= 8 else any_space for value in outs.values()],
+        scratch_shapes=list(scratch.values()),
+        compiler_params=pltpu.CompilerParams(
+            collective_id=collective_id, has_side_effects=True, vmem_limit_bytes=VMEM_LIMIT
+        ),
+        cost_estimate=pl.CostEstimate(
+            flops=8 * tokens * width * inner_width, bytes_accessed=100 * 2**20, transcendentals=0
+        ),
+    )(*args.values())
+    return types.SimpleNamespace(**dict(zip(outs, results)))
+
+
 QUERY_HEADS = 8
 KV = 4
 HEAD_SIZE = 256
@@ -1619,6 +1937,68 @@
     probs_b = probs.astype(bf16)
     mixed = jnp.einsum("krts,skh->tkrh", probs_b, values, preferred_element_type=f32)
     mixed = mixed.reshape(group_rows, q_cols).astype(bf16)
+    if n == 4 and lax.axis_size("rep") == 8:
+        part_wide = -(-part_rows // 128) * 128
+        widen = lambda array: jnp.pad(array, [(0, 0)] * (array.ndim - 1) + [(0, part_wide - part_rows)])
+        normed_cols = lax.dynamic_slice_in_dim(normed_all, me * part_rows, part_rows, axis=1)
+        nothing = jnp.zeros((width,), f32)
+        gains = jnp.stack([gain_two, gain_three, gain_four] + [nothing] * 5)
+        ahead = forward(
+            3,
+            mixed=mixed,
+            w_out=w_out,
+            tokens=tokens,
+            cotangent=cotangent,
+            gains=gains,
+            w_gate=w_gate,
+            w_up=w_up,
+            w_down=w_down,
+        )
+        found = backward(
+            7,
+            grad_ffn=ahead.grad_ffn,
+            hidden=ahead.hidden,
+            gate=ahead.gate,
+            up=ahead.up,
+            normed_two=ahead.normed_two,
+            w_down=w_down,
+            w_gate=w_gate,
+            w_up=w_up,
+            w_out=w_out,
+            middle=ahead.middle,
+            attn_out=ahead.attn_out,
+            cotangent=cotangent,
+            gains=gains,
+            gain_parts=ahead.gain_part,
+            gain_one=widen(gain_one.reshape(4, part_rows)),
+            qkv=qkv,
+            mixed=mixed,
+            probs=probs.reshape(q_heads, group_rows, group_rows),
+            tanh=tanh_part.reshape(q_heads, group_rows, group_rows),
+            normed_cols=widen(normed_cols),
+            w_query=w_query,
+            w_key=w_key,
+            w_value=w_value,
+            token_blocks=widen(tokens.reshape(tok_rows, 4, part_rows).transpose(1, 0, 2)),
+        )
+        resid = found.resid_part[:, :, :part_rows].transpose(1, 0, 2).reshape(tok_rows, width)
+        grad_tokens = (found.grad_middle + resid.astype(f32)).astype(bf16)
+        gains = found.gain_sums
+        return (
+            ahead.output,
+            grad_tokens,
+            gains[4:, :part_rows].reshape(width),
+            found.query_sum.astype(f32),
+            found.key_sum.astype(f32),
+            found.value_sum.astype(f32),
+            found.out_sum.astype(f32),
+            gains[1],
+            gains[2],
+            found.gate_sum.astype(f32),
+            found.up_sum.astype(f32),
+            found.down_sum.astype(f32),
+            gains[0],
+        )
     attn_out = scatter_rows(jnp.dot(mixed, w_out, preferred_element_type=f32).astype(bf16), 3)
     post_one, rms_two = normalize(attn_out, gain_two)
     middle = residual + post_one
@@ -1635,56 +2015,6 @@
     grad_out = cotangent.astype(f32)
     grad_ffn, grad_gain_four = norm_back(ffn_out, rms_four, gain_four, grad_out)
     grad_ffn_all = gather_rows(grad_ffn.astype(bf16), 6)
-    if n == 4 and lax.axis_size("rep") == 8:
-        part_wide = -(-part_rows // 128) * 128
-        widen = lambda array: jnp.pad(array, [(0, 0)] * (array.ndim - 1) + [(0, part_wide - part_rows)])
-        normed_cols = lax.dynamic_slice_in_dim(normed_all, me * part_rows, part_rows, axis=1)
-        nothing = jnp.zeros((width,), f32)
-        found = backward(
-            7,
-            grad_ffn=grad_ffn_all,
-            hidden=hidden_b,
-            gate=gate_pre.astype(bf16),
-            up=up_pre.astype(bf16),
-            normed_two=normed_two_all,
-            w_down=w_down,
-            w_gate=w_gate,
-            w_up=w_up,
-            w_out=w_out,
-            middle=middle,
-            attn_out=attn_out,
-            cotangent=cotangent,
-            gains=jnp.stack([gain_two, gain_three] + [nothing] * 6),
-            gain_parts=jnp.stack([grad_gain_four] + [nothing] * 7),
-            gain_one=widen(gain_one.reshape(4, part_rows)),
-            qkv=qkv,
-            mixed=mixed,
-            probs=probs.reshape(q_heads, group_rows, group_rows),
-            tanh=tanh_part.reshape(q_heads, group_rows, group_rows),
-            normed_cols=widen(normed_cols),
-            w_query=w_query,
-            w_key=w_key,
-            w_value=w_value,
-            token_blocks=widen(tokens.reshape(tok_rows, 4, part_rows).transpose(1, 0, 2)),
-        )
-        resid = found.resid_part[:, :, :part_rows].transpose(1, 0, 2).reshape(tok_rows, width)
-        grad_tokens = (found.grad_middle + resid.astype(f32)).astype(bf16)
-        gains = found.gain_sums
-        return (
-            output,
-            grad_tokens,
-            gains[4:, :part_rows].reshape(width),
-            found.query_sum.astype(f32),
-            found.key_sum.astype(f32),
-            found.value_sum.astype(f32),
-            found.out_sum.astype(f32),
-            gains[1],
-            gains[2],
-            found.gate_sum.astype(f32),
-            found.up_sum.astype(f32),
-            found.down_sum.astype(f32),
-            gains[0],
-        )
     down_part = jnp.einsum("tf,td->fd", hidden_b, grad_ffn_all, preferred_element_type=f32)
     grad_hidden = jnp.einsum("td,fd->tf", grad_ffn_all, w_down, preferred_element_type=f32)
     grad_gate, grad_up = geglu_back(grad_hidden)

time: 810 us -> 771 us (0.952); the launches traced: 801 us -> 771 us
  matrix products: 57.1 us -> 11.4 us
  Pallas kernels: 663 us -> 683 us
    dot_general x4 -> x0, matrix products: 45.7 us -> none  [the longest x1 17.1 us: body(): up_pre = jnp.dot(normed_two_all, w_up, preferred_element_type=f32)]
    pallas_call x4 -> x1, Pallas kernels: 121 us -> 142 us  [forward(): pl.pallas_call(functools.partial(forward_kernel, tuple(args) + tuple(outs...]
where the time goes in v5:
time: 771 us
  Pallas kernels  683 us (89%)
  other arithmetic  59.8 us (8%)
  local copies, waits for them, and re-layouts  15.1 us (2%)
  matrix products  11.4 us (1%)
    pallas_call x1, Pallas kernels, backward(): pl.pallas_call(functools.partial(backward_kernel, (tokens, local, width,...  473 us
    pallas_call x1, Pallas kernels, forward(): pl.pallas_call(functools.partial(forward_kernel, tuple(args) + tuple(outs...  142 us
    pallas_call x1, Pallas kernels, prologue4(): pl.pallas_call(functools.partial(prologue_kernel, counts), out_shape=(jax...  68.1 us
    convert_element_type x1, other arithmetic, body(): found.gate_sum.astype(f32)  15.8 us

profile of v5, /device:TPU:0, one launch (start us, length us, event | category | flops | bytes accessed | tf_op | source)
XLA Modules:
  0.0 770.5 jit_solution(17112290006114105170)
XLA Ops:
  0.6 0.0 copy-start.15
  0.7 0.7 convert_element_type.92
  1.4 1.4 fusion.14
  2.8 2.4 fusion.16.x_ref
  5.1 0.7 convert_element_type.94
  5.8 0.6 pad_bitcast_fusion.code_ref
  6.4 68.1 %shard_map.246 = (bf16[768,2304]{1,0:T(8,128)(2,1)}, bf16[4,16,128]{2,1,0:T(8,128)(2,1)}, bf16[2304,1024]{1,0:T(8,128)(2,1)}) custom-call(bf16[192,2304]{1,0:T(8,128)(2,1)} %fusion.16.x_ref, bf16[16,128]{1,0:T(8,128)(2,1)} %pad_bitcast_fusion.code_ref, bf16[576,2048]{1,0:T(8,128)(2,1)} %refs_20_.1, bf16[576,1024]{1,0:T(8,128)(2,1)} %refs_21_.1, ...), custom_call_target="tpu_custom_call" | custom-call | bytes 70778880 | tf_op jit(solution)/shard_map/pallas_call | solution.py:574
  74.5 0.7 copy.59
  75.2 0.1 reshape.258
  75.3 0.0 copy-done.15
  75.3 0.1 select_reduce_fusion.1
  75.4 0.1 select_reduce_fusion
  75.5 1.6 fusion.11
  77.1 7.2 convolution_convert_fusion.refs_15_
  84.4 0.0 copy-start.9
  84.4 0.1 slice.39
  84.5 1.5 fusion.4
  86.0 1.7 fusion.3
  87.7 2.9 fusion.12.refs_17_
  90.6 0.0 copy-done.9
  90.6 0.0 copy-done
  90.7 0.0 copy-start.14
  90.7 2.6 fusion.17
  93.3 1.2 copy.47.refs_0_.refs_16_
  94.5 0.0 copy-done.12
  94.5 0.0 copy-done.13
  94.5 0.0 copy-done.14
  94.5 0.7 stack.31.refs_4_.refs_12_
  95.2 141.7 %shard_map.247 = (bf16[768,2304]{1,0:T(8,128)(2,1)}, bf16[768,2304]{1,0:T(8,128)(2,1)}, bf16[768,2304]{1,0:T(8,128)(2,1)}, bf16[768,2304]{1,0:T(8,128)(2,1)}, bf...) custom-call(bf16[768,512]{1,0:T(8,128)(2,1)} %copy.47.refs_0_.refs_1, ...), custom_call_target="tpu_custom_call" | custom-call | flops 32614907904 | bytes 104857600 | tf_op jit(solution)/shard_map/pallas_call | solution.py:1768
  237.0 0.0 copy-start.2
  237.0 5.2 fusion.1.refs_18_
  242.2 1.7 constant_dynamic-slice_fusion
  243.9 1.0 pad.18.refs_19_
  245.0 0.0 copy-done.2
  245.0 1.1 reshape.256
  246.1 0.1 copy.58
  246.2 1.0 pad.19.refs_23_
  247.3 0.0 copy-done.10
  247.3 0.1 reshape.253
  247.3 0.6 pad.17.refs_14_
  248.0 473.5 %shard_map.248 = (bf16[2304,2304]{1,0:T(8,128)(2,1)}, bf16[2304,2304]{1,0:T(8,128)(2,1)}, bf16[2304,2304]{1,0:T(8,128)(2,1)}, bf16[512,2304]{1,0:T(8,128)(2,1)},...) custom-call(bf16[768,2304]{1,0:T(8,128)(2,1)} %get-tuple-element.39., ...), custom_call_target="tpu_custom_call" | custom-call | flops 326149079040 | bytes 419430400 | tf_op jit(solution)/shard_map/pallas_call | solution.py:1444
  721.4 0.0 copy-start.1
  721.5 0.0 slice-start
  721.5 0.0 slice-start.1
  721.5 15.8 %convert_element_type.111 = f32[2304,2304]{1,0:T(8,128)} convert(bf16[2304,2304]{1,0:T(8,128)(2,1)} %get-tuple-element.54) | non-fusion elementwise | flops 5308416 | bytes 31850496 | tf_op jit(solution)/shard_map/convert_element_type | solution.py:1997
  737.3 0.0 copy-done.1
  737.3 7.5 convert_element_type.112
  744.9 0.0 slice-done
  744.9 0.0 slice-done.1
  744.9 0.0 slice-done.2
  744.9 0.0 copy-start.7
  744.9 7.6 convert_element_type.113
  752.5 0.1 convert_bitcast_fusion
  752.6 1.3 copy.43
  753.9 2.4 reshape.262
  756.3 3.2 add_convert_fusion
  759.5 2.8 convert_element_type.107
  762.3 0.0 copy-done.3
  762.3 2.5 convert_element_type.110
  764.8 1.7 convert_element_type.108
  766.5 1.7 convert_element_type.109
  768.2 0.7 slice_reduce_fusion
  768.9 0.7 reshape.257
  769.6 0.9 copy.61
  (27 shorter events, 0.1 us)
Async XLA Ops:
  0.6 74.7 %copy-start.15 = (s32[1,13]{1,0:T(1,128)S(1)}, s32[1,13]{1,0:T(1,128)}, u32[]{:S(2)}) copy-start(s32[1,13]{1,0:T(1,128)} %param.17) | copy-start | bytes 160
  84.4 6.3 copy-start.9
  86.0 4.6 copy-start
  90.6 3.8 copy-start.12
  90.6 3.8 copy-start.13
  90.7 3.8 copy-start.14
  237.0 8.0 %copy-start.2 = (bf16[192,2304]{1,0:T(8,128)(2,1)S(1)}, bf16[192,2304]{1,0:T(8,128)(2,1)}, u32[]{:S(2)}) copy-start(bf16[192,2304]{1,0:T(8,128)(2,1)} %refs_2_.1) | copy-start | bytes 2654212
  242.2 5.1 copy-start.10
  721.4 15.9 %copy-start.1 = (bf16[2304,2304]{1,0:T(8,128)(2,1)S(1)}, bf16[2304,2304]{1,0:T(8,128)(2,1)}, u32[]{:S(2)}) copy-start(bf16[2304,2304]{1,0:T(8,128)(2,1)} %get-tuple-element.55) | copy-start | bytes 31850500
  721.5 23.4 %slice-start = ((s8[10616832]{0:T(1024)(128)(4,1)}), s8[4194304]{0:T(1024)(128)(4,1)S(1)}, s32[]{:S(2)}) async-start(s8[10616832]{0:T(1024)(128)(4,1)} %bitcast.62), calls=%async_computation | async-start | bytes 8388608
  721.5 23.4 %slice-start.1 = ((s8[10616832]{0:T(1024)(128)(4,1)}), s8[4194304]{0:T(1024)(128)(4,1)S(1)}, s32[]{:S(2)}) async-start(s8[10616832]{0:T(1024)(128)(4,1)} %bitcast.62), calls=%async_computation.1 | async-start | bytes 8388608
  737.3 7.5 slice-start.2
  744.9 7.6 copy-start.7
  756.3 3.2 copy-start.4
  756.3 6.0 copy-start.3
  762.3 2.5 copy-start.6
  762.3 4.2 copy-start.5
  764.8 3.4 copy-start.11
  764.8 4.8 copy-start.8

commit v6 on v5

--- a/solution.py
+++ b/solution.py
@@ -277,320 +277,6 @@
     pl.semaphore_wait(barrier, len(places))
 
 
-def gather_kernel(x_ref, out_ref, send_sem, recv_sem, local_sem):
-    me, x_other, y_other, far = plane_places()
-    rows = x_ref.shape[0]
-    half = rows // 2
-
-    def part(block, which):
-        return out_ref.at[pl.ds(pl.multiple_of(block * rows + which * half, 16), half)]
-
-    def own(which):
-        return x_ref.at[pl.ds(which * half, half)]
-
-    def send(src, dst, index, where):
-        return remote(src, dst, send_sem.at[index], recv_sem.at[index], {"shard": where})
-
-    greet((x_other, y_other))
-    local = pltpu.make_async_copy(
-        x_ref, out_ref.at[pl.ds(pl.multiple_of(me * rows, 16), rows)], local_sem
-    )
-    first = (
-        send(own(0), part(me, 0), 0, x_other),
-        send(own(1), part(me, 1), 1, y_other),
-        send(own(1), part(me, 1), 2, x_other),
-        send(own(0), part(me, 0), 3, y_other),
-    )
-    for copy in first:
-        copy.start()
-    local.start()
-    first[0].wait_recv()
-    on_y = send(part(x_other, 0), part(x_other, 0), 4, y_other)
-    on_y.start()
-    first[1].wait_recv()
-    on_x = send(part(y_other, 1), part(y_other, 1), 5, x_other)
-    on_x.start()
-    first[2].wait_recv()
-    first[3].wait_recv()
-    on_y.wait_recv()
-    on_x.wait_recv()
-    for copy in first + (on_y, on_x):
-        copy.wait_send()
-    local.wait()
-
-
-def gather4(block, collective_id):
-    rows, width = block.shape
-    sems = pltpu.SemaphoreType.DMA((6,))
-    any_space = pl.BlockSpec(memory_space=pl.ANY)
-    return pl.pallas_call(
-        gather_kernel,
-        out_shape=jax.ShapeDtypeStruct((4 * rows, width), block.dtype),
-        in_specs=[any_space],
-        out_specs=any_space,
-        scratch_shapes=[sems, sems, pltpu.SemaphoreType.DMA],
-        compiler_params=pltpu.CompilerParams(collective_id=collective_id, has_side_effects=True),
-        cost_estimate=pl.CostEstimate(
-            flops=0, bytes_accessed=40 * rows * width * 2, transcendentals=0
-        ),
-    )(block)
-
-
-def scatter_kernel(part_ref, out_ref, *scratch):
-    landed, mine, passed = scratch[:3]
-    send_sem, recv_sem, load_sem = scratch[3:]
-    me, x_other, y_other, far = plane_places()
-    rows = out_ref.shape[0]
-    half = rows // 2
-
-    def part(block, which):
-        return part_ref.at[pl.ds(pl.multiple_of(block * rows + which * half, 16), half)]
-
-    def send(src, index, where):
-        return remote(
-            src, landed.at[index], send_sem.at[index], recv_sem.at[index], {"shard": where}
-        )
-
-    def load(src, index):
-        return pltpu.make_async_copy(src, mine.at[index], load_sem.at[index])
-
-    loads = (
-        load(part(y_other, 0), 0),
-        load(part(x_other, 1), 1),
-        load(part(me, 0), 2),
-        load(part(me, 1), 3),
-    )
-    for copy in loads:
-        copy.start()
-    greet((x_other, y_other))
-    first = (
-        send(part(far, 0), 0, x_other),
-        send(part(far, 1), 1, y_other),
-        send(part(x_other, 0), 2, x_other),
-        send(part(y_other, 1), 3, y_other),
-    )
-    for copy in first:
-        copy.start()
-    for copy in loads:
-        copy.wait()
-    first[0].wait_recv()
-    passed[0] = add_low(landed[0], mine[0])
-    on_y = send(passed.at[0], 4, y_other)
-    on_y.start()
-    first[1].wait_recv()
-    passed[1] = add_low(landed[1], mine[1])
-    on_x = send(passed.at[1], 5, x_other)
-    on_x.start()
-    first[2].wait_recv()
-    mine[2] = add_low(landed[2], mine[2])
-    first[3].wait_recv()
-    mine[3] = add_low(landed[3], mine[3])
-    on_y.wait_recv()
-    out_ref[pl.ds(0, half)] = mine[2].astype(jnp.float32) + landed[4].astype(jnp.float32)
-    on_x.wait_recv()
-    out_ref[pl.ds(half, half)] = mine[3].astype(jnp.float32) + landed[5].astype(jnp.float32)
-    for copy in first + (on_y, on_x):
-        copy.wait_send()
-
-
-def scatter4(partial, collective_id):
-    rows, width = partial.shape[0] // 4, partial.shape[1]
-    half = rows // 2
-    return pl.pallas_call(
-        scatter_kernel,
-        out_shape=jax.ShapeDtypeStruct((rows, width), jnp.float32),
-        in_specs=[pl.BlockSpec(memory_space=pl.ANY)],
-        out_specs=pl.BlockSpec(memory_space=pltpu.VMEM),
-        scratch_shapes=[
-            pltpu.VMEM((6, half, width), partial.dtype),
-            pltpu.VMEM((4, half, width), partial.dtype),
-            pltpu.VMEM((2, half, width), partial.dtype),
-            pltpu.SemaphoreType.DMA((6,)),
-            pltpu.SemaphoreType.DMA((6,)),
-            pltpu.SemaphoreType.DMA((4,)),
-        ],
-        compiler_params=pltpu.CompilerParams(
-            collective_id=collective_id, has_side_effects=True, vmem_limit_bytes=32 * 1024 * 1024
-        ),
-        cost_estimate=pl.CostEstimate(
-            flops=0, bytes_accessed=40 * rows * width * 2, transcendentals=0
-        ),
-    )(partial)
-
-
-def exchange_kernel(x_ref, out_ref, send_sem, recv_sem, local_sem):
-    me = lax.axis_index("shard")
-    others = [(me + step) % 4 for step in (1, 2, 3)]
-    greet(others)
-    local = pltpu.make_async_copy(x_ref.at[me], out_ref.at[me], local_sem)
-    local.start()
-    copies = [
-        remote(x_ref.at[place], out_ref.at[me], send_sem.at[i], recv_sem.at[i], {"shard": place})
-        for i, place in enumerate(others)
-    ]
-    for copy in copies:
-        copy.start()
-    for copy in copies:
-        copy.wait()
-    local.wait()
-
-
-def exchange4(blocks, collective_id):
-    any_space = pl.BlockSpec(memory_space=pl.ANY)
-    sems = pltpu.SemaphoreType.DMA((3,))
-    return pl.pallas_call(
-        exchange_kernel,
-        out_shape=jax.ShapeDtypeStruct(blocks.shape, blocks.dtype),
-        in_specs=[any_space],
-        out_specs=any_space,
-        scratch_shapes=[sems, sems, pltpu.SemaphoreType.DMA],
-        compiler_params=pltpu.CompilerParams(collective_id=collective_id, has_side_effects=True),
-        cost_estimate=pl.CostEstimate(
-            flops=0, bytes_accessed=10 * blocks.size * 2, transcendentals=0
-        ),
-    )(blocks)
-
-
-def prologue_kernel(counts, x_ref, code_ref, query_ref, key_ref, value_ref, out_ref, codes_ref,
-                    heads_ref, send_sem, recv_sem, local_sem, code_send, code_recv,
-                    head_send, head_recv, twin_send, twin_recv, head_local):
-    me, x_other, y_other, far = plane_places()
-    place = lax.axis_index("rep")
-    core = place % 2
-    twin = {"rep": place + 1 - 2 * core}
-    others = (x_other, y_other, far)
-    rows = x_ref.shape[0]
-    half = rows // 2
-    depth = query_ref.shape[0]
-    part_depth = depth // 2
-    weights = (query_ref, key_ref, value_ref)
-    starts = (0, counts[0], counts[0] + counts[1])
-
-    barrier = pltpu.get_barrier_semaphore()
-    for other in others:
-        pl.semaphore_signal(
-            barrier, inc=1, device_id={"shard": other}, device_id_type=pl.DeviceIdType.MESH
-        )
-    pl.semaphore_signal(barrier, inc=1, device_id=twin, device_id_type=pl.DeviceIdType.MESH)
-    pl.semaphore_wait(barrier, 4)
-
-    def my_rows(owner):
-        return pl.ds(pl.multiple_of(owner * depth + core * part_depth, 16), part_depth)
-
-    def head_copy(index, kind, other):
-        columns = pl.ds(pl.multiple_of(other * counts[kind], 128), counts[kind])
-        return remote(
-            weights[kind].at[pl.ds(pl.multiple_of(core * part_depth, 16), part_depth), columns],
-            heads_ref.at[my_rows(me), pl.ds(starts[kind], counts[kind])],
-            head_send.at[index, kind],
-            head_recv.at[index, kind],
-            {"shard": other},
-        )
-
-    def part(block, which):
-        return out_ref.at[pl.ds(pl.multiple_of(block * rows + which * half, 16), half)]
-
-    def own(which):
-        return x_ref.at[pl.ds(which * half, half)]
-
-    def send(src, dst, index, where):
-        return remote(src, dst, send_sem.at[index], recv_sem.at[index], {"shard": where})
-
-    head_copies = [
-        [head_copy(index, kind, other) for kind in range(3)] for index, other in enumerate(others)
-    ]
-    for index in (2, 0, 1):
-        for copy in head_copies[index]:
-            copy.start()
-    code_copies = [
-        remote(
-            code_ref, codes_ref.at[me], code_send.at[index], code_recv.at[index], {"shard": other}
-        )
-        for index, other in enumerate(others)
-    ]
-    for copy in code_copies:
-        copy.start()
-    first = (
-        send(own(0), part(me, 0), 0, x_other),
-        send(own(1), part(me, 1), 1, y_other),
-        send(own(1), part(me, 1), 2, x_other),
-        send(own(0), part(me, 0), 3, y_other),
-    )
-    for copy in first:
-        copy.start()
-    locals_ = [
-        pltpu.make_async_copy(
-            x_ref, out_ref.at[pl.ds(pl.multiple_of(me * rows, 16), rows)], local_sem.at[0]
-        ),
-        pltpu.make_async_copy(code_ref, codes_ref.at[me], local_sem.at[1]),
-    ]
-    for kind in range(3):
-        columns = pl.ds(pl.multiple_of(me * counts[kind], 128), counts[kind])
-        locals_.append(
-            pltpu.make_async_copy(
-                weights[kind].at[:, columns],
-                heads_ref.at[
-                    pl.ds(pl.multiple_of(me * depth, 16), depth), pl.ds(starts[kind], counts[kind])
-                ],
-                head_local.at[kind],
-            )
-        )
-    for copy in locals_:
-        copy.start()
-    twins = []
-    for index in (0, 1, 2):
-        for copy in head_copies[index]:
-            copy.wait_recv()
-        block = heads_ref.at[my_rows(others[index])]
-        twins.append(remote(block, block, twin_send.at[index], twin_recv.at[index], twin))
-        twins[-1].start()
-    first[0].wait_recv()
-    on_y = send(part(x_other, 0), part(x_other, 0), 4, y_other)
-    on_y.start()
-    first[1].wait_recv()
-    on_x = send(part(y_other, 1), part(y_other, 1), 5, x_other)
-    on_x.start()
-    first[2].wait_recv()
-    first[3].wait_recv()
-    for copy in code_copies + twins:
-        copy.wait_recv()
-    on_y.wait_recv()
-    on_x.wait_recv()
-    for copy in list(first) + [on_y, on_x] + code_copies + twins:
-        copy.wait_send()
-    for group in head_copies:
-        for copy in group:
-            copy.wait_send()
-    for copy in locals_:
-        copy.wait()
-
-
-def prologue4(block, codes, w_query, w_key, w_value, collective_id):
-    rows, width = block.shape
-    counts = tuple(weight.shape[1] // 4 for weight in (w_query, w_key, w_value))
-    depth = w_query.shape[0]
-    any_space = pl.BlockSpec(memory_space=pl.ANY)
-    dma = pltpu.SemaphoreType.DMA
-    return pl.pallas_call(
-        functools.partial(prologue_kernel, counts),
-        out_shape=(
-            jax.ShapeDtypeStruct((4 * rows, width), block.dtype),
-            jax.ShapeDtypeStruct((4,) + codes.shape, codes.dtype),
-            jax.ShapeDtypeStruct((4 * depth, sum(counts)), w_query.dtype),
-        ),
-        in_specs=[any_space] * 5,
-        out_specs=[any_space] * 3,
-        scratch_shapes=[
-            dma((6,)), dma((6,)), dma((2,)), dma((3,)), dma((3,)),
-            dma((3, 3)), dma((3, 3)), dma((3,)), dma((3,)), dma((3,)),
-        ],
-        compiler_params=pltpu.CompilerParams(collective_id=collective_id, has_side_effects=True),
-        cost_estimate=pl.CostEstimate(
-            flops=0, bytes_accessed=80 * rows * width * 2, transcendentals=0
-        ),
-    )(block, codes, w_query, w_key, w_value)
-
-
 TILE = 256
 PAIR = 2 * CHUNK
 DEEP = 8
@@ -618,7 +304,7 @@
     k_cols = head_cols // 4
     heads = q_cols // HEAD_SIZE
     part = width // 4
-    part_wide = r.gain_one.shape[1]
+    part_wide = r.normed_cols.shape[1]
     side = 2 * head_cols
     n_a = inner_width // TILE
     n_b = width // TILE
@@ -672,7 +358,7 @@
         load(r.qkv, r.qkv_buf, 6),
         load(r.mixed, r.mixed_buf, 7),
         load(r.normed_cols, r.cols_buf, 8),
-        load(r.token_blocks, r.token_buf, 9),
+        load(r.tokens, r.token_buf, 9),
     )
 
     def weight_tile(index):
@@ -734,7 +420,7 @@
         columns = pl.ds(pl.multiple_of(tile * TILE, TILE), TILE)
 
         def rows_of(index, carry):
-            rows = pl.ds(pl.multiple_of(index * 32, 32), 32)
+            rows = pl.ds(pl.multiple_of(index * 128, 128), 128)
             grad = r.wide[rows]
             gate = r.gate_buf[buf, rows].astype(f32)
             up = r.up_buf[buf, rows].astype(f32)
@@ -745,7 +431,7 @@
             r.up_grad[rows, columns] = (grad * (0.5 * gate * (1.0 + curve))).astype(bf16)
             return carry
 
-        lax.fori_loop(0, tokens // 32, rows_of, 0)
+        lax.fori_loop(0, tokens // 128, rows_of, 0)
 
         @pl.when(tile + 2 < n_a)
         def _():
@@ -847,9 +533,6 @@
             lax.fori_loop(0, half // 16, functools.partial(rows_of, which), 0)
         for copy in c_on:
             copy.wait_send()
-        keep_middle.start()
-
-    keep_middle = pltpu.make_async_copy(r.middle_buf, r.grad_middle, r.keep_sem.at[0])
 
     def gather_copies(rows, source, target, send_sem, recv_sem):
         def send(owner, which, index, where, src):
@@ -917,7 +600,7 @@
         r.score_grad[...] = dot_rows(grad_out, values)
 
         def rows_of(index, carry):
-            here = pl.ds(pl.multiple_of(index * 16, 16), 16)
+            here = pl.ds(pl.multiple_of(index * 64, 64), 64)
             probs = r.probs_buf[here]
             grad = r.score_grad[here]
             curve = r.tanh_buf[here]
@@ -927,7 +610,7 @@
             r.probs_low[here] = probs.astype(bf16)
             return carry
 
-        lax.fori_loop(0, block // 16, rows_of, 0)
+        lax.fori_loop(0, block // 64, rows_of, 0)
 
         @pl.when(item + 1 < heads * n_blocks)
         def _():
@@ -1011,25 +694,17 @@
 
         def rows_of(index, carry):
             rows = pl.ds(pl.multiple_of(index * 16, 16), 16)
-            squares = jnp.zeros((16, 1), f32)
-            mean = jnp.zeros((16, 1), f32)
-            for owner in range(4):
-                tokens_in = r.token_buf[owner, rows].astype(f32)
-                weighted = r.norm_grad[owner, rows].astype(f32) * r.gain_one[owner : owner + 1]
-                squares += jnp.sum(tokens_in * tokens_in, axis=-1, keepdims=True)
-                mean += jnp.sum(weighted * tokens_in, axis=-1, keepdims=True)
-            inv = lax.rsqrt(squares * (1.0 / width) + norm_eps)
-            mean = mean * (1.0 / width)
-            for owner in range(4):
-                tokens_in = r.token_buf[owner, rows].astype(f32)
-                grad = r.norm_grad[owner, rows].astype(f32)
-                r.gain_own[4 + owner : 5 + owner, 0:part_wide] += jnp.sum(
-                    grad * tokens_in * inv, axis=0, keepdims=True
-                )
-                weighted = grad * r.gain_one[owner : owner + 1]
-                r.norm_grad[owner, rows] = (
-                    inv * weighted - tokens_in * (inv * inv * inv) * mean
-                ).astype(bf16)
+            grad = jnp.concatenate(
+                [r.norm_grad[owner, rows].astype(f32)[:, :part] for owner in range(4)], axis=1
+            )
+            values = r.token_buf[rows].astype(f32)
+            inv = lax.rsqrt(jnp.mean(values * values, axis=-1, keepdims=True) + norm_eps)
+            weighted = grad * r.gains[3:4]
+            mean = jnp.mean(weighted * values, axis=-1, keepdims=True)
+            r.gain_own[3:4] += jnp.sum(grad * values * inv, axis=0, keepdims=True)
+            r.cot_buf[rows] = (
+                r.middle_buf[rows] + inv * weighted - values * (inv * inv * inv) * mean
+            ).astype(bf16)
             return carry
 
         lax.fori_loop(0, local // 16, rows_of, 0)
@@ -1037,7 +712,7 @@
         for copy in gain_plane:
             copy.start()
 
-    keep_part = pltpu.make_async_copy(r.norm_grad, r.resid_part, r.keep_sem.at[2])
+    keep_part = pltpu.make_async_copy(r.cot_buf, r.grad_tokens, r.keep_sem.at[0])
     gain_plane = [
         remote(r.gain_own, r.gain_plane.at[me], r.gain_send.at[i], r.gain_recv.at[i], where)
         for i, where in enumerate(plane)
@@ -1333,7 +1008,7 @@
         return carry
 
     lax.fori_loop(0, steps, arrived, 0)
-    for copy in (keep_middle, keep_part, keep_gains):
+    for copy in (keep_part, keep_gains):
         copy.wait()
 
 
@@ -1346,7 +1021,7 @@
     half = local // 2
     head_cols = given.qkv.shape[1]
     part = width // 4
-    part_wide = given.gain_one.shape[1]
+    part_wide = given.normed_cols.shape[1]
     out_rows = given.w_out.shape[0]
     side = 2 * head_cols
     slot_width = max(width, inner_width, side)
@@ -1362,8 +1037,7 @@
         query_sum=shape((part, side), bf16),
         key_sum=shape((part, side // 2), bf16),
         value_sum=shape((part, side // 2), bf16),
-        grad_middle=shape((local, width), f32),
-        resid_part=shape((4, local, part_wide), bf16),
+        grad_tokens=shape((local, width), bf16),
         gain_sums=shape((8, width), f32),
         partial=shape((tokens, width), bf16),
         grad_qkv=shape((4 * tokens, head_cols), bf16),
@@ -1387,7 +1061,7 @@
         qkv_buf=vmem((tokens, head_cols), bf16),
         mixed_buf=vmem((tokens, out_rows), bf16),
         cols_buf=vmem((tokens, -(-part // PAIR) * PAIR), bf16),
-        token_buf=vmem((4, local, part_wide), bf16),
+        token_buf=vmem((local, width), bf16),
         all_grad=vmem((tokens, width), bf16),
         mixed_grad=vmem((tokens, out_rows), bf16),
         probs_buf=vmem((block, tokens), f32),
@@ -1562,8 +1236,8 @@
         copy.wait()
 
     def sum_rows(landed, which, index):
-        rows = pl.ds(pl.multiple_of(me * local + which * half + index * 16, 16), 16)
-        here = pl.ds(pl.multiple_of(index * 16, 16), 16)
+        rows = pl.ds(pl.multiple_of(me * local + which * half + index * 32, 16), 32)
+        here = pl.ds(pl.multiple_of(index * 32, 16), 32)
         return (
             r.partial[rows].astype(f32)
             + landed[2 + which, here].astype(f32)
@@ -1571,14 +1245,14 @@
         )
 
     def middle_rows(which, index, carry):
-        rows = pl.ds(pl.multiple_of(which * half + index * 16, 16), 16)
+        rows = pl.ds(pl.multiple_of(which * half + index * 32, 16), 32)
         attn = sum_rows(r.a_landed, which, index)
         r.attn_buf[rows] = attn
         inv = lax.rsqrt(jnp.mean(attn * attn, axis=-1, keepdims=True) + norm_eps)
         middle = r.token_buf[rows].astype(f32) + attn * inv * r.gains[0:1]
         r.middle_buf[rows] = middle
         inv = lax.rsqrt(jnp.mean(middle * middle, axis=-1, keepdims=True) + norm_eps)
-        r.two_buf[pl.ds(pl.multiple_of(me * local + which * half + index * 16, 16), 16)] = (
+        r.two_buf[pl.ds(pl.multiple_of(me * local + which * half + index * 32, 16), 32)] = (
             middle * inv * r.gains[1:2]
         ).astype(bf16)
         return carry
@@ -1586,7 +1260,7 @@
     for which in range(2):
         a_near[which].wait_recv()
         a_on[which].wait_recv()
-        lax.fori_loop(0, half // 16, functools.partial(middle_rows, which), 0)
+        lax.fori_loop(0, half // 32, functools.partial(middle_rows, which), 0)
         for copy in b_starts[which]:
             copy.start()
     keep = [
@@ -1620,17 +1294,17 @@
             r.up_wide[...] = dot_plain(block, r.up_weight[:, columns])
 
             def rows_of(index, carry):
-                here = pl.ds(pl.multiple_of(index * 32, 32), 32)
+                here = pl.ds(pl.multiple_of(index * half, 16), half)
                 gate, up = r.gate_wide[here], r.up_wide[here]
                 r.gate_stage[here, columns] = gate.astype(bf16)
                 r.up_stage[here, columns] = up.astype(bf16)
                 curve = jnp.tanh(ROOT_TWO_PI * (gate + 0.044715 * (gate * gate * gate)))
                 r.hidden_buf[
-                    pl.ds(pl.multiple_of(owner * local + index * 32, 32), 32), columns
+                    pl.ds(pl.multiple_of(owner * local + index * half, 16), half), columns
                 ] = (0.5 * gate * (1.0 + curve) * up).astype(bf16)
                 return carry
 
-            lax.fori_loop(0, local // 32, rows_of, 0)
+            lax.fori_loop(0, 2, rows_of, 0)
             return carry
 
         lax.fori_loop(0, inner_width // TILE, tile, 0)
@@ -1678,7 +1352,7 @@
     pass_sums(r.c_landed, c_far, c_on)
 
     def last_rows(which, index, carry):
-        rows = pl.ds(pl.multiple_of(which * half + index * 16, 16), 16)
+        rows = pl.ds(pl.multiple_of(which * half + index * 32, 16), 32)
         ffn = sum_rows(r.c_landed, which, index)
         inv = lax.rsqrt(jnp.mean(ffn * ffn, axis=-1, keepdims=True) + norm_eps)
         r.token_buf[rows] = (r.middle_buf[rows] + ffn * inv * r.gains[2:3]).astype(bf16)
@@ -1692,7 +1366,7 @@
     for which in range(2):
         c_near[which].wait_recv()
         c_on[which].wait_recv()
-        lax.fori_loop(0, half // 16, functools.partial(last_rows, which), 0)
+        lax.fori_loop(0, half // 32, functools.partial(last_rows, which), 0)
         for copy in d_starts[which]:
             copy.start()
     keep_own = pltpu.make_async_copy(r.cot_buf, r.grad_ffn.at[block_rows(me)], r.keep_sem.at[6])
@@ -1784,6 +1458,307 @@
     return types.SimpleNamespace(**dict(zip(outs, results)))
 
 
+def attend_kernel(names, *refs):
+    r = types.SimpleNamespace(**dict(zip(names, refs)))
+    f32, bf16 = jnp.float32, jnp.bfloat16
+    local, width = r.tokens.shape
+    tokens, head_cols = r.qkv.shape
+    part = r.w_query.shape[0]
+    piece = part // 4
+    half = local // 2
+    weights = (r.w_query, r.w_key, r.w_value)
+    sizes = [weight.shape[1] // 4 for weight in weights]
+    starts = (0, sizes[0], sizes[0] + sizes[1])
+    q_cols, k_cols = sizes[0], sizes[1]
+    heads = q_cols // HEAD_SIZE
+    block = min(TILE, tokens)
+    n_blocks = tokens // block
+    head_scale = HEAD_SIZE ** (-0.5)
+
+    me, x_place, y_place, far_place = plane_places()
+    others = (x_place, y_place, far_place)
+    x_other, y_other = {"shard": x_place}, {"shard": y_place}
+    place = lax.axis_index("rep")
+    chip, core = place // 2, place % 2
+    twin = {"rep": place + 1 - 2 * core}
+    next_chip = {"rep": place + 2 - 4 * (chip % 2)}
+    quarter = (chip % 2) * 2 + core
+    next_quarter = (1 - chip % 2) * 2 + core
+
+    load_tokens = pltpu.make_async_copy(r.tokens, r.token_buf, r.load_sem.at[0])
+    load_info = pltpu.make_async_copy(
+        r.info, r.info_buf.at[pl.ds(pl.multiple_of(me * local, 16), local)], r.load_sem.at[1]
+    )
+    load_heads = [
+        pltpu.make_async_copy(
+            weights[kind].at[:, pl.ds(pl.multiple_of(me * sizes[kind], 128), sizes[kind])],
+            r.heads_buf.at[
+                pl.ds(pl.multiple_of(me * part, 16), part), pl.ds(starts[kind], sizes[kind])
+            ],
+            r.load_sem.at[2 + kind],
+        )
+        for kind in range(3)
+    ]
+    load_tokens.start()
+    load_info.start()
+    for copy in load_heads:
+        copy.start()
+
+    barrier = pltpu.get_barrier_semaphore()
+    for where in [{"shard": other} for other in others] + [twin, next_chip]:
+        pl.semaphore_signal(barrier, inc=1, device_id=where, device_id_type=pl.DeviceIdType.MESH)
+    pl.semaphore_wait(barrier, 5)
+
+    def piece_rows(owner, which):
+        return pl.ds(pl.multiple_of(owner * part + which * piece, 16), piece)
+
+    fetch = [
+        [
+            remote(
+                weights[kind].at[
+                    pl.ds(pl.multiple_of(quarter * piece, 16), piece),
+                    pl.ds(pl.multiple_of(other * sizes[kind], 128), sizes[kind]),
+                ],
+                r.heads_buf.at[piece_rows(me, quarter), pl.ds(starts[kind], sizes[kind])],
+                r.fetch_send.at[i, kind], r.fetch_recv.at[i, kind], {"shard": other},
+            )
+            for kind in range(3)
+        ]
+        for i, other in enumerate(others)
+    ]
+    for i in (2, 0, 1):
+        for copy in fetch[i]:
+            copy.start()
+    tell_info = [
+        remote(
+            r.info, r.info_buf.at[pl.ds(pl.multiple_of(me * local, 16), local)],
+            r.info_send.at[i], r.info_recv.at[i], {"shard": other},
+        )
+        for i, other in enumerate(others)
+    ]
+    for copy in tell_info:
+        copy.start()
+
+    def pass_piece(i, which, where, index):
+        ref = r.heads_buf.at[piece_rows(others[i], which)]
+        return remote(ref, ref, r.pass_send.at[index, i], r.pass_recv.at[index, i], where)
+
+    to_chip = [pass_piece(i, quarter, next_chip, 0) for i in range(3)]
+    to_twin = [pass_piece(i, quarter, twin, 1) for i in range(3)]
+    on_twin = [pass_piece(i, next_quarter, twin, 2) for i in range(3)]
+
+    def half_rows(owner, which):
+        return r.all_buf.at[pl.ds(pl.multiple_of(owner * local + which * half, 16), half)]
+
+    def send(owner, which, index, where):
+        ref = half_rows(owner, which)
+        return remote(ref, ref, r.all_send.at[index], r.all_recv.at[index], where)
+
+    own = [
+        [send(me, which, 2 * which + i, where) for i, where in enumerate((x_other, y_other))]
+        for which in range(2)
+    ]
+    on = (send(x_place, 0, 4, y_other), send(y_place, 1, 5, x_other))
+
+    load_tokens.wait()
+
+    def norm_rows(which, index, carry):
+        rows = pl.ds(pl.multiple_of(which * half + index * 32, 16), 32)
+        values = r.token_buf[rows].astype(f32)
+        inv = lax.rsqrt(jnp.mean(values * values, axis=-1, keepdims=True) + norm_eps)
+        r.all_buf[pl.ds(pl.multiple_of(me * local + which * half + index * 32, 16), 32)] = (
+            values * inv * r.gains[3:4]
+        ).astype(bf16)
+        return carry
+
+    for which in range(2):
+        lax.fori_loop(0, half // 32, functools.partial(norm_rows, which), 0)
+        for copy in own[which]:
+            copy.start()
+
+    for i in (2, 0, 1):
+        for copy in fetch[i]:
+            copy.wait_recv()
+        to_chip[i].start()
+        to_twin[i].start()
+    own[0][0].wait_recv()
+    on[0].start()
+    own[1][1].wait_recv()
+    on[1].start()
+    for i in (2, 0, 1):
+        to_chip[i].wait_recv()
+        on_twin[i].start()
+
+    load_info.wait()
+    for copy in tell_info:
+        copy.wait_recv()
+    r.key_info[...] = jnp.transpose(r.info_buf[...].astype(f32))[0:8]
+    for copy in load_heads:
+        copy.wait()
+    for copy in to_twin + on_twin:
+        copy.wait_recv()
+
+    def project(owner):
+        rows = pl.ds(pl.multiple_of(owner * local, 16), local)
+        r.qkv_buf[rows] = dot_plain(r.all_buf[rows], r.heads_buf[...]).astype(bf16)
+
+    project(me)
+    own[1][0].wait_recv()
+    project(x_place)
+    own[0][1].wait_recv()
+    project(y_place)
+    for copy in on:
+        copy.wait_recv()
+    project(far_place)
+    keep = [pltpu.make_async_copy(r.qkv_buf, r.qkv, r.keep_sem.at[0])]
+    keep[0].start()
+
+    def keep_item(item):
+        head, rows = item // n_blocks, pl.ds((item % n_blocks) * block, block)
+        slot = item % 2
+        return [
+            pltpu.make_async_copy(r.probs_stage.at[slot], r.probs.at[head, rows], r.stage_sem.at[slot, 0]),
+            pltpu.make_async_copy(r.tanh_stage.at[slot], r.tanh.at[head, rows], r.stage_sem.at[slot, 1]),
+        ]
+
+    for item in range(heads * n_blocks):
+        head, first, slot = item // n_blocks, (item % n_blocks) * block, item % 2
+        limit = first + block
+        columns = pl.ds(head * HEAD_SIZE, HEAD_SIZE)
+        r.score[:, pl.ds(0, limit)] = dot_rows(
+            r.qkv_buf[pl.ds(first, block), columns], r.qkv_buf[pl.ds(0, limit), pl.ds(q_cols, k_cols)]
+        )
+        if item >= 2:
+            for copy in keep_item(item - 2):
+                copy.wait()
+        if limit < tokens:
+            nothing = jnp.zeros((block, tokens - limit), f32)
+            r.probs_stage[slot, :, pl.ds(limit, tokens - limit)] = nothing
+            r.tanh_stage[slot, :, pl.ds(limit, tokens - limit)] = nothing
+
+        def rows_of(index, carry, first=first, limit=limit, slot=slot):
+            here = pl.ds(pl.multiple_of(index * 64, 64), 64)
+            info = r.info_buf[pl.ds(pl.multiple_of(first + index * 64, 64), 64)].astype(f32)
+            keys = r.key_info[3:4, pl.ds(0, limit)]
+            query_at = lax.broadcasted_iota(jnp.int32, (64, limit), 0) + (first + index * 64)
+            key_at = lax.broadcasted_iota(jnp.int32, (64, limit), 1)
+            related = (keys == info[:, 0:1]) | (keys == info[:, 1:2]) | (keys == info[:, 2:3])
+            visible = ((key_at <= query_at) & related) | (key_at == query_at)
+            curve = jnp.tanh(r.score[here, pl.ds(0, limit)] * (head_scale / softcap))
+            masked = jnp.where(visible, softcap * curve, -1e30)
+            terms = jnp.exp(masked - jnp.max(masked, axis=-1, keepdims=True))
+            probs = terms / jnp.sum(terms, axis=-1, keepdims=True)
+            r.tanh_stage[slot, here, pl.ds(0, limit)] = curve
+            r.probs_stage[slot, here, pl.ds(0, limit)] = probs
+            r.probs_low[here, pl.ds(0, limit)] = probs.astype(bf16)
+            return carry
+
+        lax.fori_loop(0, block // 64, rows_of, 0)
+        for copy in keep_item(item):
+            copy.start()
+        r.mixed_buf[pl.ds(first, block), columns] = dot_plain(
+            r.probs_low[:, pl.ds(0, limit)],
+            r.qkv_buf[pl.ds(0, limit), pl.ds(q_cols + k_cols, k_cols)],
+        ).astype(bf16)
+
+    keep.append(pltpu.make_async_copy(r.mixed_buf, r.mixed, r.keep_sem.at[1]))
+    keep[1].start()
+
+    wide = r.cols_buf.shape[1]
+    for owner in range(4):
+
+        @pl.when(me == owner)
+        def _():
+            def rows_of(index, carry):
+                rows = pl.ds(pl.multiple_of(index * 64, 64), 64)
+                some = r.all_buf[rows, owner * part : (owner + 1) * part]
+                if wide > part:
+                    some = jnp.concatenate((some, jnp.zeros((64, wide - part), bf16)), axis=1)
+                r.cols_buf[rows] = some
+                return carry
+
+            lax.fori_loop(0, tokens // 64, rows_of, 0)
+
+    keep.append(pltpu.make_async_copy(r.cols_buf, r.normed_cols, r.keep_sem.at[2]))
+    keep[2].start()
+    for group in fetch + own:
+        for copy in group:
+            copy.wait_send()
+    for copy in list(on) + tell_info + to_chip + to_twin + on_twin:
+        copy.wait_send()
+    last = heads * n_blocks
+    for item in range(max(0, last - 2), last):
+        for copy in keep_item(item):
+            copy.wait()
+    for copy in keep:
+        copy.wait()
+
+
+def attend(collective_id, **args):
+    f32, bf16 = jnp.float32, jnp.bfloat16
+    given = types.SimpleNamespace(**args)
+    local, width = given.tokens.shape
+    tokens = 4 * local
+    part = given.w_query.shape[0]
+    part_wide = -(-part // PAIR) * PAIR
+    q_cols, k_cols = given.w_query.shape[1] // 4, given.w_key.shape[1] // 4
+    head_cols = q_cols + 2 * k_cols
+    heads = q_cols // HEAD_SIZE
+    block = min(TILE, tokens)
+    vmem, dma, shape = pltpu.VMEM, pltpu.SemaphoreType.DMA, jax.ShapeDtypeStruct
+    outs = dict(
+        qkv=shape((tokens, head_cols), bf16),
+        mixed=shape((tokens, q_cols), bf16),
+        probs=shape((heads, tokens, tokens), f32),
+        tanh=shape((heads, tokens, tokens), f32),
+        normed_cols=shape((tokens, part_wide), bf16),
+    )
+    scratch = dict(
+        token_buf=vmem((local, width), bf16),
+        all_buf=vmem((tokens, width), bf16),
+        heads_buf=vmem((width, head_cols), bf16),
+        info_buf=vmem((tokens, 128), bf16),
+        key_info=vmem((8, tokens), f32),
+        qkv_buf=vmem((tokens, head_cols), bf16),
+        mixed_buf=vmem((tokens, q_cols), bf16),
+        cols_buf=vmem((tokens, part_wide), bf16),
+        score=vmem((block, tokens), f32),
+        probs_stage=vmem((2, block, tokens), f32),
+        tanh_stage=vmem((2, block, tokens), f32),
+        probs_low=vmem((block, tokens), bf16),
+        load_sem=dma((5,)),
+        keep_sem=dma((3,)),
+        stage_sem=dma((2, 2)),
+        fetch_send=dma((3, 3)),
+        fetch_recv=dma((3, 3)),
+        info_send=dma((3,)),
+        info_recv=dma((3,)),
+        pass_send=dma((3, 3)),
+        pass_recv=dma((3, 3)),
+        all_send=dma((6,)),
+        all_recv=dma((6,)),
+    )
+    any_space = pl.BlockSpec(memory_space=pl.ANY)
+    small = pl.BlockSpec(memory_space=pltpu.VMEM)
+    results = pl.pallas_call(
+        functools.partial(attend_kernel, tuple(args) + tuple(outs) + tuple(scratch)),
+        out_shape=list(outs.values()),
+        in_specs=[
+            small if value.ndim == 2 and value.shape[0] <= 8 else any_space
+            for value in args.values()
+        ],
+        out_specs=[any_space] * len(outs),
+        scratch_shapes=list(scratch.values()),
+        compiler_params=pltpu.CompilerParams(
+            collective_id=collective_id, has_side_effects=True, vmem_limit_bytes=VMEM_LIMIT
+        ),
+        cost_estimate=pl.CostEstimate(
+            flops=4 * tokens * width * head_cols, bytes_accessed=100 * 2**20, transcendentals=0
+        ),
+    )(*args.values())
+    return types.SimpleNamespace(**dict(zip(outs, results)))
+
+
 QUERY_HEADS = 8
 KV = 4
 HEAD_SIZE = 256
@@ -1810,34 +1785,22 @@
     return jax.nn.gelu(gate_pre, approximate=True) * up_pre
 
 
-def gather_rows(block, collective_id):
-    if lax.axis_size("shard") == 4:
-        return gather4(block, collective_id)
+def gather_rows(block):
     return lax.all_gather(block, "shard", axis=0, tiled=True)
 
 
-def scatter_rows(partial, collective_id):
-    if lax.axis_size("shard") == 4:
-        return scatter4(partial, collective_id)
+def scatter_rows(partial):
     summed = lax.psum_scatter(partial, "shard", scatter_dimension=0, tiled=True)
     return summed.astype(jnp.float32)
 
 
-def exchange(blocks, collective_id):
-    if lax.axis_size("shard") == 4:
-        return exchange4(blocks, collective_id)
+def exchange(blocks):
     return lax.all_to_all(blocks, "shard", 0, 0, tiled=True)
 
 
 def first_gather(normed, seg_ids, w_query, w_key, w_value):
     n = lax.axis_size("shard")
-    tok_rows, width = normed.shape
-    codes = seg_ids.astype(jnp.bfloat16)
-    if n == 4:
-        codes = jnp.pad(codes, (0, 2048 - tok_rows)).reshape(16, 128)
-        normed_all, codes, heads = prologue4(normed, codes, w_query, w_key, w_value, 2)
-        codes = codes.reshape(n, -1)[:, :tok_rows].reshape(-1)
-        return normed_all, codes.astype(jnp.int32), heads
+    width = normed.shape[1]
     part_rows = w_query.shape[0]
     share = max(1, n // KV)
 
@@ -1850,10 +1813,9 @@
     parts = jnp.concatenate(
         (w_query.reshape(part_rows, n, -1), by_device(w_key), by_device(w_value)), axis=2
     ).transpose(1, 0, 2)
-    heads = lax.all_to_all(parts, "shard", 0, 0, tiled=True).reshape(width, -1)
-    normed_all = lax.all_gather(normed, "shard", axis=0, tiled=True)
-    codes = lax.all_gather(codes, "shard", axis=0, tiled=True)
-    return normed_all, codes.astype(jnp.int32), heads
+    heads = exchange(parts).reshape(width, -1)
+    codes = gather_rows(seg_ids.astype(jnp.bfloat16))
+    return gather_rows(normed), codes.astype(jnp.int32), heads
 
 
 def rep_sum(grads, width):
@@ -1861,6 +1823,86 @@
     return [
         total.reshape(grad.shape).astype(jnp.float32) for total, grad in zip(summed, grads)
     ]
+
+
+def plane_layer(
+    tokens, seg_ids, parents, attn_gain, w_query, w_key, w_value, w_out, post_attn_gain,
+    ffn_gain, w_gate, w_up, w_down, post_ffn_gain, cotangent,
+):
+    f32, bf16 = jnp.float32, jnp.bfloat16
+    tok_rows, width = tokens.shape
+    nothing = jnp.zeros((width,), f32)
+    gains = jnp.stack(
+        [gain.astype(f32) for gain in (post_attn_gain, ffn_gain, post_ffn_gain, attn_gain)]
+        + [nothing] * 4
+    )
+    parent_row = parents[0]
+    labels = jnp.arange(SEGS)
+
+    def lookup(ident):
+        return jnp.sum(jnp.where(ident[:, None] == labels[None, :], parent_row[None, :], 0), axis=1)
+
+    real = seg_ids < SEGS
+    parent_one = lookup(seg_ids)
+    codes = [jnp.where(real, code, -1) for code in (seg_ids, parent_one, lookup(parent_one))]
+    codes.append(jnp.where(real, seg_ids, -2))
+    info = jnp.pad(jnp.stack(codes, axis=1).astype(bf16), ((0, 0), (0, 124)))
+    heads = attend(
+        2, tokens=tokens, gains=gains, info=info, w_query=w_query, w_key=w_key, w_value=w_value
+    )
+    ahead = forward(
+        3,
+        mixed=heads.mixed,
+        w_out=w_out,
+        tokens=tokens,
+        cotangent=cotangent,
+        gains=gains,
+        w_gate=w_gate,
+        w_up=w_up,
+        w_down=w_down,
+    )
+    found = backward(
+        4,
+        grad_ffn=ahead.grad_ffn,
+        hidden=ahead.hidden,
+        gate=ahead.gate,
+        up=ahead.up,
+        normed_two=ahead.normed_two,
+        w_down=w_down,
+        w_gate=w_gate,
+        w_up=w_up,
+        w_out=w_out,
+        middle=ahead.middle,
+        attn_out=ahead.attn_out,
+        cotangent=cotangent,
+        gains=gains,
+        gain_parts=ahead.gain_part,
+        qkv=heads.qkv,
+        mixed=heads.mixed,
+        probs=heads.probs,
+        tanh=heads.tanh,
+        normed_cols=heads.normed_cols,
+        w_query=w_query,
+        w_key=w_key,
+        w_value=w_value,
+        tokens=tokens,
+    )
+    gain_sums = found.gain_sums
+    return (
+        ahead.output,
+        found.grad_tokens,
+        gain_sums[3],
+        found.query_sum.astype(f32),
+        found.key_sum.astype(f32),
+        found.value_sum.astype(f32),
+        found.out_sum.astype(f32),
+        gain_sums[1],
+        gain_sums[2],
+        found.gate_sum.astype(f32),
+        found.up_sum.astype(f32),
+        found.down_sum.astype(f32),
+        gain_sums[0],
+    )
 
 
 def body(
@@ -1880,6 +1922,11 @@
     post_ffn_gain,
     cotangent,
 ):
+    if lax.axis_size("shard") == 4 and lax.axis_size("rep") == 8:
+        return plane_layer(
+            tokens, seg_ids, parents, attn_gain, w_query, w_key, w_value, w_out, post_attn_gain,
+            ffn_gain, w_gate, w_up, w_down, post_ffn_gain, cotangent,
+        )
     f32, bf16 = jnp.float32, jnp.bfloat16
     tok_rows, width = tokens.shape
     n = lax.axis_size("shard")
@@ -1937,84 +1984,22 @@
     probs_b = probs.astype(bf16)
     mixed = jnp.einsum("krts,skh->tkrh", probs_b, values, preferred_element_type=f32)
     mixed = mixed.reshape(group_rows, q_cols).astype(bf16)
-    if n == 4 and lax.axis_size("rep") == 8:
-        part_wide = -(-part_rows // 128) * 128
-        widen = lambda array: jnp.pad(array, [(0, 0)] * (array.ndim - 1) + [(0, part_wide - part_rows)])
-        normed_cols = lax.dynamic_slice_in_dim(normed_all, me * part_rows, part_rows, axis=1)
-        nothing = jnp.zeros((width,), f32)
-        gains = jnp.stack([gain_two, gain_three, gain_four] + [nothing] * 5)
-        ahead = forward(
-            3,
-            mixed=mixed,
-            w_out=w_out,
-            tokens=tokens,
-            cotangent=cotangent,
-            gains=gains,
-            w_gate=w_gate,
-            w_up=w_up,
-            w_down=w_down,
-        )
-        found = backward(
-            7,
-            grad_ffn=ahead.grad_ffn,
-            hidden=ahead.hidden,
-            gate=ahead.gate,
-            up=ahead.up,
-            normed_two=ahead.normed_two,
-            w_down=w_down,
-            w_gate=w_gate,
-            w_up=w_up,
-            w_out=w_out,
-            middle=ahead.middle,
-            attn_out=ahead.attn_out,
-            cotangent=cotangent,
-            gains=gains,
-            gain_parts=ahead.gain_part,
-            gain_one=widen(gain_one.reshape(4, part_rows)),
-            qkv=qkv,
-            mixed=mixed,
-            probs=probs.reshape(q_heads, group_rows, group_rows),
-            tanh=tanh_part.reshape(q_heads, group_rows, group_rows),
-            normed_cols=widen(normed_cols),
-            w_query=w_query,
-            w_key=w_key,
-            w_value=w_value,
-            token_blocks=widen(tokens.reshape(tok_rows, 4, part_rows).transpose(1, 0, 2)),
-        )
-        resid = found.resid_part[:, :, :part_rows].transpose(1, 0, 2).reshape(tok_rows, width)
-        grad_tokens = (found.grad_middle + resid.astype(f32)).astype(bf16)
-        gains = found.gain_sums
-        return (
-            ahead.output,
-            grad_tokens,
-            gains[4:, :part_rows].reshape(width),
-            found.query_sum.astype(f32),
-            found.key_sum.astype(f32),
-            found.value_sum.astype(f32),
-            found.out_sum.astype(f32),
-            gains[1],
-            gains[2],
-            found.gate_sum.astype(f32),
-            found.up_sum.astype(f32),
-            found.down_sum.astype(f32),
-            gains[0],
-        )
-    attn_out = scatter_rows(jnp.dot(mixed, w_out, preferred_element_type=f32).astype(bf16), 3)
+    attn_out = scatter_rows(jnp.dot(mixed, w_out, preferred_element_type=f32).astype(bf16))
     post_one, rms_two = normalize(attn_out, gain_two)
     middle = residual + post_one
     normed_two, rms_three = normalize(middle, gain_three)
-    normed_two_all = gather_rows(normed_two.astype(bf16), 4)
+    normed_two_all = gather_rows(normed_two.astype(bf16))
     gate_pre = jnp.dot(normed_two_all, w_gate, preferred_element_type=f32)
     up_pre = jnp.dot(normed_two_all, w_up, preferred_element_type=f32)
     hidden, geglu_back = jax.vjp(geglu, gate_pre, up_pre)
     hidden_b = hidden.astype(bf16)
-    ffn_out = scatter_rows(jnp.dot(hidden_b, w_down, preferred_element_type=f32).astype(bf16), 5)
+    ffn_out = scatter_rows(jnp.dot(hidden_b, w_down, preferred_element_type=f32).astype(bf16))
     post_two, rms_four = normalize(ffn_out, gain_four)
     output = (middle + post_two).astype(bf16)
 
     grad_out = cotangent.astype(f32)
     grad_ffn, grad_gain_four = norm_back(ffn_out, rms_four, gain_four, grad_out)
-    grad_ffn_all = gather_rows(grad_ffn.astype(bf16), 6)
+    grad_ffn_all = gather_rows(grad_ffn.astype(bf16))
     down_part = jnp.einsum("tf,td->fd", hidden_b, grad_ffn_all, preferred_element_type=f32)
     grad_hidden = jnp.einsum("td,fd->tf", grad_ffn_all, w_down, preferred_element_type=f32)
     grad_gate, grad_up = geglu_back(grad_hidden)
@@ -2022,13 +2007,13 @@
     grad_up_b = grad_up.astype(bf16)
     grad_normed_two = jnp.einsum("tf,df->td", grad_gate_b, w_gate, preferred_element_type=f32)
     grad_normed_two += jnp.einsum("tf,df->td", grad_up_b, w_up, preferred_element_type=f32)
-    grad_normed_two = scatter_rows(grad_normed_two.astype(bf16), 7)
+    grad_normed_two = scatter_rows(grad_normed_two.astype(bf16))
     gate_part = jnp.einsum("td,tf->df", normed_two_all, grad_gate_b, preferred_element_type=f32)
     up_part = jnp.einsum("td,tf->df", normed_two_all, grad_up_b, preferred_element_type=f32)
     grad_middle_part, grad_gain_three = norm_back(middle, rms_three, gain_three, grad_normed_two)
     grad_middle = grad_out + grad_middle_part
     grad_attn, grad_gain_two = norm_back(attn_out, rms_two, gain_two, grad_middle)
-    grad_attn_all = gather_rows(grad_attn.astype(bf16), 8)
+    grad_attn_all = gather_rows(grad_attn.astype(bf16))
     out_part = jnp.einsum("tj,td->jd", mixed, grad_attn_all, preferred_element_type=f32)
     grad_mixed = jnp.einsum("td,jd->tj", grad_attn_all, w_out, preferred_element_type=f32)
     grad_mixed = grad_mixed.astype(bf16).reshape(group_rows, kv_heads, repeat, HEAD_SIZE)
@@ -2048,7 +2033,7 @@
         ),
         axis=1,
     ).astype(bf16)
-    grad_parts = gather_rows(grad_parts, 9).reshape(n, group_rows, -1)
+    grad_parts = gather_rows(grad_parts).reshape(n, group_rows, -1)
 
     def whole_heads(parts):
         if share > 1:
@@ -2065,7 +2050,7 @@
     )
     qkv_local = jnp.concatenate((w_query, w_key, w_value), axis=1)
     grad_normed = jnp.einsum("tj,dj->td", grad_qkv, qkv_local, preferred_element_type=f32)
-    grad_normed = exchange(grad_normed.astype(bf16).reshape(n, tok_rows, part_rows), 10)
+    grad_normed = exchange(grad_normed.astype(bf16).reshape(n, tok_rows, part_rows))
     grad_normed = grad_normed.transpose(1, 0, 2).reshape(tok_rows, width).astype(f32)
     normed_cols = lax.dynamic_slice_in_dim(normed_all, me * part_rows, part_rows, axis=1)
     qkv_part = jnp.einsum("td,tj->dj", normed_cols, grad_qkv, preferred_element_type=f32)

time: 771 us -> 728 us (0.944)
  other arithmetic: 59.8 us -> 41.8 us
  matrix products: 11.4 us -> 0 us
  local copies, waits for them, and re-layouts: 15.1 us -> 6.87 us
    dot_general x3 -> x0, matrix products: 11.4 us -> none  [the longest x1 7.23 us: body(): jnp.dot(normed_all, qkv_heads, preferred_element_type=f32).astype(bf16)]
    reshape x2 -> x0, other arithmetic: 8.16 us -> none  [the longest x1 5.22 us: body(): tanh_part.reshape(q_heads, group_rows, group_rows)]
    convert_element_type x13 -> x7, other arithmetic: 46.8 us -> 39.6 us  [the longest x1 15.6 us: plane_layer(): found.gate_sum.astype(f32)]
where the time goes in v6:
time: 728 us
  Pallas kernels  678 us (93%)
  other arithmetic  41.8 us (6%)
    pallas_call x1, Pallas kernels, backward(): pl.pallas_call(functools.partial(backward_kernel, (tokens, local, width,...  474 us
    pallas_call x1, Pallas kernels, forward(): pl.pallas_call(functools.partial(forward_kernel, tuple(args) + tuple(outs...  140 us
    pallas_call x1, Pallas kernels, attend(): pl.pallas_call(functools.partial(attend_kernel, tuple(args) + tuple(outs)...  64.7 us
    convert_element_type x1, other arithmetic, plane_layer(): found.gate_sum.astype(f32)  15.6 us

profile of v6, /device:TPU:0, one launch (start us, length us, event | category | flops | bytes accessed | tf_op | source)
XLA Modules:
  0.0 727.9 jit_solution(17820634537172018079)
XLA Ops:
  0.6 0.8 select_reduce_fusion.1
  1.4 0.7 select_reduce_fusion
  2.2 0.7 select_convert_fusion.3
  2.9 0.1 copy.33
  3.1 0.6 pad.4.refs_2_
  3.7 0.7 reshape.28
  4.4 0.7 reshape.29
  5.1 0.7 reshape.30
  5.8 0.7 reshape.31
  6.5 0.7 stack.59.refs_1_.refs_4_.refs_12_
  7.2 64.7 %shard_map.246 = (bf16[768,1024]{1,0:T(8,128)(2,1)}, bf16[768,512]{1,0:T(8,128)(2,1)}, f32[2,768,768]{2,1,0:T(8,128)}, f32[2,768,768]{2,1,0:T(8,128)}, bf16[768,640]{1,0:T(8,128)(2,1)}) custom-call(bf16[192,2304]{1,0:T(8,128)(2,1)} %refs_22_.1, f32[8,2304]{1,0:T(8,128)} %stack.59.refs_1_.refs_4_.refs_12_, bf16[192,128]{1,0:T(8,128)(2,1)} %pad.4.refs_2_, ...), custom_call_target="tpu_custom_call" | custom-call | flops 7247757312 | bytes 104857600 | tf_op jit(solution)/shard_map/pallas_call | solution.py:1743
  71.9 140.0 %shard_map.247 = (bf16[768,2304]{1,0:T(8,128)(2,1)}, bf16[768,2304]{1,0:T(8,128)(2,1)}, bf16[768,2304]{1,0:T(8,128)(2,1)}, bf16[768,2304]{1,0:T(8,128)(2,1)}, bf...) custom-call(bf16[768,512]{1,0:T(8,128)(2,1)} %get-tuple-element.36.r, ...), custom_call_target="tpu_custom_call" | custom-call | flops 32614907904 | bytes 104857600 | tf_op jit(solution)/shard_map/pallas_call | solution.py:1442
  211.9 473.7 %shard_map.248 = (bf16[2304,2304]{1,0:T(8,128)(2,1)}, bf16[2304,2304]{1,0:T(8,128)(2,1)}, bf16[2304,2304]{1,0:T(8,128)(2,1)}, bf16[512,2304]{1,0:T(8,128)(2,1)},...) custom-call(bf16[768,2304]{1,0:T(8,128)(2,1)} %get-tuple-element.38., ...), custom_call_target="tpu_custom_call" | custom-call | flops 326149079040 | bytes 419430400 | tf_op jit(solution)/shard_map/pallas_call | solution.py:1118
  685.7 0.0 copy-start
  685.7 0.0 slice-start
  685.7 0.0 slice-start.1
  685.7 15.6 %convert_element_type.32 = f32[2304,2304]{1,0:T(8,128)} convert(bf16[2304,2304]{1,0:T(8,128)(2,1)} %get-tuple-element.56) | non-fusion elementwise | flops 5308416 | bytes 31850496 | tf_op jit(solution)/shard_map/convert_element_type | solution.py:1901
  701.3 0.0 copy-done
  701.3 0.0 slice-start.2
  701.3 7.7 %convert_element_type.33 = f32[2304,2304]{1,0:T(8,128)} convert(bf16[2304,2304]{1,0:T(8,128)(2,1)S(1)} %copy-done) | non-fusion elementwise | flops 5308416 | bytes 31850496 | tf_op jit(solution)/shard_map/convert_element_type | solution.py:1902
  709.0 0.0 slice-done
  709.0 0.0 slice-done.1
  709.0 0.0 slice-done.2
  709.0 0.0 copy-start.2
  709.0 7.6 %convert_element_type.34 = f32[2304,2304]{1,0:T(8,128)} convert(bf16[2304,2304]{1,0:T(8,128)(2,1)S(1)} %bitcast.2) | non-fusion elementwise | flops 5308416 | bytes 31850496 | tf_op jit(solution)/shard_map/convert_element_type | solution.py:1903
  716.6 0.0 copy-done.2
  716.6 0.0 copy-start.1
  716.6 2.8 convert_element_type.28
  719.4 0.0 copy-done.1
  719.4 0.0 copy-start.4
  719.4 2.5 convert_element_type.31
  721.9 0.0 copy-start.3
  721.9 0.0 copy-done.4
  721.9 0.0 copy-start.7
  721.9 0.0 copy-start.5
  721.9 1.7 convert_element_type.29
  723.6 0.0 copy-start.6
  723.6 0.0 copy-done.3
  723.7 1.7 convert_element_type.30
  725.3 0.0 copy-done.7
  725.3 0.7 slice_reduce_fusion
  726.0 0.0 copy-done.5
  726.0 0.9 copy.36
  727.0 0.0 copy-done.6
  727.0 0.9 copy.37
  (7 shorter events, 0.0 us)
Async XLA Ops:
  685.7 15.7 %copy-start = (bf16[2304,2304]{1,0:T(8,128)(2,1)S(1)}, bf16[2304,2304]{1,0:T(8,128)(2,1)}, u32[]{:S(2)}) copy-start(bf16[2304,2304]{1,0:T(8,128)(2,1)} %get-tuple-element.57) | copy-start | bytes 31850500
  685.7 23.3 %slice-start = ((s8[10616832]{0:T(1024)(128)(4,1)}), s8[4194304]{0:T(1024)(128)(4,1)S(1)}, s32[]{:S(2)}) async-start(s8[10616832]{0:T(1024)(128)(4,1)} %bitcast.1), calls=%async_computation | async-start | bytes 8388608
  685.7 23.3 %slice-start.1 = ((s8[10616832]{0:T(1024)(128)(4,1)}), s8[4194304]{0:T(1024)(128)(4,1)S(1)}, s32[]{:S(2)}) async-start(s8[10616832]{0:T(1024)(128)(4,1)} %bitcast.1), calls=%async_computation.1 | async-start | bytes 8388608
  701.3 7.7 %slice-start.2 = ((s8[10616832]{0:T(1024)(128)(4,1)}), s8[2228224]{0:T(1024)(128)(4,1)S(1)}, s32[]{:S(2)}) async-start(s8[10616832]{0:T(1024)(128)(4,1)} %bitcast.1), calls=%async_computation.2 | async-start | bytes 4456448
  709.0 7.6 %copy-start.2 = (bf16[576,2048]{1,0:T(8,128)(2,1)S(1)}, bf16[576,2048]{1,0:T(8,128)(2,1)}, u32[]{:S(2)}) copy-start(bf16[576,2048]{1,0:T(8,128)(2,1)} %get-tuple-element.52) | copy-start | bytes 7077892
  716.6 2.8 copy-start.1
  719.4 2.5 copy-start.4
  721.9 1.7 copy-start.3
  721.9 3.4 copy-start.7
  721.9 4.1 copy-start.5
  723.6 3.3 copy-start.6

commit v7 on v6

--- a/solution.py
+++ b/solution.py
@@ -279,7 +279,9 @@
 
 TILE = 256
 PAIR = 2 * CHUNK
-DEEP = 8
+LINE = 32
+DEEP = 12
+LAST = 6
 ROOT_TWO_PI = math.sqrt(2.0 / math.pi)
 
 
@@ -293,6 +295,10 @@
 
 def dot_columns(left, right):
     return lax.dot_general(left, right, (((0,), (0,)), ((), ())), preferred_element_type=jnp.float32)
+
+
+def column_pieces(width):
+    return 3 if width % 384 == 0 else 2
 
 
 def backward_kernel(dims, names, *refs):
@@ -310,13 +316,19 @@
     n_b = width // TILE
     block = min(TILE, tokens)
     n_blocks = tokens // block
+    pieces = column_pieces(width)
+    piece = width // pieces
+    group = PAIR * pieces
 
     counts = (
-        inner_width // PAIR, width // PAIR, width // PAIR, r.w_out.shape[0] // PAIR, part // CHUNK
+        inner_width // PAIR, width // PAIR, width // PAIR, r.w_out.shape[0] // PAIR,
+        part // (2 * LINE),
     )
     first = [sum(counts[:job]) for job in range(6)]
-    steps = first[5]
-    b_at = (n_a + 1) // 2
+    units = first[5]
+    steps = 2 * units
+    a_at = pieces + 1
+    b_at = a_at + (n_a + 1) // 2
     c_at = b_at + n_b
     d_at = c_at + 5
     f_at = d_at + 5
@@ -325,7 +337,7 @@
     i_at = h_at + 9
     k_at = i_at + 3
     assert b_at <= first[1] and f_at < first[3] and i_at < first[4] and first[1] <= i_at
-    assert first[2] <= i_at and k_at + 5 <= steps + 8
+    assert first[2] <= i_at and k_at + 5 <= units + 5 and counts[0] // pieces >= 2
 
     place = lax.axis_index("rep")
     chips = lax.axis_size("rep") // 2
@@ -348,7 +360,10 @@
     def load(src, dst, index):
         return pltpu.make_async_copy(src, dst, r.load_sem.at[index])
 
-    load_ffn = load(r.grad_ffn, r.ffn_buf.at[:, pl.ds(0, width)], 0)
+    load_ffn = load(
+        r.grad_ffn,
+        r.ffn_buf.at[pl.ds(pl.multiple_of(me * local, 16), local), pl.ds(0, width)], 0,
+    )
     load_hidden = load(r.hidden, r.hidden_buf.at[:, pl.ds(0, inner_width)], 1)
     load_two = load(r.normed_two, r.two_buf, 2)
     load_small = (
@@ -387,11 +402,13 @@
             r.stage.at[tile % 2], r.partial.at[:, columns], r.stage_sem.at[tile % 2]
         )
 
+    for index, gain in enumerate((r.post_attn_gain, r.ffn_gain, r.post_ffn_gain, r.attn_gain)):
+        r.gains[index : index + 1] = gain[...].astype(jnp.float32).reshape(1, gain.shape[0])
     load_ffn.start()
+    load_hidden.start()
     for buf in range(2):
         for copy in a_loads(buf, buf):
             copy.start()
-    load_hidden.start()
     load_two.start()
     for copy in load_small:
         copy.start()
@@ -411,7 +428,50 @@
         tell(barrier, outer)
         pl.semaphore_wait(barrier, 7)
 
+    def ffn_copies(index):
+        across = pl.ds(index * piece, piece)
+
+        def send(owner, which, at, where, own):
+            here = pl.ds(pl.multiple_of(owner * local + which * half, 16), half)
+            src = r.grad_ffn.at[pl.ds(which * half, half), across]
+            return remote(
+                src if own else r.ffn_buf.at[here, across], r.ffn_buf.at[here, across],
+                r.ffn_send.at[index, at], r.ffn_recv.at[index, at], where,
+            )
+
+        starts = (
+            send(me, 0, 0, x_other, True), send(me, 1, 1, y_other, True),
+            send(me, 1, 2, x_other, True), send(me, 0, 3, y_other, True),
+        )
+        return starts, (send(x_place, 0, 4, y_other, False), send(y_place, 1, 5, x_other, False))
+
+    ffn_pieces = [ffn_copies(index) for index in range(pieces)]
+
+    def ffn_pass(index):
+        starts, passes = ffn_pieces[index]
+        for i in range(2):
+            starts[i].wait_recv()
+            passes[i].start()
+
+    def ffn_arrived(index):
+        starts, passes = ffn_pieces[index]
+        for copy in starts[2:] + passes:
+            copy.wait_recv()
+
+    def ffn_sent():
+        for starts, passes in ffn_pieces:
+            for copy in starts + passes:
+                copy.wait_send()
+
+    for copy in ffn_pieces[0][0]:
+        copy.start()
+    ffn_pass(0)
+    for starts, _ in ffn_pieces[1:]:
+        for copy in starts:
+            copy.start()
     load_ffn.wait()
+    load_hidden.wait()
+    ffn_arrived(0)
 
     def a_tile(tile, buf):
         for copy in a_loads(tile, buf):
@@ -743,18 +803,42 @@
 
     sums = (r.down_sum, r.gate_sum, r.up_sum, r.out_sum)
 
-    def by_job(step, use):
+    def by_job(step, use, scale=2):
         for job in range(5):
 
-            @pl.when((step >= first[job]) & (step < first[job + 1]))
+            @pl.when((step >= scale * first[job]) & (step < scale * first[job + 1]))
             def _():
-                use(job, step - first[job])
+                use(job, step - scale * first[job])
+
+    def by_width(step, use):
+        if side == r.acc.shape[2]:
+            use(pl.ds(0, side))
+            return
+
+        @pl.when(step < 2 * first[4])
+        def _():
+            use(pl.ds(0, r.acc.shape[2]))
+
+        @pl.when(step >= 2 * first[4])
+        def _():
+            use(pl.ds(0, side))
 
     def results(job, index, slot):
+        if job == 0:
+            unit, which = index // 2, index % 2
+            low = (unit % (inner_width // group)) * group + (2 * which + core) * pieces * LINE
+            across = pl.ds(pl.multiple_of(unit // (inner_width // group) * piece, 128), piece)
+            return [
+                (
+                    r.total.at[slot, :, pl.ds(i * piece, piece)],
+                    r.down_sum.at[pl.ds(pl.multiple_of(low + i * LINE, LINE), LINE), across],
+                )
+                for i in range(pieces)
+            ]
         if job < 4:
-            rows = pl.ds(pl.multiple_of((2 * index + core) * CHUNK, CHUNK), CHUNK)
+            rows = pl.ds(pl.multiple_of((2 * index + core) * LINE, LINE), LINE)
             return [(r.total.at[slot, :, pl.ds(0, sums[job].shape[1])], sums[job].at[rows])]
-        rows = pl.ds(pl.multiple_of(index * CHUNK, CHUNK), CHUNK)
+        rows = pl.ds(pl.multiple_of(index * LINE, LINE), LINE)
         pairs, start = [], 0
         for ref in (r.query_sum, r.key_sum, r.value_sum):
             size = ref.shape[1] // 2
@@ -764,43 +848,62 @@
         return pairs
 
     def pair_copies(job, index, step):
-        slot = step % 4
+        slot = step % LAST
         return [
             remote(src, dst, r.pair_send.at[slot, i], r.pair_recv.at[step, i], twin)
             for i, (src, dst) in enumerate(results(job, index, slot))
         ]
 
     def store_copies(job, index, step):
-        slot = step % 4
+        slot = step % LAST
         return [
             pltpu.make_async_copy(src, dst, r.store_sem.at[slot, i])
             for i, (src, dst) in enumerate(results(job, index, slot))
         ]
 
-    def sib_copy(step):
-        give = pl.ds(pl.multiple_of((1 - core) * CHUNK, CHUNK), CHUNK)
+    def made_rows(step, owner):
+        return pl.ds(pl.multiple_of((step % 2) * 2 * LINE + owner * LINE, LINE), LINE)
+
+    def sib_copy(step, across):
         return remote(
-            r.made.at[step % 2, give], r.sib.at[step % 4],
-            r.sib_send.at[step % 4], r.sib_recv.at[step % 4], twin,
+            r.made.at[step // 2 % 2, made_rows(step, 1 - core), across],
+            r.sib.at[step % 4, :, across], r.sib_send.at[step % 4], r.sib_recv.at[step % 4], twin,
         )
 
-    def up_copy(step, dst, sem):
+    def up_copy(step, across, dst, sem):
         slot = step % DEEP
-        return remote(r.acc.at[slot], dst.at[slot], r.up_send.at[slot], sem.at[slot], inner)
-
-    def down_copy(step):
         return remote(
-            r.total.at[step % 4], r.inner_in.at[step % DEEP],
-            r.down_send.at[step % 4], r.inner_recv.at[step % DEEP], outer,
+            r.acc.at[slot, :, across], dst.at[slot, :, across], r.up_send.at[slot], sem.at[slot], inner
         )
 
-    def make(step):
-        slot = step % 2
+    def down_copy(step, across):
+        return remote(
+            r.total.at[step % LAST, :, across], r.inner_in.at[step % DEEP, :, across],
+            r.down_send.at[step % LAST], r.inner_recv.at[step % DEEP], outer,
+        )
+
+    def up_sent(step):
+        by_width(step, lambda across: up_copy(step, across, r.outer_in, r.outer_recv).wait_send())
+
+    def make(unit):
+        slot = unit % 2
 
         def product(job, index):
+            if job == 0:
+                n_groups = inner_width // group
+                rows = pl.ds(pl.multiple_of(index % n_groups * group, PAIR), group)
+                across = pl.ds(pl.multiple_of(index // n_groups * piece, 128), piece)
+                some = dot_columns(r.hidden_buf[:, rows], r.ffn_buf[:, across]).astype(bf16)
+                for row in range(4):
+                    for i in range(pieces):
+                        low = (row * pieces + i) * LINE
+                        r.made[slot, pl.ds(row * LINE, LINE), pl.ds(i * piece, piece)] = some[
+                            low : low + LINE
+                        ]
+                return
             if job < 4:
-                left_buf = (r.hidden_buf, r.two_buf, r.two_buf, r.mixed_buf)[job]
-                right_buf = (r.ffn_buf, r.gate_grad, r.up_grad, r.all_grad)[job]
+                left_buf = (None, r.two_buf, r.two_buf, r.mixed_buf)[job]
+                right_buf = (None, r.gate_grad, r.up_grad, r.all_grad)[job]
                 columns = pl.ds(pl.multiple_of(index * PAIR, PAIR), PAIR)
                 across = pl.ds(0, sums[job].shape[1])
                 r.made[slot, :, across] = dot_columns(
@@ -810,17 +913,20 @@
             columns = pl.ds(pl.multiple_of((index // 2) * PAIR, PAIR), PAIR)
             for which, buf in enumerate((r.hidden_buf, r.ffn_buf)):
                 r.both[...] = dot_columns(r.cols_buf[:, columns], buf[:, pl.ds(0, side)]).astype(bf16)
-                r.made[slot, pl.ds(which * CHUNK, CHUNK), pl.ds(0, side)] = r.both[
-                    pl.ds(pl.multiple_of((index % 2) * CHUNK, CHUNK), CHUNK)
-                ]
-
-        by_job(step, product)
-
+                for row in range(2):
+                    low = pl.multiple_of((index % 2) * 2 * LINE + row * LINE, LINE)
+                    r.made[slot, pl.ds((2 * row + which) * LINE, LINE), pl.ds(0, side)] = r.both[
+                        pl.ds(low, LINE)
+                    ]
+
+        by_job(unit, product, 1)
+
+    def give(step):
         @pl.when(step >= 4)
         def _():
             pl.semaphore_wait(r.sib_credit, 1)
 
-        sib_copy(step).start()
+        by_width(step, lambda across: sib_copy(step, across).start())
 
     def send_up(step):
         @pl.when(step >= DEEP)
@@ -829,22 +935,21 @@
 
         @pl.when(is_mid)
         def _():
-            up_copy(step, r.inner_in, r.inner_recv).start()
+            by_width(step, lambda across: up_copy(step, across, r.inner_in, r.inner_recv).start())
 
         @pl.when(jnp.logical_not(is_mid))
         def _():
-            up_copy(step, r.outer_in, r.outer_recv).start()
+            by_width(step, lambda across: up_copy(step, across, r.outer_in, r.outer_recv).start())
 
     def pair_up(step):
         slot = step % DEEP
-        sib_copy(step).wait()
+        by_width(step, lambda across: sib_copy(step, across).wait())
 
         @pl.when(step >= DEEP)
         def _():
-            up_copy(step, r.outer_in, r.outer_recv).wait_send()
-
-        mine = pl.ds(pl.multiple_of(core * CHUNK, CHUNK), CHUNK)
-        r.acc[slot] = add_low(r.made[step % 2, mine], r.sib[step % 4])
+            up_sent(step - DEEP)
+
+        r.acc[slot] = add_low(r.made[step // 2 % 2, made_rows(step, core)], r.sib[step % 4])
 
         @pl.when(step + 4 < steps)
         def _():
@@ -856,7 +961,7 @@
 
     def from_outer(step):
         slot = step % DEEP
-        up_copy(step, r.outer_in, r.outer_recv).wait_recv()
+        by_width(step, lambda across: up_copy(step, across, r.outer_in, r.outer_recv).wait_recv())
         r.acc[slot] = add_low(r.acc[slot], r.outer_in[slot])
 
         @pl.when(step + DEEP < steps)
@@ -876,19 +981,19 @@
 
         @pl.when(jnp.logical_not(is_end))
         def _():
-            down_copy(step).wait_send()
+            by_width(step, lambda across: down_copy(step, across).wait_send())
 
     def from_inner(step):
         slot = step % DEEP
-        down_copy(step).wait_recv()
-
-        @pl.when(step >= 4)
-        def _():
-            sends_done(step - 4)
+        by_width(step, lambda across: down_copy(step, across).wait_recv())
+
+        @pl.when(step >= LAST)
+        def _():
+            sends_done(step - LAST)
 
         @pl.when(is_mid)
         def _():
-            r.total[step % 4] = add_low(r.acc[slot], r.inner_in[slot])
+            r.total[step % LAST] = add_low(r.acc[slot], r.inner_in[slot])
 
             @pl.when(step + DEEP < steps)
             def _():
@@ -896,7 +1001,7 @@
 
         @pl.when(jnp.logical_not(is_mid))
         def _():
-            r.total[step % 4] = r.inner_in[slot]
+            r.total[step % LAST] = r.inner_in[slot]
 
             @pl.when(step + DEEP < steps)
             def _():
@@ -908,7 +1013,7 @@
             def _():
                 pl.semaphore_wait(r.down_credit, 1)
 
-            down_copy(step).start()
+            by_width(step, lambda across: down_copy(step, across).start())
 
         def use(job, index):
             for copy in pair_copies(job, index, step) + store_copies(job, index, step):
@@ -917,37 +1022,30 @@
         by_job(step, use)
 
     lag_outer = 3
-    lag_inner = jnp.where(is_end, 8, 6)
-    load_hidden.wait()
-    load_two.wait()
+    lag_inner = jnp.where(is_end, 10, 6)
 
     def at(now, step, use):
         @pl.when(now == step)
         def _():
             use()
 
-    def tick(now, carry):
-        @pl.when(now < steps)
-        def _():
-            make(now)
-
-        @pl.when((now >= 1) & (now - 1 < steps))
-        def _():
-            pair_up(now - 1)
-
-        @pl.when(jnp.logical_not(is_end) & (now >= lag_outer) & (now - lag_outer < steps))
-        def _():
-            from_outer(now - lag_outer)
-
-        @pl.when((now >= lag_inner) & (now - lag_inner < steps))
-        def _():
-            from_inner(now - lag_inner)
+    def work(now):
+        @pl.when(now == 0)
+        def _():
+            load_two.wait()
+
+        for index in range(1, pieces):
+            at(now, index, functools.partial(ffn_pass, index))
+
+            at(now, index + 1, functools.partial(ffn_arrived, index))
+
+        at(now, b_at, ffn_sent)
 
         for buf in range(2):
 
-            @pl.when(2 * now + buf < n_a)
+            @pl.when((now >= a_at) & (2 * (now - a_at) + buf < n_a))
             def _():
-                a_tile(2 * now + buf, buf)
+                a_tile(2 * (now - a_at) + buf, buf)
 
         @pl.when(now == b_at - 1)
         def _():
@@ -983,18 +1081,44 @@
         at(now, k_at + 1, k_plane)
         for index in range(3):
             at(now, k_at + 2 + index, functools.partial(k_rep, index))
+
+    def tick(now, carry):
+        @pl.when((now % 2 == 0) & (now < steps))
+        def _():
+            make(now // 2)
+
+        @pl.when(now < steps)
+        def _():
+            give(now)
+
+        @pl.when((now >= 1) & (now - 1 < steps))
+        def _():
+            pair_up(now - 1)
+
+        @pl.when(jnp.logical_not(is_end) & (now >= lag_outer) & (now - lag_outer < steps))
+        def _():
+            from_outer(now - lag_outer)
+
+        @pl.when((now >= lag_inner) & (now - lag_inner < steps))
+        def _():
+            from_inner(now - lag_inner)
+
+        @pl.when(now % 2 == 1)
+        def _():
+            work(now // 2)
+
         return carry
 
-    lax.fori_loop(0, steps + 8, tick, 0)
+    lax.fori_loop(0, steps + 10, tick, 0)
 
     def finish(step, carry):
         sends_done(step)
         return carry
 
-    lax.fori_loop(steps - 4, steps, finish, 0)
+    lax.fori_loop(steps - LAST, steps, finish, 0)
 
     def finish_up(step, carry):
-        up_copy(step, r.outer_in, r.outer_recv).wait_send()
+        up_sent(step)
         return carry
 
     lax.fori_loop(steps - DEEP, steps, finish_up, 0)
@@ -1015,7 +1139,7 @@
 def backward(collective_id, **args):
     f32, bf16 = jnp.float32, jnp.bfloat16
     given = types.SimpleNamespace(**args)
-    tokens, width = given.grad_ffn.shape
+    tokens, width = given.normed_two.shape
     inner_width = given.hidden.shape[1]
     local = tokens // 4
     half = local // 2
@@ -1025,8 +1149,9 @@
     out_rows = given.w_out.shape[0]
     side = 2 * head_cols
     slot_width = max(width, inner_width, side)
+    pieces = column_pieces(width)
     block = min(TILE, tokens)
-    steps = (inner_width + 2 * width + out_rows) // PAIR + part // CHUNK
+    steps = 2 * ((inner_width + 2 * width + out_rows) // PAIR + part // (2 * LINE))
     vmem, dma, credit = pltpu.VMEM, pltpu.SemaphoreType.DMA, pltpu.SemaphoreType.REGULAR
     shape = jax.ShapeDtypeStruct
     outs = dict(
@@ -1072,6 +1197,7 @@
         kv_grad=vmem((2, tokens, head_cols // 4), f32),
         head_grad=vmem((tokens, head_cols), bf16),
         norm_grad=vmem((4, local, part_wide), bf16),
+        gains=vmem((8, width), f32),
         gain_own=vmem((8, width), f32),
         gain_plane=vmem((4, 8, width), f32),
         gain_mine=vmem((3, 8, width), f32),
@@ -1079,14 +1205,16 @@
         gain_total=vmem((8, width), f32),
         made=vmem((2, PAIR, slot_width), bf16),
         both=vmem((PAIR, side), bf16),
-        sib=vmem((4, CHUNK, slot_width), bf16),
-        acc=vmem((DEEP, CHUNK, slot_width), bf16),
-        outer_in=vmem((DEEP, CHUNK, slot_width), bf16),
-        inner_in=vmem((DEEP, CHUNK, slot_width), bf16),
-        total=vmem((4, CHUNK, slot_width), bf16),
+        sib=vmem((4, LINE, slot_width), bf16),
+        acc=vmem((DEEP, LINE, slot_width), bf16),
+        outer_in=vmem((DEEP, LINE, slot_width), bf16),
+        inner_in=vmem((DEEP, LINE, slot_width), bf16),
+        total=vmem((LAST, LINE, slot_width), bf16),
         load_sem=dma((42,)),
         stage_sem=dma((2,)),
         keep_sem=dma((4,)),
+        ffn_send=dma((pieces, 6)),
+        ffn_recv=dma((pieces, 6)),
         c_send=dma((6,)),
         c_recv=dma((6,)),
         e_send=dma((6,)),
@@ -1102,10 +1230,10 @@
         up_send=dma((DEEP,)),
         outer_recv=dma((DEEP,)),
         inner_recv=dma((DEEP,)),
-        down_send=dma((4,)),
-        pair_send=dma((4, 3)),
-        pair_recv=dma((steps, 3)),
-        store_sem=dma((4, 3)),
+        down_send=dma((LAST,)),
+        pair_send=dma((LAST, pieces)),
+        pair_recv=dma((steps, pieces)),
+        store_sem=dma((LAST, pieces)),
         sib_credit=credit,
         up_credit=credit,
         down_credit=credit,
@@ -1113,7 +1241,7 @@
     any_space = pl.BlockSpec(memory_space=pl.ANY)
     small = pl.BlockSpec(memory_space=pltpu.VMEM)
     in_specs = [
-        small if value.ndim == 2 and value.shape[0] <= 8 else any_space for value in args.values()
+        small if value.ndim == 1 or value.shape[0] == 8 else any_space for value in args.values()
     ]
     results = pl.pallas_call(
         functools.partial(
@@ -1167,6 +1295,8 @@
     )
     for copy in early + small + big:
         copy.start()
+    for index, gain in enumerate((r.post_attn_gain, r.ffn_gain, r.post_ffn_gain, r.attn_gain)):
+        r.gains[index : index + 1] = gain[...].astype(jnp.float32).reshape(1, gain.shape[0])
     greet((x_place, y_place))
 
     def summing(landed, send_sem, recv_sem):
@@ -1211,9 +1341,6 @@
     c_far, c_near, c_on = summing(r.c_landed, r.c_send, r.c_recv)
     b_starts, b_on = gathering(
         lambda which: r.two_buf.at[half_rows(me, which)], r.two_buf, r.b_send, r.b_recv
-    )
-    d_starts, d_on = gathering(
-        lambda which: r.cot_buf.at[pl.ds(which * half, half)], r.grad_ffn, r.d_send, r.d_recv
     )
 
     for copy in early:
@@ -1367,21 +1494,11 @@
         c_near[which].wait_recv()
         c_on[which].wait_recv()
         lax.fori_loop(0, half // 32, functools.partial(last_rows, which), 0)
-        for copy in d_starts[which]:
-            copy.start()
-    keep_own = pltpu.make_async_copy(r.cot_buf, r.grad_ffn.at[block_rows(me)], r.keep_sem.at[6])
+    keep_own = pltpu.make_async_copy(r.cot_buf, r.grad_ffn, r.keep_sem.at[6])
     keep_out = pltpu.make_async_copy(r.token_buf, r.output, r.keep_sem.at[7])
     keep_own.start()
     keep_out.start()
-    d_starts[0][0].wait_recv()
-    d_on[0].start()
-    d_starts[1][1].wait_recv()
-    d_on[1].start()
-    d_starts[1][0].wait_recv()
-    d_starts[0][1].wait_recv()
-    for copy in d_on:
-        copy.wait_recv()
-    for copy in b_starts[0] + b_starts[1] + list(b_on + c_far + c_near + c_on) + d_starts[0] + d_starts[1] + list(d_on):
+    for copy in b_starts[0] + b_starts[1] + list(b_on + c_far + c_near + c_on):
         copy.wait_send()
     for copy in keep + keep_block(far_place) + [keep_two, keep_own, keep_out]:
         copy.wait()
@@ -1396,7 +1513,7 @@
     inner_width = given.w_down.shape[0]
     vmem, dma, shape = pltpu.VMEM, pltpu.SemaphoreType.DMA, jax.ShapeDtypeStruct
     outs = dict(
-        grad_ffn=shape((tokens, width), bf16),
+        grad_ffn=shape((local, width), bf16),
         hidden=shape((tokens, inner_width), bf16),
         gate=shape((tokens, inner_width), bf16),
         up=shape((tokens, inner_width), bf16),
@@ -1418,6 +1535,7 @@
         passed=vmem((2, half, width), bf16),
         a_landed=vmem((6, half, width), bf16),
         c_landed=vmem((6, half, width), bf16),
+        gains=vmem((8, width), f32),
         attn_buf=vmem((local, width), f32),
         middle_buf=vmem((local, width), f32),
         two_buf=vmem((tokens, width), bf16),
@@ -1434,8 +1552,6 @@
         b_recv=dma((6,)),
         c_send=dma((6,)),
         c_recv=dma((6,)),
-        d_send=dma((6,)),
-        d_recv=dma((6,)),
     )
     any_space = pl.BlockSpec(memory_space=pl.ANY)
     small = pl.BlockSpec(memory_space=pltpu.VMEM)
@@ -1443,7 +1559,7 @@
         functools.partial(forward_kernel, tuple(args) + tuple(outs) + tuple(scratch)),
         out_shape=list(outs.values()),
         in_specs=[
-            small if value.ndim == 2 and value.shape[0] <= 8 else any_space
+            small if value.ndim == 1 else any_space
             for value in args.values()
         ],
         out_specs=[small if value.shape[0] <= 8 else any_space for value in outs.values()],
@@ -1486,9 +1602,6 @@
     next_quarter = (1 - chip % 2) * 2 + core
 
     load_tokens = pltpu.make_async_copy(r.tokens, r.token_buf, r.load_sem.at[0])
-    load_info = pltpu.make_async_copy(
-        r.info, r.info_buf.at[pl.ds(pl.multiple_of(me * local, 16), local)], r.load_sem.at[1]
-    )
     load_heads = [
         pltpu.make_async_copy(
             weights[kind].at[:, pl.ds(pl.multiple_of(me * sizes[kind], 128), sizes[kind])],
@@ -1500,9 +1613,23 @@
         for kind in range(3)
     ]
     load_tokens.start()
-    load_info.start()
     for copy in load_heads:
         copy.start()
+
+    def lookup(ident):
+        found = jnp.full_like(ident, -1)
+        for label in range(SEGS):
+            found = jnp.where(ident == label, r.parents[0, label], found)
+        return found
+
+    ident = r.seg_ids[...]
+    parent_one = lookup(ident)
+    lanes = lax.broadcasted_iota(jnp.int32, ident.shape, 1)
+    codes = jnp.where(ident < SEGS, ident, jnp.where(lanes == 3, -2, -1))
+    codes = jnp.where(lanes == 1, parent_one, jnp.where(lanes == 2, lookup(parent_one), codes))
+    info_rows = pl.ds(pl.multiple_of(me * local, 16), local)
+    r.info_buf[info_rows] = codes.astype(f32).astype(bf16)
+    r.gain[...] = r.attn_gain[...].astype(f32).reshape(1, width)
 
     barrier = pltpu.get_barrier_semaphore()
     for where in [{"shard": other} for other in others] + [twin, next_chip]:
@@ -1531,7 +1658,7 @@
             copy.start()
     tell_info = [
         remote(
-            r.info, r.info_buf.at[pl.ds(pl.multiple_of(me * local, 16), local)],
+            r.info_buf.at[info_rows], r.info_buf.at[info_rows],
             r.info_send.at[i], r.info_recv.at[i], {"shard": other},
         )
         for i, other in enumerate(others)
@@ -1567,7 +1694,7 @@
         values = r.token_buf[rows].astype(f32)
         inv = lax.rsqrt(jnp.mean(values * values, axis=-1, keepdims=True) + norm_eps)
         r.all_buf[pl.ds(pl.multiple_of(me * local + which * half + index * 32, 16), 32)] = (
-            values * inv * r.gains[3:4]
+            values * inv * r.gain[...]
         ).astype(bf16)
         return carry
 
@@ -1589,7 +1716,6 @@
         to_chip[i].wait_recv()
         on_twin[i].start()
 
-    load_info.wait()
     for copy in tell_info:
         copy.wait_recv()
     r.key_info[...] = jnp.transpose(r.info_buf[...].astype(f32))[0:8]
@@ -1719,6 +1845,7 @@
         heads_buf=vmem((width, head_cols), bf16),
         info_buf=vmem((tokens, 128), bf16),
         key_info=vmem((8, tokens), f32),
+        gain=vmem((1, width), f32),
         qkv_buf=vmem((tokens, head_cols), bf16),
         mixed_buf=vmem((tokens, q_cols), bf16),
         cols_buf=vmem((tokens, part_wide), bf16),
@@ -1744,7 +1871,8 @@
         functools.partial(attend_kernel, tuple(args) + tuple(outs) + tuple(scratch)),
         out_shape=list(outs.values()),
         in_specs=[
-            small if value.ndim == 2 and value.shape[0] <= 8 else any_space
+            pl.BlockSpec(memory_space=pltpu.SMEM) if value.shape[0] == 1
+            else small if value.ndim == 1 or value.shape[1] == 128 else any_space
             for value in args.values()
         ],
         out_specs=[any_space] * len(outs),
@@ -1829,26 +1957,22 @@
     tokens, seg_ids, parents, attn_gain, w_query, w_key, w_value, w_out, post_attn_gain,
     ffn_gain, w_gate, w_up, w_down, post_ffn_gain, cotangent,
 ):
-    f32, bf16 = jnp.float32, jnp.bfloat16
-    tok_rows, width = tokens.shape
-    nothing = jnp.zeros((width,), f32)
-    gains = jnp.stack(
-        [gain.astype(f32) for gain in (post_attn_gain, ffn_gain, post_ffn_gain, attn_gain)]
-        + [nothing] * 4
-    )
-    parent_row = parents[0]
-    labels = jnp.arange(SEGS)
-
-    def lookup(ident):
-        return jnp.sum(jnp.where(ident[:, None] == labels[None, :], parent_row[None, :], 0), axis=1)
-
-    real = seg_ids < SEGS
-    parent_one = lookup(seg_ids)
-    codes = [jnp.where(real, code, -1) for code in (seg_ids, parent_one, lookup(parent_one))]
-    codes.append(jnp.where(real, seg_ids, -2))
-    info = jnp.pad(jnp.stack(codes, axis=1).astype(bf16), ((0, 0), (0, 124)))
+    f32 = jnp.float32
     heads = attend(
-        2, tokens=tokens, gains=gains, info=info, w_query=w_query, w_key=w_key, w_value=w_value
+        2,
+        tokens=tokens,
+        attn_gain=attn_gain,
+        seg_ids=jnp.broadcast_to(seg_ids[:, None], (tokens.shape[0], 128)),
+        parents=parents,
+        w_query=w_query,
+        w_key=w_key,
+        w_value=w_value,
+    )
+    gains = dict(
+        attn_gain=attn_gain,
+        post_attn_gain=post_attn_gain,
+        ffn_gain=ffn_gain,
+        post_ffn_gain=post_ffn_gain,
     )
     ahead = forward(
         3,
@@ -1856,7 +1980,7 @@
         w_out=w_out,
         tokens=tokens,
         cotangent=cotangent,
-        gains=gains,
+        **gains,
         w_gate=w_gate,
         w_up=w_up,
         w_down=w_down,
@@ -1875,7 +1999,7 @@
         middle=ahead.middle,
         attn_out=ahead.attn_out,
         cotangent=cotangent,
-        gains=gains,
+        **gains,
         gain_parts=ahead.gain_part,
         qkv=heads.qkv,
         mixed=heads.mixed,

time: 728 us -> 694 us (0.953)
  Pallas kernels: 678 us -> 650 us
    pallas_call x1, Pallas kernels: 140 us -> 114 us  [forward(): pl.pallas_call(functools.partial(forward_kernel, tuple(args) + tuple(outs...]
where the time goes in v7:
time: 694 us
  Pallas kernels  650 us (94%)
  other arithmetic  39.6 us (6%)
    pallas_call x1, Pallas kernels, backward(): pl.pallas_call(functools.partial(backward_kernel, (tokens, local, width,...  471 us
    pallas_call x1, Pallas kernels, forward(): pl.pallas_call(functools.partial(forward_kernel, tuple(args) + tuple(outs...  114 us
    pallas_call x1, Pallas kernels, attend(): pl.pallas_call(functools.partial(attend_kernel, tuple(args) + tuple(outs)...  65 us
    convert_element_type x1, other arithmetic, plane_layer(): found.gate_sum.astype(f32)  15.6 us

profile of v7, /device:TPU:0, one launch (start us, length us, event | category | flops | bytes accessed | tf_op | source)
XLA Modules:
  0.0 693.9 jit_solution(13229996179419297747)
XLA Ops:
  0.6 1.4 broadcast_in_dim.2.refs_2_
  2.1 65.0 %shard_map.246 = (bf16[768,1024]{1,0:T(8,128)(2,1)}, bf16[768,512]{1,0:T(8,128)(2,1)}, f32[2,768,768]{2,1,0:T(8,128)}, f32[2,768,768]{2,1,0:T(8,128)}, bf16[768,640]{1,0:T(8,128)(2,1)}) custom-call(bf16[192,2304]{1,0:T(8,128)(2,1)} %refs_25_.1, bf16[2304]{0:T(1024)(128)(2,1)} %refs_12_.1, s32[192,128]{1,0:T(8,128)} %broadcast_in_dim.2.refs_2_, ...), custom_call_target="tpu_custom_call" | custom-call | flops 7247757312 | bytes 104857600 | tf_op jit(solution)/shard_map/pallas_call | solution.py:1870
  67.0 113.6 %shard_map.247 = (bf16[192,2304]{1,0:T(8,128)(2,1)}, bf16[768,2304]{1,0:T(8,128)(2,1)}, bf16[768,2304]{1,0:T(8,128)(2,1)}, bf16[768,2304]{1,0:T(8,128)(2,1)}, bf...) custom-call(bf16[768,512]{1,0:T(8,128)(2,1)} %get-tuple-element.36.r, ...), custom_call_target="tpu_custom_call" | custom-call | flops 32614907904 | bytes 104857600 | tf_op jit(solution)/shard_map/pallas_call | solution.py:1558
  180.6 471.0 %shard_map.248 = (bf16[2304,2304]{1,0:T(8,128)(2,1)}, bf16[2304,2304]{1,0:T(8,128)(2,1)}, bf16[2304,2304]{1,0:T(8,128)(2,1)}, bf16[512,2304]{1,0:T(8,128)(2,1)},...) custom-call(bf16[192,2304]{1,0:T(8,128)(2,1)} %get-tuple-element.38., ...), custom_call_target="tpu_custom_call" | custom-call | flops 326149079040 | bytes 419430400 | tf_op jit(solution)/shard_map/pallas_call | solution.py:1246
  651.7 0.0 copy-start
  651.7 0.0 slice-start
  651.7 0.0 slice-start.1
  651.7 15.6 %convert_element_type.25 = f32[2304,2304]{1,0:T(8,128)} convert(bf16[2304,2304]{1,0:T(8,128)(2,1)} %get-tuple-element.56) | non-fusion elementwise | flops 5308416 | bytes 31850496 | tf_op jit(solution)/shard_map/convert_element_type | solution.py:2025
  667.3 0.0 copy-done
  667.3 0.0 slice-start.2
  667.3 7.7 %convert_element_type.26 = f32[2304,2304]{1,0:T(8,128)} convert(bf16[2304,2304]{1,0:T(8,128)(2,1)S(1)} %copy-done) | non-fusion elementwise | flops 5308416 | bytes 31850496 | tf_op jit(solution)/shard_map/convert_element_type | solution.py:2026
  675.0 0.0 slice-done
  675.0 0.0 slice-done.1
  675.0 0.0 slice-done.2
  675.0 0.0 copy-start.2
  675.0 7.6 %convert_element_type.27 = f32[2304,2304]{1,0:T(8,128)} convert(bf16[2304,2304]{1,0:T(8,128)(2,1)S(1)} %bitcast.1) | non-fusion elementwise | flops 5308416 | bytes 31850496 | tf_op jit(solution)/shard_map/convert_element_type | solution.py:2027
  682.6 0.0 copy-done.2
  682.6 0.0 copy-start.1
  682.6 2.8 convert_element_type.21
  685.4 0.0 copy-done.1
  685.4 0.0 copy-start.4
  685.4 2.5 convert_element_type.24
  687.9 0.0 copy-start.3
  687.9 0.0 copy-done.4
  687.9 0.0 copy-start.7
  687.9 0.0 copy-start.5
  687.9 1.7 convert_element_type.22
  689.6 0.0 copy-start.6
  689.6 0.0 copy-done.3
  689.6 1.7 convert_element_type.23
  691.3 0.0 copy-done.7
  691.3 0.7 slice_reduce_fusion
  692.0 0.0 copy-done.5
  692.0 0.9 copy.30
  692.9 0.0 copy-done.6
  692.9 0.9 copy.31
  (1 shorter events, 0.0 us)
Async XLA Ops:
  651.7 15.7 %copy-start = (bf16[2304,2304]{1,0:T(8,128)(2,1)S(1)}, bf16[2304,2304]{1,0:T(8,128)(2,1)}, u32[]{:S(2)}) copy-start(bf16[2304,2304]{1,0:T(8,128)(2,1)} %get-tuple-element.57) | copy-start | bytes 31850500
  651.7 23.3 %slice-start = ((s8[10616832]{0:T(1024)(128)(4,1)}), s8[4194304]{0:T(1024)(128)(4,1)S(1)}, s32[]{:S(2)}) async-start(s8[10616832]{0:T(1024)(128)(4,1)} %bitcast), calls=%async_computation | async-start | bytes 8388608
  651.7 23.3 %slice-start.1 = ((s8[10616832]{0:T(1024)(128)(4,1)}), s8[4194304]{0:T(1024)(128)(4,1)S(1)}, s32[]{:S(2)}) async-start(s8[10616832]{0:T(1024)(128)(4,1)} %bitcast), calls=%async_computation.1 | async-start | bytes 8388608
  667.3 7.7 %slice-start.2 = ((s8[10616832]{0:T(1024)(128)(4,1)}), s8[2228224]{0:T(1024)(128)(4,1)S(1)}, s32[]{:S(2)}) async-start(s8[10616832]{0:T(1024)(128)(4,1)} %bitcast), calls=%async_computation.2 | async-start | bytes 4456448
  675.0 7.6 %copy-start.2 = (bf16[576,2048]{1,0:T(8,128)(2,1)S(1)}, bf16[576,2048]{1,0:T(8,128)(2,1)}, u32[]{:S(2)}) copy-start(bf16[576,2048]{1,0:T(8,128)(2,1)} %get-tuple-element.52) | copy-start | bytes 7077892
  682.6 2.8 copy-start.1
  685.4 2.5 copy-start.4
  687.9 1.7 copy-start.3
  687.9 3.4 copy-start.7
  687.9 4.1 copy-start.5
  689.6 3.3 copy-start.6

commit v8 on v7

--- a/solution.py
+++ b/solution.py
@@ -330,12 +330,12 @@
     a_at = pieces + 1
     b_at = a_at + (n_a + 1) // 2
     c_at = b_at + n_b
-    d_at = c_at + 5
-    f_at = d_at + 5
+    d_at = c_at + 6
+    f_at = d_at + 7
     g_at = f_at + 1
     h_at = g_at + heads * n_blocks
-    i_at = h_at + 9
-    k_at = i_at + 3
+    i_at = h_at + 10
+    k_at = i_at + n_blocks + 2
     assert b_at <= first[1] and f_at < first[3] and i_at < first[4] and first[1] <= i_at
     assert first[2] <= i_at and k_at + 5 <= units + 5 and counts[0] // pieces >= 2
 
@@ -552,14 +552,15 @@
             r.c_mine[index] = add_low(r.c_mine[index], r.c_landed[index])
             c_on[index].start()
 
-    def d_norms():
-        for copy in load_small:
-            copy.wait()
-        for copy in c_first:
-            copy.wait_send()
-        for copy in c_first[2:] + c_on:
-            copy.wait_recv()
-        r.gain_own[...] = r.gain_parts[...]
+    def d_norms(which):
+        if which == 0:
+            for copy in load_small:
+                copy.wait()
+            for copy in c_first:
+                copy.wait_send()
+            r.gain_own[...] = r.gain_parts[...]
+        c_first[2 + which].wait_recv()
+        c_on[which].wait_recv()
 
         def rows_of(which, index, carry):
             here = pl.ds(pl.multiple_of(index * 16, 16), 16)
@@ -589,10 +590,12 @@
             )
             return carry
 
-        for which in range(2):
-            lax.fori_loop(0, half // 16, functools.partial(rows_of, which), 0)
-        for copy in c_on:
-            copy.wait_send()
+        lax.fori_loop(0, half // 16, functools.partial(rows_of, which), 0)
+        for index in ((0, 3), (1, 2))[which]:
+            e_first[index].start()
+        if which == 1:
+            for copy in c_on:
+                copy.wait_send()
 
     def gather_copies(rows, source, target, send_sem, recv_sem):
         def send(owner, which, index, where, src):
@@ -727,21 +730,19 @@
         for copy in i_loads:
             copy.wait()
 
-    def i_norm():
-        def rows_of(index, carry):
-            rows = pl.ds(pl.multiple_of(index * block, block), block)
-            some = jnp.zeros((block, part_wide), f32)
-            for owner in range(4):
-                for kind, size in enumerate((q_cols, k_cols, k_cols)):
-                    held = r.gate_grad if kind == 0 else r.weights
-                    start = (0, 0, 4 * k_cols)[kind] + owner * size
-                    some += dot_rows(
-                        side_of(owner, kind)[rows], held[pl.ds(0, part_wide), pl.ds(start, size)]
-                    )
-            r.head_grad[rows, pl.ds(0, part_wide)] = some.astype(bf16)
-            return carry
-
-        lax.fori_loop(0, n_blocks, rows_of, 0)
+    def i_norm(index):
+        rows = pl.ds(index * block, block)
+        some = jnp.zeros((block, part_wide), f32)
+        for owner in range(4):
+            for kind, size in enumerate((q_cols, k_cols, k_cols)):
+                held = r.gate_grad if kind == 0 else r.weights
+                start = (0, 0, 4 * k_cols)[kind] + owner * size
+                some += dot_rows(
+                    side_of(owner, kind)[rows], held[pl.ds(0, part_wide), pl.ds(start, size)]
+                )
+        r.head_grad[rows, pl.ds(0, part_wide)] = some.astype(bf16)
+        if index < n_blocks - 1:
+            return
         for copy in i_copies:
             copy.start()
         r.norm_grad[me] = r.head_grad[
@@ -1060,13 +1061,9 @@
         at(now, c_at + 1, load_out.start)
         at(now, c_at + 2, c_pass)
 
-        @pl.when(now == d_at)
-        def _():
-            d_norms()
-            for copy in e_first:
-                copy.start()
-
-        at(now, d_at + 2, lambda: pass_on(e_first, e_on))
+        at(now, d_at, lambda: d_norms(0))
+        at(now, d_at + 1, lambda: d_norms(1))
+        at(now, d_at + 3, lambda: pass_on(e_first, e_on))
         at(now, f_at, f_mixed)
 
         @pl.when((now >= g_at) & (now < h_at))
@@ -1076,7 +1073,8 @@
         at(now, h_at, h_start)
         at(now, h_at + 4, lambda: pass_on(h_first, h_on))
         at(now, i_at, i_start)
-        at(now, i_at + 1, i_norm)
+        for index in range(n_blocks):
+            at(now, i_at + 1 + index, functools.partial(i_norm, index))
         at(now, k_at, k_norm)
         at(now, k_at + 1, k_plane)
         for index in range(3):
@@ -1388,8 +1386,9 @@
         a_near[which].wait_recv()
         a_on[which].wait_recv()
         lax.fori_loop(0, half // 32, functools.partial(middle_rows, which), 0)
-        for copy in b_starts[which]:
-            copy.start()
+        b_starts[which][which].start()
+    for which in range(2):
+        b_starts[which][1 - which].start()
     keep = [
         pltpu.make_async_copy(r.attn_buf, r.attn_out, r.keep_sem.at[0]),
         pltpu.make_async_copy(r.middle_buf, r.middle, r.keep_sem.at[1]),
@@ -1399,81 +1398,86 @@
     for copy in a_far + a_near + a_on:
         copy.wait_send()
 
-    def keep_block(owner):
-        rows = block_rows(owner)
+    def keep_block(halves):
         return [
-            pltpu.make_async_copy(buf, dst.at[rows], r.keep_sem.at[2 + i])
-            for i, (buf, dst) in enumerate(
-                ((r.gate_stage, r.gate), (r.up_stage, r.up), (r.hidden_buf.at[rows], r.hidden))
+            pltpu.make_async_copy(src, dst.at[half_rows(*halves[i])], r.keep_sem.at[2 + 2 * kind + i])
+            for i in range(2)
+            for kind, (src, dst) in enumerate(
+                (
+                    (r.gate_stage.at[pl.ds(i * half, half)], r.gate),
+                    (r.up_stage.at[pl.ds(i * half, half)], r.up),
+                    (r.hidden_buf.at[half_rows(*halves[i])], r.hidden),
+                )
             )
         ]
 
-    def feed(owner, before):
-        rows = block_rows(owner)
+    def feed(halves, before):
+        for i in range(2):
+            r.block[pl.ds(i * half, half), pl.ds(0, width)] = r.two_buf[half_rows(*halves[i])]
         if before is not None:
             for copy in keep_block(before):
                 copy.wait()
 
         def tile(index, carry):
             columns = pl.ds(pl.multiple_of(index * TILE, TILE), TILE)
-            block = r.two_buf[rows]
-            r.gate_wide[...] = dot_plain(block, r.gate_weight[:, columns])
-            r.up_wide[...] = dot_plain(block, r.up_weight[:, columns])
-
-            def rows_of(index, carry):
-                here = pl.ds(pl.multiple_of(index * half, 16), half)
+            r.gate_wide[...] = dot_plain(r.block[:, pl.ds(0, width)], r.gate_weight[:, columns])
+            r.up_wide[...] = dot_plain(r.block[:, pl.ds(0, width)], r.up_weight[:, columns])
+            for i in range(2):
+                here = pl.ds(i * half, half)
                 gate, up = r.gate_wide[here], r.up_wide[here]
                 r.gate_stage[here, columns] = gate.astype(bf16)
                 r.up_stage[here, columns] = up.astype(bf16)
                 curve = jnp.tanh(ROOT_TWO_PI * (gate + 0.044715 * (gate * gate * gate)))
-                r.hidden_buf[
-                    pl.ds(pl.multiple_of(owner * local + index * half, 16), half), columns
-                ] = (0.5 * gate * (1.0 + curve) * up).astype(bf16)
-                return carry
-
-            lax.fori_loop(0, 2, rows_of, 0)
+                r.hidden_buf[half_rows(*halves[i]), columns] = (
+                    0.5 * gate * (1.0 + curve) * up
+                ).astype(bf16)
             return carry
 
         lax.fori_loop(0, inner_width // TILE, tile, 0)
-        for copy in keep_block(owner):
+        for copy in keep_block(halves):
             copy.start()
 
-    def shrink(owner):
-        rows = block_rows(owner)
+    def shrink(halves):
+        for i in range(2):
+            r.block[pl.ds(i * half, half), pl.ds(0, inner_width)] = r.hidden_buf[half_rows(*halves[i])]
 
         def tile(index, carry):
             columns = pl.ds(pl.multiple_of(index * TILE, TILE), TILE)
-            r.partial[rows, columns] = dot_plain(
-                r.hidden_buf[rows], r.down_weight[:, columns]
-            ).astype(bf16)
+            some = dot_plain(r.block[:, pl.ds(0, inner_width)], r.down_weight[:, columns]).astype(bf16)
+            for i in range(2):
+                r.partial[half_rows(*halves[i]), columns] = some[i * half : (i + 1) * half]
             return carry
 
         lax.fori_loop(0, width // TILE, tile, 0)
 
+    mine = ((me, 0), (me, 1))
+    early_halves = ((x_place, 0), (y_place, 1))
+    late_halves = ((x_place, 1), (y_place, 0))
+    far_halves = ((far_place, 0), (far_place, 1))
     big[0].wait()
     big[1].wait()
-    feed(me, None)
+    feed(mine, None)
     big[2].wait()
     b_starts[0][0].wait_recv()
     b_on[0].start()
     b_starts[1][1].wait_recv()
     b_on[1].start()
-    shrink(me)
+    feed(early_halves, mine)
+    shrink(early_halves)
+    for copy in c_near:
+        copy.start()
     b_starts[1][0].wait_recv()
-    feed(x_place, me)
-    shrink(x_place)
-    c_near[0].start()
     b_starts[0][1].wait_recv()
-    feed(y_place, x_place)
-    shrink(y_place)
-    c_near[1].start()
+    feed(late_halves, early_halves)
     for copy in b_on:
         copy.wait_recv()
-    feed(far_place, y_place)
-    shrink(far_place)
+    feed(far_halves, late_halves)
+    shrink(far_halves)
     for copy in c_far:
         copy.start()
-    keep_two = pltpu.make_async_copy(r.two_buf, r.normed_two, r.keep_sem.at[5])
+    shrink(late_halves)
+    shrink(mine)
+    keep_two = pltpu.make_async_copy(r.two_buf, r.normed_two, r.keep_sem.at[8])
     keep_two.start()
     r.gain_part[...] = jnp.zeros_like(r.gain_part)
     pass_sums(r.c_landed, c_far, c_on)
@@ -1494,13 +1498,13 @@
         c_near[which].wait_recv()
         c_on[which].wait_recv()
         lax.fori_loop(0, half // 32, functools.partial(last_rows, which), 0)
-    keep_own = pltpu.make_async_copy(r.cot_buf, r.grad_ffn, r.keep_sem.at[6])
-    keep_out = pltpu.make_async_copy(r.token_buf, r.output, r.keep_sem.at[7])
+    keep_own = pltpu.make_async_copy(r.cot_buf, r.grad_ffn, r.keep_sem.at[9])
+    keep_out = pltpu.make_async_copy(r.token_buf, r.output, r.keep_sem.at[10])
     keep_own.start()
     keep_out.start()
     for copy in b_starts[0] + b_starts[1] + list(b_on + c_far + c_near + c_on):
         copy.wait_send()
-    for copy in keep + keep_block(far_place) + [keep_two, keep_own, keep_out]:
+    for copy in keep + keep_block(far_halves) + [keep_two, keep_own, keep_out]:
         copy.wait()
 
 
@@ -1542,10 +1546,11 @@
         hidden_buf=vmem((tokens, inner_width), bf16),
         gate_stage=vmem((local, inner_width), bf16),
         up_stage=vmem((local, inner_width), bf16),
+        block=vmem((local, max(width, inner_width)), bf16),
         gate_wide=vmem((local, TILE), f32),
         up_wide=vmem((local, TILE), f32),
         load_sem=dma((7,)),
-        keep_sem=dma((8,)),
+        keep_sem=dma((11,)),
         a_send=dma((6,)),
         a_recv=dma((6,)),
         b_send=dma((6,)),

time: 694 us -> 674 us (0.971)
  Pallas kernels: 650 us -> 629 us
    pallas_call x1, Pallas kernels: 114 us -> 97.1 us  [forward(): pl.pallas_call(functools.partial(forward_kernel, tuple(args) + tuple(outs...]
where the time goes in v8:
time: 674 us; the launch traced here: 673 us
  Pallas kernels  629 us (93%)
  other arithmetic  39.6 us (6%)
    pallas_call x1, Pallas kernels, backward(): pl.pallas_call(functools.partial(backward_kernel, (tokens, local, width,...  467 us
    pallas_call x1, Pallas kernels, forward(): pl.pallas_call(functools.partial(forward_kernel, tuple(args) + tuple(outs...  97.1 us
    pallas_call x1, Pallas kernels, attend(): pl.pallas_call(functools.partial(attend_kernel, tuple(args) + tuple(outs)...  65 us
    convert_element_type x1, other arithmetic, plane_layer(): found.gate_sum.astype(f32)  15.6 us

profile of v8, /device:TPU:0, one launch (start us, length us, event | category | flops | bytes accessed | tf_op | source)
XLA Modules:
  0.0 673.3 jit_solution(1161417936280307835)
XLA Ops:
  0.6 1.4 broadcast_in_dim.2.refs_2_
  2.1 65.0 %shard_map.246 = (bf16[768,1024]{1,0:T(8,128)(2,1)}, bf16[768,512]{1,0:T(8,128)(2,1)}, f32[2,768,768]{2,1,0:T(8,128)}, f32[2,768,768]{2,1,0:T(8,128)}, bf16[768,640]{1,0:T(8,128)(2,1)}) custom-call(bf16[192,2304]{1,0:T(8,128)(2,1)} %refs_25_.1, bf16[2304]{0:T(1024)(128)(2,1)} %refs_12_.1, s32[192,128]{1,0:T(8,128)} %broadcast_in_dim.2.refs_2_, ...), custom_call_target="tpu_custom_call" | custom-call | flops 7247757312 | bytes 104857600 | tf_op jit(solution)/shard_map/pallas_call | solution.py:1875
  67.0 97.1 %shard_map.247 = (bf16[192,2304]{1,0:T(8,128)(2,1)}, bf16[768,2304]{1,0:T(8,128)(2,1)}, bf16[768,2304]{1,0:T(8,128)(2,1)}, bf16[768,2304]{1,0:T(8,128)(2,1)}, bf...) custom-call(bf16[768,512]{1,0:T(8,128)(2,1)} %get-tuple-element.36.r, ...), custom_call_target="tpu_custom_call" | custom-call | flops 32614907904 | bytes 104857600 | tf_op jit(solution)/shard_map/pallas_call | solution.py:1563
  164.1 466.9 %shard_map.248 = (bf16[2304,2304]{1,0:T(8,128)(2,1)}, bf16[2304,2304]{1,0:T(8,128)(2,1)}, bf16[2304,2304]{1,0:T(8,128)(2,1)}, bf16[512,2304]{1,0:T(8,128)(2,1)},...) custom-call(bf16[192,2304]{1,0:T(8,128)(2,1)} %get-tuple-element.38., ...), custom_call_target="tpu_custom_call" | custom-call | flops 326149079040 | bytes 419430400 | tf_op jit(solution)/shard_map/pallas_call | solution.py:1244
  631.1 0.0 copy-start
  631.1 0.0 slice-start
  631.1 0.0 slice-start.1
  631.1 15.6 %convert_element_type.25 = f32[2304,2304]{1,0:T(8,128)} convert(bf16[2304,2304]{1,0:T(8,128)(2,1)} %get-tuple-element.56) | non-fusion elementwise | flops 5308416 | bytes 31850496 | tf_op jit(solution)/shard_map/convert_element_type | solution.py:2030
  646.7 0.0 copy-done
  646.7 0.0 slice-start.2
  646.7 7.7 %convert_element_type.26 = f32[2304,2304]{1,0:T(8,128)} convert(bf16[2304,2304]{1,0:T(8,128)(2,1)S(1)} %copy-done) | non-fusion elementwise | flops 5308416 | bytes 31850496 | tf_op jit(solution)/shard_map/convert_element_type | solution.py:2031
  654.4 0.0 slice-done
  654.4 0.0 slice-done.1
  654.4 0.0 slice-done.2
  654.4 0.0 copy-start.2
  654.4 7.6 %convert_element_type.27 = f32[2304,2304]{1,0:T(8,128)} convert(bf16[2304,2304]{1,0:T(8,128)(2,1)S(1)} %bitcast.1) | non-fusion elementwise | flops 5308416 | bytes 31850496 | tf_op jit(solution)/shard_map/convert_element_type | solution.py:2032
  662.0 0.0 copy-done.2
  662.0 0.0 copy-start.1
  662.0 2.8 convert_element_type.21
  664.8 0.0 copy-done.1
  664.8 0.0 copy-start.4
  664.8 2.5 convert_element_type.24
  667.3 0.0 copy-start.3
  667.3 0.0 copy-done.4
  667.3 0.0 copy-start.7
  667.3 0.0 copy-start.5
  667.3 1.7 convert_element_type.22
  669.0 0.0 copy-start.6
  669.0 0.0 copy-done.3
  669.1 1.7 convert_element_type.23
  670.7 0.0 copy-done.7
  670.7 0.7 slice_reduce_fusion
  671.4 0.0 copy-done.5
  671.4 0.9 copy.30
  672.4 0.0 copy-done.6
  672.4 0.9 copy.31
  (1 shorter events, 0.0 us)
Async XLA Ops:
  631.1 15.7 %copy-start = (bf16[2304,2304]{1,0:T(8,128)(2,1)S(1)}, bf16[2304,2304]{1,0:T(8,128)(2,1)}, u32[]{:S(2)}) copy-start(bf16[2304,2304]{1,0:T(8,128)(2,1)} %get-tuple-element.57) | copy-start | bytes 31850500
  631.1 23.3 %slice-start = ((s8[10616832]{0:T(1024)(128)(4,1)}), s8[4194304]{0:T(1024)(128)(4,1)S(1)}, s32[]{:S(2)}) async-start(s8[10616832]{0:T(1024)(128)(4,1)} %bitcast), calls=%async_computation | async-start | bytes 8388608
  631.1 23.3 %slice-start.1 = ((s8[10616832]{0:T(1024)(128)(4,1)}), s8[4194304]{0:T(1024)(128)(4,1)S(1)}, s32[]{:S(2)}) async-start(s8[10616832]{0:T(1024)(128)(4,1)} %bitcast), calls=%async_computation.1 | async-start | bytes 8388608
  646.7 7.7 %slice-start.2 = ((s8[10616832]{0:T(1024)(128)(4,1)}), s8[2228224]{0:T(1024)(128)(4,1)S(1)}, s32[]{:S(2)}) async-start(s8[10616832]{0:T(1024)(128)(4,1)} %bitcast), calls=%async_computation.2 | async-start | bytes 4456448
  654.4 7.6 %copy-start.2 = (bf16[576,2048]{1,0:T(8,128)(2,1)S(1)}, bf16[576,2048]{1,0:T(8,128)(2,1)}, u32[]{:S(2)}) copy-start(bf16[576,2048]{1,0:T(8,128)(2,1)} %get-tuple-element.52) | copy-start | bytes 7077892
  662.0 2.8 copy-start.1
  664.8 2.5 copy-start.4
  667.3 1.7 copy-start.3
  667.3 3.4 copy-start.7
  667.3 4.1 copy-start.5
  669.0 3.3 copy-start.6

commit v9 on v8

--- a/solution.py
+++ b/solution.py
@@ -280,7 +280,7 @@
 TILE = 256
 PAIR = 2 * CHUNK
 LINE = 32
-DEEP = 12
+DEEP = 10
 LAST = 6
 ROOT_TWO_PI = math.sqrt(2.0 / math.pi)
 
@@ -1023,7 +1023,7 @@
         by_job(step, use)
 
     lag_outer = 3
-    lag_inner = jnp.where(is_end, 10, 6)
+    lag_inner = jnp.where(is_end, 8, 5)
 
     def at(now, step, use):
         @pl.when(now == step)
@@ -1705,8 +1705,9 @@
 
     for which in range(2):
         lax.fori_loop(0, half // 32, functools.partial(norm_rows, which), 0)
-        for copy in own[which]:
-            copy.start()
+        own[which][which].start()
+    for which in range(2):
+        own[which][1 - which].start()
 
     for i in (2, 0, 1):
         for copy in fetch[i]:
@@ -1729,6 +1730,23 @@
     for copy in to_twin + on_twin:
         copy.wait_recv()
 
+    wide = r.cols_buf.shape[1]
+
+    def keep_columns(block_of):
+        for owner in range(4):
+
+            @pl.when(me == owner)
+            def _():
+                def rows_of(index, carry):
+                    rows = pl.ds(pl.multiple_of(block_of * local + index * half, 16), half)
+                    some = r.all_buf[rows, owner * part : (owner + 1) * part]
+                    if wide > part:
+                        some = jnp.concatenate((some, jnp.zeros((half, wide - part), bf16)), axis=1)
+                    r.cols_buf[rows] = some
+                    return carry
+
+                lax.fori_loop(0, 2, rows_of, 0)
+
     def project(owner):
         rows = pl.ds(pl.multiple_of(owner * local, 16), local)
         r.qkv_buf[rows] = dot_plain(r.all_buf[rows], r.heads_buf[...]).astype(bf16)
@@ -1738,11 +1756,18 @@
     project(x_place)
     own[0][1].wait_recv()
     project(y_place)
+    for owner in (me, x_place, y_place):
+        keep_columns(owner)
     for copy in on:
         copy.wait_recv()
     project(far_place)
-    keep = [pltpu.make_async_copy(r.qkv_buf, r.qkv, r.keep_sem.at[0])]
-    keep[0].start()
+    keep_columns(far_place)
+    keep = [
+        pltpu.make_async_copy(r.qkv_buf, r.qkv, r.keep_sem.at[0]),
+        pltpu.make_async_copy(r.cols_buf, r.normed_cols, r.keep_sem.at[2]),
+    ]
+    for copy in keep:
+        copy.start()
 
     def keep_item(item):
         head, rows = item // n_blocks, pl.ds((item % n_blocks) * block, block)
@@ -1778,7 +1803,7 @@
             curve = jnp.tanh(r.score[here, pl.ds(0, limit)] * (head_scale / softcap))
             masked = jnp.where(visible, softcap * curve, -1e30)
             terms = jnp.exp(masked - jnp.max(masked, axis=-1, keepdims=True))
-            probs = terms / jnp.sum(terms, axis=-1, keepdims=True)
+            probs = terms * (1.0 / jnp.sum(terms, axis=-1, keepdims=True))
             r.tanh_stage[slot, here, pl.ds(0, limit)] = curve
             r.probs_stage[slot, here, pl.ds(0, limit)] = probs
             r.probs_low[here, pl.ds(0, limit)] = probs.astype(bf16)
@@ -1793,25 +1818,8 @@
         ).astype(bf16)
 
     keep.append(pltpu.make_async_copy(r.mixed_buf, r.mixed, r.keep_sem.at[1]))
-    keep[1].start()
-
-    wide = r.cols_buf.shape[1]
-    for owner in range(4):
-
-        @pl.when(me == owner)
-        def _():
-            def rows_of(index, carry):
-                rows = pl.ds(pl.multiple_of(index * 64, 64), 64)
-                some = r.all_buf[rows, owner * part : (owner + 1) * part]
-                if wide > part:
-                    some = jnp.concatenate((some, jnp.zeros((64, wide - part), bf16)), axis=1)
-                r.cols_buf[rows] = some
-                return carry
-
-            lax.fori_loop(0, tokens // 64, rows_of, 0)
-
-    keep.append(pltpu.make_async_copy(r.cols_buf, r.normed_cols, r.keep_sem.at[2]))
     keep[2].start()
+
     for group in fetch + own:
         for copy in group:
             copy.wait_send()

time: 674 us -> 672 us (level)
  no operation moved by 1% of the time
where the time goes in v9:
time: 672 us
  Pallas kernels  627 us (93%)
  other arithmetic  39.6 us (6%)
    pallas_call x1, Pallas kernels, backward(): pl.pallas_call(functools.partial(backward_kernel, (tokens, local, width,...  466 us
    pallas_call x1, Pallas kernels, forward(): pl.pallas_call(functools.partial(forward_kernel, tuple(args) + tuple(outs...  98.8 us
    pallas_call x1, Pallas kernels, attend(): pl.pallas_call(functools.partial(attend_kernel, tuple(args) + tuple(outs)...  62.6 us
    convert_element_type x1, other arithmetic, plane_layer(): found.gate_sum.astype(f32)  15.6 us

profile of v9, /device:TPU:0, one launch (start us, length us, event | category | flops | bytes accessed | tf_op | source)
XLA Modules:
  0.0 671.6 jit_solution(1751782908774283338)
XLA Ops:
  0.6 1.4 broadcast_in_dim.2.refs_2_
  2.1 62.6 %shard_map.246 = (bf16[768,1024]{1,0:T(8,128)(2,1)}, bf16[768,512]{1,0:T(8,128)(2,1)}, f32[2,768,768]{2,1,0:T(8,128)}, f32[2,768,768]{2,1,0:T(8,128)}, bf16[768,640]{1,0:T(8,128)(2,1)}) custom-call(bf16[192,2304]{1,0:T(8,128)(2,1)} %refs_25_.1, bf16[2304]{0:T(1024)(128)(2,1)} %refs_12_.1, s32[192,128]{1,0:T(8,128)} %broadcast_in_dim.2.refs_2_, ...), custom_call_target="tpu_custom_call" | custom-call | flops 7247757312 | bytes 104857600 | tf_op jit(solution)/shard_map/pallas_call | solution.py:1883
  64.6 98.8 %shard_map.247 = (bf16[192,2304]{1,0:T(8,128)(2,1)}, bf16[768,2304]{1,0:T(8,128)(2,1)}, bf16[768,2304]{1,0:T(8,128)(2,1)}, bf16[768,2304]{1,0:T(8,128)(2,1)}, bf...) custom-call(bf16[768,512]{1,0:T(8,128)(2,1)} %get-tuple-element.36.r, ...), custom_call_target="tpu_custom_call" | custom-call | flops 32614907904 | bytes 104857600 | tf_op jit(solution)/shard_map/pallas_call | solution.py:1563
  163.5 465.9 %shard_map.248 = (bf16[2304,2304]{1,0:T(8,128)(2,1)}, bf16[2304,2304]{1,0:T(8,128)(2,1)}, bf16[2304,2304]{1,0:T(8,128)(2,1)}, bf16[512,2304]{1,0:T(8,128)(2,1)},...) custom-call(bf16[192,2304]{1,0:T(8,128)(2,1)} %get-tuple-element.38., ...), custom_call_target="tpu_custom_call" | custom-call | flops 326149079040 | bytes 419430400 | tf_op jit(solution)/shard_map/pallas_call | solution.py:1244
  629.4 0.0 copy-start
  629.4 0.0 slice-start
  629.4 0.0 slice-start.1
  629.4 15.6 %convert_element_type.25 = f32[2304,2304]{1,0:T(8,128)} convert(bf16[2304,2304]{1,0:T(8,128)(2,1)} %get-tuple-element.56) | non-fusion elementwise | flops 5308416 | bytes 31850496 | tf_op jit(solution)/shard_map/convert_element_type | solution.py:2038
  645.1 0.0 copy-done
  645.1 0.0 slice-start.2
  645.1 7.7 %convert_element_type.26 = f32[2304,2304]{1,0:T(8,128)} convert(bf16[2304,2304]{1,0:T(8,128)(2,1)S(1)} %copy-done) | non-fusion elementwise | flops 5308416 | bytes 31850496 | tf_op jit(solution)/shard_map/convert_element_type | solution.py:2039
  652.7 0.0 slice-done
  652.7 0.0 slice-done.1
  652.7 0.0 slice-done.2
  652.8 0.0 copy-start.2
  652.8 7.6 %convert_element_type.27 = f32[2304,2304]{1,0:T(8,128)} convert(bf16[2304,2304]{1,0:T(8,128)(2,1)S(1)} %bitcast.1) | non-fusion elementwise | flops 5308416 | bytes 31850496 | tf_op jit(solution)/shard_map/convert_element_type | solution.py:2040
  660.3 0.0 copy-done.2
  660.3 0.0 copy-start.1
  660.3 2.8 convert_element_type.21
  663.1 0.0 copy-done.1
  663.1 0.0 copy-start.4
  663.1 2.5 convert_element_type.24
  665.7 0.0 copy-start.3
  665.7 0.0 copy-done.4
  665.7 0.0 copy-start.7
  665.7 0.0 copy-start.5
  665.7 1.7 convert_element_type.22
  667.4 0.0 copy-start.6
  667.4 0.0 copy-done.3
  667.4 1.7 convert_element_type.23
  669.1 0.0 copy-done.7
  669.1 0.7 slice_reduce_fusion
  669.8 0.0 copy-done.5
  669.8 0.9 copy.30
  670.7 0.0 copy-done.6
  670.7 0.9 copy.31
  (1 shorter events, 0.0 us)
Async XLA Ops:
  629.4 15.7 %copy-start = (bf16[2304,2304]{1,0:T(8,128)(2,1)S(1)}, bf16[2304,2304]{1,0:T(8,128)(2,1)}, u32[]{:S(2)}) copy-start(bf16[2304,2304]{1,0:T(8,128)(2,1)} %get-tuple-element.57) | copy-start | bytes 31850500
  629.4 23.3 %slice-start = ((s8[10616832]{0:T(1024)(128)(4,1)}), s8[4194304]{0:T(1024)(128)(4,1)S(1)}, s32[]{:S(2)}) async-start(s8[10616832]{0:T(1024)(128)(4,1)} %bitcast), calls=%async_computation | async-start | bytes 8388608
  629.4 23.3 %slice-start.1 = ((s8[10616832]{0:T(1024)(128)(4,1)}), s8[4194304]{0:T(1024)(128)(4,1)S(1)}, s32[]{:S(2)}) async-start(s8[10616832]{0:T(1024)(128)(4,1)} %bitcast), calls=%async_computation.1 | async-start | bytes 8388608
  645.1 7.7 %slice-start.2 = ((s8[10616832]{0:T(1024)(128)(4,1)}), s8[2228224]{0:T(1024)(128)(4,1)S(1)}, s32[]{:S(2)}) async-start(s8[10616832]{0:T(1024)(128)(4,1)} %bitcast), calls=%async_computation.2 | async-start | bytes 4456448
  652.8 7.6 %copy-start.2 = (bf16[576,2048]{1,0:T(8,128)(2,1)S(1)}, bf16[576,2048]{1,0:T(8,128)(2,1)}, u32[]{:S(2)}) copy-start(bf16[576,2048]{1,0:T(8,128)(2,1)} %get-tuple-element.52) | copy-start | bytes 7077892
  660.3 2.8 copy-start.1
  663.1 2.5 copy-start.4
  665.7 1.7 copy-start.3
  665.7 3.4 copy-start.7
  665.7 4.1 copy-start.5
  667.4 3.3 copy-start.6
